TPU v7x, 32 devices: a whole 2x2x4 slice. The times are simulated.
32 devices in a mesh: seq: 4 (over x, core), fsdp: 8 (over z, y).
Axes of the slice: x: 2, y: 2, z: 4, core: 2. Of those that a mesh axis runs over, the one named last changes fastest.
Arguments:
- hidden_in: bfloat16 [2, 4096, 2048], P(None, ('seq', 'fsdp')), may hold values from -6 to 6
- out_cotangent: bfloat16 [2, 4096, 2048], P(None, ('seq', 'fsdp')), may hold values from -6 to 6
- positions: int32 [2, 4096], replicated, may hold values from 0 to 4095, as said below
- block_mask: int32 [2, 16, 16], replicated, may hold values from 0 to 1, as said below
- norm_gain: bfloat16 [2048], P('fsdp'), may hold values from 0.5 to 1.5
- norm_bias: bfloat16 [2048], P('fsdp'), may hold values from -3 to 3
- qkv_weight: bfloat16 [2048, 2304], P('fsdp'), may hold values from -0.125 to 0.125
- proj_weight: bfloat16 [2048, 2048], P('fsdp'), may hold values from -3 to 3
- mlp_gain: bfloat16 [2048], P('fsdp'), may hold values from 0.5 to 1.5
- mlp_bias: bfloat16 [2048], P('fsdp'), may hold values from -3 to 3
- fc_weight: bfloat16 [2048, 8192], P('fsdp'), may hold values from -0.125 to 0.125
- down_weight: bfloat16 [8192, 2048], P('fsdp'), may hold values from -0.0625 to 0.0625
Outputs:
- hidden_out: bfloat16 [2, 4096, 2048], P(None, ('seq', 'fsdp'))
- grad_input: bfloat16 [2, 4096, 2048], P(None, ('seq', 'fsdp'))
- grad_norm_gain: float32 [2048], P('fsdp')
- grad_norm_bias: float32 [2048], P('fsdp')
- grad_qkv: float32 [2048, 2304], P('fsdp')
- grad_proj: float32 [2048, 2048], P('fsdp')
- grad_mlp_gain: float32 [2048], P('fsdp')
- grad_mlp_bias: float32 [2048], P('fsdp')
- grad_fc: float32 [2048, 8192], P('fsdp')
- grad_down: float32 [8192, 2048], P('fsdp')
Inputs may be any that keep to these rules, and one draw needn't show every extreme that they name: In each sequence positions start at 0, and each next entry is either 0 (a new packed document begins) or one more than the entry before it. One of the 2 sequences, which one drawn from the seed, is a single document of 4096 tokens; in the others no document is longer than 2048 tokens, and the first one has exactly that length. block_mask[b, i, j] is 1 where i = j and 0 where j > i.
All inputs are finite; a program needn't handle non-finite values.
Results may differ from a plain program's by a relative error of at most 0.019.
Values may be sent and summed in bfloat16 or wider, within the bound.
A program may use at most 448 MiB of HBM per device.

v0:
```python
import jax
import jax.numpy as jnp
from jax import lax
from jax.sharding import PartitionSpec as P

HEADS = 16
HD = 128
MB = 2
BLOCK = 256


EPS = 1e-05
NEG_FILL = -1e30


def layer_norm(values):
    mean = jnp.mean(values, axis=-1, keepdims=True)
    center = values - mean
    inverse = lax.rsqrt(jnp.mean(center * center, axis=-1, keepdims=True) + EPS)
    return (center * inverse, inverse)


def norm_back(grad, normed, inverse):
    return inverse * (
        grad
        - jnp.mean(grad, axis=-1, keepdims=True)
        - normed * jnp.mean(grad * normed, axis=-1, keepdims=True)
    )


def contract_rows(left, right):
    return lax.dot_general(
        left, right, (((0,), (0,)), ((), ())), preferred_element_type=jnp.float32
    )


def contract_cols(left, right):
    return lax.dot_general(
        left, right, (((1,), (1,)), ((), ())), preferred_element_type=jnp.float32
    )


def gelu_tanh(values):
    return jax.nn.gelu(values, approximate=True)


def piece_rows(places, mask_table, first_token, count):
    tokens = first_token + jnp.arange(count, dtype=jnp.int32)
    offsets = lax.dynamic_slice_in_dim(places, first_token, count, 0)
    first_keys = tokens - offsets
    mask_rows = jnp.take(mask_table, tokens // BLOCK, axis=0)
    return (tokens, first_keys, mask_rows)


def tile_scores(query_rows, key_values, tile, key_tile, tokens, first_keys, mask_rows, heads_here):
    start = tile * key_tile
    block = lax.dynamic_slice_in_dim(key_values, start, key_tile, 0)
    keys = block[:, :HD]
    values = block[:, HD:]
    scores = contract_cols(query_rows, keys) * HD ** (-0.5)
    key_index = start + jnp.arange(key_tile, dtype=jnp.int32)
    marks = lax.dynamic_slice_in_dim(mask_rows, start // BLOCK, key_tile // BLOCK, 1)
    marks = jnp.repeat(marks, BLOCK, axis=1)
    allowed = (
        (marks == 1)
        & (key_index[None, :] <= tokens[:, None])
        & (key_index[None, :] >= first_keys[:, None])
    )
    allowed = jnp.repeat(allowed, heads_here, axis=0)
    return (jnp.where(allowed, scores, NEG_FILL), allowed, keys, values)


def tile_range(tokens, first_keys, key_tile):
    return (first_keys[0] // key_tile, tokens[tokens.shape[0] - 1] // key_tile + 1)


def attend_piece(query_rows, key_values, tokens, first_keys, mask_rows, heads_here, key_tile):
    rows = query_rows.shape[0]
    low_tile, high_tile = tile_range(tokens, first_keys, key_tile)

    def gather_stats(tile, carry):
        highest, total = carry
        scores, allowed, keys, values = tile_scores(
            query_rows, key_values, tile, key_tile, tokens, first_keys, mask_rows, heads_here
        )
        new_high = jnp.maximum(highest, jnp.max(scores, axis=1))
        terms = jnp.where(allowed, jnp.exp(scores - new_high[:, None]), 0.0)
        return (new_high, total * jnp.exp(highest - new_high) + jnp.sum(terms, axis=1))

    start_stats = (jnp.full((rows,), NEG_FILL, jnp.float32), jnp.zeros((rows,), jnp.float32))
    highest, total = lax.fori_loop(low_tile, high_tile, gather_stats, start_stats)
    log_total = highest + jnp.log(total)

    def weigh(tile, carry):
        result, remainder = carry
        scores, allowed, keys, values = tile_scores(
            query_rows, key_values, tile, key_tile, tokens, first_keys, mask_rows, heads_here
        )
        weights = jnp.where(allowed, jnp.exp(scores - log_total[:, None]), 0.0)
        rounded = weights.astype(jnp.bfloat16)
        leftover = (weights - rounded.astype(jnp.float32)).astype(jnp.bfloat16)
        result = result + jnp.dot(rounded, values, preferred_element_type=jnp.float32)
        remainder = remainder + jnp.dot(leftover, values, preferred_element_type=jnp.float32)
        return (result, remainder)

    empty = jnp.zeros((rows, HD), jnp.float32)
    result, remainder = lax.fori_loop(low_tile, high_tile, weigh, (empty, empty))
    return (result.astype(jnp.bfloat16), result + remainder, log_total)


def attend_back(
    query_rows,
    key_values,
    grad_rows,
    exact_out,
    log_total,
    tokens,
    first_keys,
    mask_rows,
    heads_here,
    key_tile,
    key_grads,
):
    rows = query_rows.shape[0]
    scale = HD ** (-0.5)
    low_tile, high_tile = tile_range(tokens, first_keys, key_tile)
    delta = jnp.sum(grad_rows.astype(jnp.float32) * exact_out, axis=1)

    def step(tile, carry):
        query_grad, grads_kv = carry
        scores, allowed, keys, values = tile_scores(
            query_rows, key_values, tile, key_tile, tokens, first_keys, mask_rows, heads_here
        )
        weights = jnp.where(allowed, jnp.exp(scores - log_total[:, None]), 0.0)
        weight_grad = contract_cols(grad_rows, values)
        score_grad = (weights * (weight_grad - delta[:, None])).astype(jnp.bfloat16)
        query_grad = query_grad + jnp.dot(score_grad, keys, preferred_element_type=jnp.float32)
        key_part = contract_rows(score_grad, query_rows) * scale
        value_part = contract_rows(weights.astype(jnp.bfloat16), grad_rows)
        start = tile * key_tile
        current = lax.dynamic_slice_in_dim(grads_kv, start, key_tile, 0)
        grads_kv = lax.dynamic_update_slice_in_dim(
            grads_kv, current + jnp.concatenate([key_part, value_part], axis=1), start, 0
        )
        return (query_grad, grads_kv)

    query_grad, key_grads = lax.fori_loop(
        low_tile, high_tile, step, (jnp.zeros((rows, HD), jnp.float32), key_grads)
    )
    return ((query_grad * scale).astype(jnp.bfloat16), key_grads)


def shards(
    hidden_in,
    out_cotangent,
    positions,
    block_mask,
    norm_gain,
    norm_bias,
    qkv_weight,
    proj_weight,
    mlp_gain,
    mlp_bias,
    fc_weight,
    down_weight,
):
    seq_count = lax.axis_size("seq")
    fsdp_count = lax.axis_size("fsdp")
    fsdp_place = lax.axis_index("fsdp")
    count = hidden_in.shape[1]
    width = hidden_in.shape[2]
    length = positions.shape[1]
    heads_here = HEADS // seq_count
    key_tile = 1024
    shapes = (
        norm_gain,
        norm_bias,
        qkv_weight,
        proj_weight,
        mlp_gain,
        mlp_bias,
        fc_weight,
        down_weight,
    )
    totals = [jnp.zeros(p.shape, jnp.float32) for p in shapes]
    results = []
    input_grads = []
    for batch in range(MB):
        inputs = hidden_in[batch].astype(jnp.float32)
        gain_one, bias_one, qkv_full, proj_full = (
            lax.all_gather(norm_gain, "fsdp", axis=0, tiled=True),
            lax.all_gather(norm_bias, "fsdp", axis=0, tiled=True),
            lax.all_gather(qkv_weight, "fsdp", axis=0, tiled=True),
            lax.all_gather(proj_weight, "fsdp", axis=0, tiled=True),
        )
        normed_one, inverse_one = layer_norm(inputs)
        attn_in = (normed_one * gain_one.astype(jnp.float32) + bias_one.astype(jnp.float32)).astype(
            jnp.bfloat16
        )
        projected = jnp.dot(attn_in, qkv_full, preferred_element_type=jnp.float32)
        queries = projected[:, :width].astype(jnp.bfloat16)
        key_values = projected[:, width:].astype(jnp.bfloat16)
        query_heads = lax.all_to_all(queries, "seq", split_axis=1, concat_axis=0, tiled=True)
        key_values_all = lax.all_gather(key_values, ("seq", "fsdp"), axis=0, tiled=True)
        places = positions[batch]
        mask_table = block_mask[batch]
        pieces = []
        for piece in range(seq_count):
            first_token = (piece * fsdp_count + fsdp_place) * count
            tokens, first_keys, mask_rows = piece_rows(places, mask_table, first_token, count)
            query_rows = query_heads[piece * count : (piece + 1) * count].reshape(
                count * heads_here, HD
            )
            rounded_out, exact_out, log_total = attend_piece(
                query_rows, key_values_all, tokens, first_keys, mask_rows, heads_here, key_tile
            )
            pieces.append(
                (tokens, first_keys, mask_rows, query_rows, rounded_out, exact_out, log_total)
            )
        head_out = jnp.concatenate(
            [entry[4].reshape(count, heads_here * HD) for entry in pieces], axis=0
        )
        attn_out = lax.all_to_all(head_out, "seq", split_axis=0, concat_axis=1, tiled=True)
        resid = inputs + jnp.dot(attn_out, proj_full, preferred_element_type=jnp.float32)
        gain_two, bias_two, fc_full, down_full = (
            lax.all_gather(mlp_gain, "fsdp", axis=0, tiled=True),
            lax.all_gather(mlp_bias, "fsdp", axis=0, tiled=True),
            lax.all_gather(fc_weight, "fsdp", axis=0, tiled=True),
            lax.all_gather(down_weight, "fsdp", axis=0, tiled=True),
        )
        normed_two, inverse_two = layer_norm(resid)
        mlp_in = (normed_two * gain_two.astype(jnp.float32) + bias_two.astype(jnp.float32)).astype(
            jnp.bfloat16
        )
        pre_act = jnp.dot(mlp_in, fc_full, preferred_element_type=jnp.float32)
        activ = gelu_tanh(pre_act).astype(jnp.bfloat16)
        results.append(
            (resid + jnp.dot(activ, down_full, preferred_element_type=jnp.float32)).astype(
                jnp.bfloat16
            )
        )
        cotangent = out_cotangent[batch]
        gain_two, bias_two, fc_full, down_full = (
            lax.all_gather(mlp_gain, "fsdp", axis=0, tiled=True),
            lax.all_gather(mlp_bias, "fsdp", axis=0, tiled=True),
            lax.all_gather(fc_weight, "fsdp", axis=0, tiled=True),
            lax.all_gather(down_weight, "fsdp", axis=0, tiled=True),
        )
        activ_grad = contract_cols(cotangent, down_full)
        unused, gelu_pull = jax.vjp(gelu_tanh, pre_act)
        pre_grad = gelu_pull(activ_grad)[0].astype(jnp.bfloat16)
        mlp_in_grad = contract_cols(pre_grad, fc_full)
        mlp_gain_part = jnp.sum(mlp_in_grad * normed_two, axis=0)
        mlp_bias_part = jnp.sum(mlp_in_grad, axis=0)
        down_grad = lax.psum_scatter(
            contract_rows(activ, cotangent).astype(jnp.bfloat16),
            "fsdp",
            scatter_dimension=0,
            tiled=True,
        ).astype(jnp.float32)
        fc_grad, mlp_gain_grad, mlp_bias_grad = (
            lax.psum_scatter(
                contract_rows(mlp_in, pre_grad).astype(jnp.bfloat16),
                "fsdp",
                scatter_dimension=0,
                tiled=True,
            ).astype(jnp.float32),
            lax.psum_scatter(
                mlp_gain_part.astype(jnp.bfloat16), "fsdp", scatter_dimension=0, tiled=True
            ).astype(jnp.float32),
            lax.psum_scatter(
                mlp_bias_part.astype(jnp.bfloat16), "fsdp", scatter_dimension=0, tiled=True
            ).astype(jnp.float32),
        )
        resid_grad = cotangent.astype(jnp.float32) + norm_back(
            mlp_in_grad * gain_two.astype(jnp.float32), normed_two, inverse_two
        )
        branch_grad = resid_grad.astype(jnp.bfloat16)
        gain_one, bias_one, qkv_full, proj_full = (
            lax.all_gather(norm_gain, "fsdp", axis=0, tiled=True),
            lax.all_gather(norm_bias, "fsdp", axis=0, tiled=True),
            lax.all_gather(qkv_weight, "fsdp", axis=0, tiled=True),
            lax.all_gather(proj_weight, "fsdp", axis=0, tiled=True),
        )
        heads_grad = contract_cols(branch_grad, proj_full).astype(jnp.bfloat16)
        grad_heads_local = lax.all_to_all(
            heads_grad, "seq", split_axis=1, concat_axis=0, tiled=True
        )
        key_grads = jnp.zeros((length, 2 * HD), jnp.float32)
        query_grads = []
        for piece in range(seq_count):
            tokens, first_keys, mask_rows, query_rows, rounded_out, exact_out, log_total = pieces[
                piece
            ]
            grad_rows = grad_heads_local[piece * count : (piece + 1) * count].reshape(
                count * heads_here, HD
            )
            query_grad, key_grads = attend_back(
                query_rows,
                key_values_all,
                grad_rows,
                exact_out,
                log_total,
                tokens,
                first_keys,
                mask_rows,
                heads_here,
                key_tile,
                key_grads,
            )
            query_grads.append(query_grad.reshape(count, heads_here * HD))
        query_grad_local = lax.all_to_all(
            jnp.concatenate(query_grads, axis=0), "seq", split_axis=0, concat_axis=1, tiled=True
        )
        kv_grad = lax.psum_scatter(
            key_grads, ("seq", "fsdp"), scatter_dimension=0, tiled=True
        ).astype(jnp.bfloat16)
        qkv_grad_rows = jnp.concatenate([query_grad_local, kv_grad], axis=1)
        attn_in_grad = contract_cols(qkv_grad_rows, qkv_full)
        norm_gain_part = jnp.sum(attn_in_grad * normed_one, axis=0)
        norm_bias_part = jnp.sum(attn_in_grad, axis=0)
        qkv_grad, proj_grad, gain_grad, bias_grad = (
            lax.psum_scatter(
                contract_rows(attn_in, qkv_grad_rows).astype(jnp.bfloat16),
                "fsdp",
                scatter_dimension=0,
                tiled=True,
            ).astype(jnp.float32),
            lax.psum_scatter(
                contract_rows(attn_out, branch_grad).astype(jnp.bfloat16),
                "fsdp",
                scatter_dimension=0,
                tiled=True,
            ).astype(jnp.float32),
            lax.psum_scatter(
                norm_gain_part.astype(jnp.bfloat16), "fsdp", scatter_dimension=0, tiled=True
            ).astype(jnp.float32),
            lax.psum_scatter(
                norm_bias_part.astype(jnp.bfloat16), "fsdp", scatter_dimension=0, tiled=True
            ).astype(jnp.float32),
        )
        updates = (
            gain_grad,
            bias_grad,
            qkv_grad,
            proj_grad,
            mlp_gain_grad,
            mlp_bias_grad,
            fc_grad,
            down_grad,
        )
        totals = [old + new for old, new in zip(totals, updates)]
        input_grads.append(
            (
                resid_grad
                + norm_back(attn_in_grad * gain_one.astype(jnp.float32), normed_one, inverse_one)
            ).astype(jnp.bfloat16)
        )
    summed = (
        lax.psum(totals[0].astype(jnp.bfloat16), "seq").astype(jnp.float32),
        lax.psum(totals[1].astype(jnp.bfloat16), "seq").astype(jnp.float32),
        lax.psum(totals[2].astype(jnp.bfloat16), "seq").astype(jnp.float32),
        lax.psum(totals[3].astype(jnp.bfloat16), "seq").astype(jnp.float32),
        lax.psum(totals[4].astype(jnp.bfloat16), "seq").astype(jnp.float32),
        lax.psum(totals[5].astype(jnp.bfloat16), "seq").astype(jnp.float32),
        lax.psum(totals[6].astype(jnp.bfloat16), "seq").astype(jnp.float32),
        lax.psum(totals[7].astype(jnp.bfloat16), "seq").astype(jnp.float32),
    )
    return (
        jnp.stack(results),
        jnp.stack(input_grads),
        summed[0],
        summed[1],
        summed[2],
        summed[3],
        summed[4],
        summed[5],
        summed[6],
        summed[7],
    )


def solution(mesh):
    in_specs = (
        P(None, ("seq", "fsdp"), None),
        P(None, ("seq", "fsdp"), None),
        P(),
        P(),
        P("fsdp"),
        P("fsdp"),
        P("fsdp", None),
        P("fsdp", None),
        P("fsdp"),
        P("fsdp"),
        P("fsdp", None),
        P("fsdp", None),
    )
    out_specs = (
        P(None, ("seq", "fsdp"), None),
        P(None, ("seq", "fsdp"), None),
        P("fsdp"),
        P("fsdp"),
        P("fsdp", None),
        P("fsdp", None),
        P("fsdp"),
        P("fsdp"),
        P("fsdp", None),
        P("fsdp", None),
    )
    return jax.shard_map(shards, mesh=mesh, in_specs=in_specs, out_specs=out_specs, check_vma=False)
```

profile of v0, /device:TPU:0, one launch (start us, length us, event | category | flops | bytes accessed | tf_op | source)
XLA Modules:
  0.0 5299.5 jit_solution(14530334657540480392)
XLA Ops:
  8.6 22.4 all-gather.1
  50.0 100.9 %all-gather.11.cloned.1.call-done = bf16[2048,2304]{1,0:T(8,128)(2,1)} async-done(((bf16[256,2304]{1,0:T(8,128)(2,1)}), bf16[2048,2304]{1,0:T(8,128)(2,1)}) %all-gather.11.cloned.1.call-update) | async-done | bytes 9437200 | tf_op jit(solution)/shard_map/all_gather | solution.py:193
  232.4 36.1 while.375
  283.2 26.6 while.373
  469.8 34.1 all-gather.2
  514.5 519.7 %all-gather.17.cloned.1.call-done = bf16[2048,8192]{1,0:T(8,128)(2,1)} async-done(((bf16[256,8192]{1,0:T(8,128)(2,1)}), bf16[2048,8192]{1,0:T(8,128)(2,1)}) %all-gather.17.cloned.1.call-update) | async-done | bytes 33554448 | tf_op jit(solution)/shard_map/all_gather | solution.py:228
  1070.0 603.4 %all-gather.19.cloned.1.call-done = bf16[8192,2048]{1,0:T(8,128)(2,1)} async-done(((bf16[1024,2048]{1,0:T(8,128)(2,1)}), bf16[8192,2048]{1,0:T(8,128)(2,1)}) %all-gather.19.cloned.1.call-update) | async-done | bytes 33554448 | tf_op jit(solution)/shard_map/all_gather | solution.py:229
  1793.5 24.8 while.377
  1854.6 25.4 while.381
  1882.9 37.8 while.382
  1923.6 50.7 while.383
  1976.2 21.0 while.379
  2025.3 93.9 %reduce-scatter.13.cloned.1.call-done = f32[128,256]{0,1:T(8,128)} async-done(((f32[4096,256]{0,1:T(8,128)}), f32[128,256]{0,1:T(8,128)}) %reduce-scatter.13.cloned.1.call-update) | async-done | bytes 131088 | tf_op jit(solution)/shard_map/reduce_scatter | solution.py:315
  2138.5 124.0 %reduce-scatter.11.cloned.1.call-done = f32[128,256]{0,1:T(8,128)} async-done(((f32[4096,256]{0,1:T(8,128)}), f32[128,256]{0,1:T(8,128)}) %reduce-scatter.11.cloned.1.call-update) | async-done | bytes 131088 | tf_op jit(solution)/shard_map/reduce_scatter | solution.py:315
  2356.1 56.9 %reduce-scatter.21.cloned.1.call-done = bf16[256,2048]{1,0:T(8,128)(2,1)} async-done(((bf16[2048,2048]{1,0:T(8,128)(2,1)}), bf16[256,2048]{1,0:T(8,128)(2,1)}) %reduce-scatter.21.cloned.1.call-update) | async-done | bytes 1048592 | tf_op jit(solution)/shard_map/reduce_scatter | solution.py:329
  2413.1 152.6 %reduce-scatter.19.cloned.1.call-done = bf16[256,2048]{1,0:T(8,128)(2,1)} async-done(((bf16[2048,2048]{1,0:T(8,128)(2,1)}), bf16[256,2048]{1,0:T(8,128)(2,1)}) %reduce-scatter.19.cloned.1.call-update) | async-done | bytes 1048592 | tf_op jit(solution)/shard_map/reduce_scatter | solution.py:329
  2568.5 163.2 %reduce-scatter.17.cloned.1.call-done = bf16[256,2304]{1,0:T(8,128)(2,1)} async-done(((bf16[2048,2304]{1,0:T(8,128)(2,1)}), bf16[256,2304]{1,0:T(8,128)(2,1)}) %reduce-scatter.17.cloned.1.call-update) | async-done | bytes 1179664 | tf_op jit(solution)/shard_map/reduce_scatter | solution.py:323
  2731.7 165.9 %reduce-scatter.15.cloned.1.call-done = bf16[256,2304]{1,0:T(8,128)(2,1)} async-done(((bf16[2048,2304]{1,0:T(8,128)(2,1)}), bf16[256,2304]{1,0:T(8,128)(2,1)}) %reduce-scatter.15.cloned.1.call-update) | async-done | bytes 1179664 | tf_op jit(solution)/shard_map/reduce_scatter | solution.py:323
  2900.5 542.8 %reduce-scatter.25.cloned.1.call-done = bf16[256,8192]{1,0:T(8,128)(2,1)} async-done(((bf16[2048,8192]{1,0:T(8,128)(2,1)}), bf16[256,8192]{1,0:T(8,128)(2,1)}) %reduce-scatter.25.cloned.1.call-update) | async-done | bytes 4194320 | tf_op jit(solution)/shard_map/reduce_scatter | solution.py:262
  3443.3 546.3 %reduce-scatter.23.cloned.1.call-done = bf16[256,8192]{1,0:T(8,128)(2,1)} async-done(((bf16[2048,8192]{1,0:T(8,128)(2,1)}), bf16[256,8192]{1,0:T(8,128)(2,1)}) %reduce-scatter.23.cloned.1.call-update) | async-done | bytes 4194320 | tf_op jit(solution)/shard_map/reduce_scatter | solution.py:262
  3996.7 539.3 %reduce-scatter.29.cloned.1.call-done = bf16[1024,2048]{1,0:T(8,128)(2,1)} async-done(((bf16[8192,2048]{1,0:T(8,128)(2,1)}), bf16[1024,2048]{1,0:T(8,128)(2,1)}) %reduce-scatter.29.cloned.1.call-update) | async-done | bytes 4194320 | tf_op jit(solution)/shard_map/reduce_scatter | solution.py:255
  4536.0 546.3 %reduce-scatter.27.cloned.1.call-done = bf16[1024,2048]{1,0:T(8,128)(2,1)} async-done(((bf16[8192,2048]{1,0:T(8,128)(2,1)}), bf16[1024,2048]{1,0:T(8,128)(2,1)}) %reduce-scatter.27.cloned.1.call-update) | async-done | bytes 4194320 | tf_op jit(solution)/shard_map/reduce_scatter | solution.py:255
  5125.2 35.4 all-reduce.8
  5173.1 106.4 %all-reduce.13.cloned.1.call-done = (bf16[256,2304]{1,0:T(8,128)(2,1)}, bf16[256,2048]{1,0:T(8,128)(2,1)}, bf16[256,8192]{1,0:T(8,128)(2,1)}, bf16[1024,2048]{1,0:T(8,128)(2,1)}) async-done(((bf16[256,2304]{1,0:T(8,128)(2,1)}, bf16[256,2048]{1,0:T(8,128)(2,1)}, bf16[256,8192]{1,0:T(8,128)(2,1)}, bf16[1024,2048]{1,0:T(8,128)(2,1)}), (bf16[256,2304]{1,0:T(8,128)(2,1)}, bf16[256,2048]{1,0:T(8,128)(2,1)}, ...) | async-done | bytes 10616848 | tf_op jit(solution)/shard_map/psum | solution.py:362
  (1439 shorter events, 1092.7 us)
Async XLA Ops:
  7.2 143.7 %all-gather.11.cloned.1.call-start = ((), (), s32[]{:S(2)}) async-start(), calls=%async_computation.18 | async-start | bytes 10616832 | tf_op jit(solution)/shard_map/all_gather | solution.py:193
  7.9 205.3 %all-gather.21.cloned.1.call-start = ((), (), s32[]{:S(2)}) async-start(), calls=%async_computation.23 | async-start | bytes 2162688 | tf_op jit(solution)/shard_map/all_gather | solution.py:204
  156.8 204.7 %all-gather.13.cloned.1.call-start = ((), (), s32[]{:S(2)}) async-start(), calls=%async_computation.19 | async-start | bytes 2162688 | tf_op jit(solution)/shard_map/all_gather | solution.py:204
  162.7 343.6 %all-gather.15.cloned.1.call-start = ((), (), s32[]{:S(2)}) async-start(), calls=%async_computation.20 | async-start | bytes 9437184 | tf_op jit(solution)/shard_map/all_gather | solution.py:194
  163.3 870.9 %all-gather.17.cloned.1.call-start = ((), (), s32[]{:S(2)}) async-start(), calls=%async_computation.21 | async-start | bytes 37748736 | tf_op jit(solution)/shard_map/all_gather | solution.py:228
  163.9 1509.5 %all-gather.19.cloned.1.call-start = ((), (), s32[]{:S(2)}) async-start(), calls=%async_computation.22 | async-start | bytes 37748736 | tf_op jit(solution)/shard_map/all_gather | solution.py:229
  168.5 21.8 all-to-all-start.2
  190.3 16.0 all-to-all-start
  357.3 90.0 %all-to-all-start.3 = ((bf16[4,128,512]{2,1,0:T(8,128)(2,1)}), bf16[4,128,512]{2,1,0:T(8,128)(2,1)}, u32[]{:S(2)}, u32[]{:S(2)}) async-start(bf16[4,128,512]{2,1,0:T(8,128)(2,1)} %bitcast.34), calls=%async_computation.3 | async-start | bytes 1048576 | tf_op jit(solution)/shard_map/all_to_all | solution.py:223
  447.3 57.9 %all-to-all-start.1 = ((bf16[4,128,512]{2,1,0:T(8,128)(2,1)}), bf16[4,128,512]{2,1,0:T(8,128)(2,1)S(1)}, u32[]{:S(2)}, u32[]{:S(2)}) async-start(bf16[4,128,512]{2,1,0:T(8,128)(2,1)} %bitcast.17), calls=%async_computation.1 | async-start | bytes 1048576 | tf_op jit(solution)/shard_map/all_to_all | solution.py:223
  503.9 1244.2 %copy-start.115 = (f32[8,1,256]{2,1,0:T(1,128)}, f32[8,1,256]{2,1,0:T(1,128)S(1)}, u32[]{:S(2)}) copy-start(f32[8,1,256]{2,1,0:T(1,128)S(1)} %convert_element_type.654) | copy-start | bytes 24580
  1759.4 12.3 all-to-all-start.4
  1771.6 61.1 %all-to-all-start.6 = ((bf16[128,4,512]{2,0,1:T(8,128)(2,1)}), bf16[128,4,512]{2,0,1:T(8,128)(2,1)}, u32[]{:S(2)}, u32[]{:S(2)}) async-start(bf16[128,4,512]{2,0,1:T(8,128)(2,1)} %bitcast.529), calls=%async_computation.7 | async-start | bytes 1048576 | tf_op jit(solution)/shard_map/all_to_all | solution.py:286
  1775.8 343.3 %reduce-scatter.13.cloned.1.call-start = ((), (), s32[]{:S(2)}) async-start(), calls=%async_computation.25 | async-start | bytes 4325376 | tf_op jit(solution)/shard_map/reduce_scatter | solution.py:315
  1974.3 288.2 %reduce-scatter.11.cloned.1.call-start = ((), (), s32[]{:S(2)}) async-start(), calls=%async_computation.24 | async-start | bytes 4325376 | tf_op jit(solution)/shard_map/reduce_scatter | solution.py:315
  1997.2 415.8 %reduce-scatter.21.cloned.1.call-start = ((), (), s32[]{:S(2)}) async-start(), calls=%async_computation.29 | async-start | bytes 9437184 | tf_op jit(solution)/shard_map/reduce_scatter | solution.py:329
  2004.3 561.3 %reduce-scatter.19.cloned.1.call-start = ((), (), s32[]{:S(2)}) async-start(), calls=%async_computation.28 | async-start | bytes 9437184 | tf_op jit(solution)/shard_map/reduce_scatter | solution.py:329
  2011.4 720.3 %reduce-scatter.17.cloned.1.call-start = ((), (), s32[]{:S(2)}) async-start(), calls=%async_computation.27 | async-start | bytes 10616832 | tf_op jit(solution)/shard_map/reduce_scatter | solution.py:323
  2125.5 772.1 %reduce-scatter.15.cloned.1.call-start = ((), (), s32[]{:S(2)}) async-start(), calls=%async_computation.26 | async-start | bytes 10616832 | tf_op jit(solution)/shard_map/reduce_scatter | solution.py:323
  2268.9 1174.4 %reduce-scatter.25.cloned.1.call-start = ((), (), s32[]{:S(2)}) async-start(), calls=%async_computation.31 | async-start | bytes 37748736 | tf_op jit(solution)/shard_map/reduce_scatter | solution.py:262
  2286.3 1703.4 %reduce-scatter.23.cloned.1.call-start = ((), (), s32[]{:S(2)}) async-start(), calls=%async_computation.30 | async-start | bytes 37748736 | tf_op jit(solution)/shard_map/reduce_scatter | solution.py:262
  2303.3 2232.6 %reduce-scatter.29.cloned.1.call-start = ((), (), s32[]{:S(2)}) async-start(), calls=%async_computation.33 | async-start | bytes 37748736 | tf_op jit(solution)/shard_map/reduce_scatter | solution.py:255
  2319.9 2762.4 %reduce-scatter.27.cloned.1.call-start = ((), (), s32[]{:S(2)}) async-start(), calls=%async_computation.32 | async-start | bytes 37748736 | tf_op jit(solution)/shard_map/reduce_scatter | solution.py:255
  2336.2 2943.2 %all-reduce.13.cloned.1.call-start = ((), (), s32[]{:S(2)}) async-start(), calls=%async_computation.34 | async-start | bytes 21233664 | tf_op jit(solution)/shard_map/psum | solution.py:362
  (239 other events, 11613.3 us)
Sparse Core Ops, SparseCore 0:
  10.2 140.6 all-gather.10
  156.9 56.3 all-gather.20
  216.2 54.5 all-gather.12
  272.8 123.6 all-gather.14
  397.9 636.2 all-gather.16
  1035.6 637.6 all-gather.18
  1974.4 144.6 reduce-scatter.12
  2121.4 141.1 reduce-scatter.10
  2266.8 146.2 reduce-scatter.20
  2417.5 148.0 reduce-scatter.18
  2569.2 162.4 reduce-scatter.16
  2735.2 162.3 reduce-scatter.14
  2901.4 541.9 reduce-scatter.24
  3447.0 542.6 reduce-scatter.22
  3993.3 542.6 reduce-scatter.28
  4539.6 542.6 reduce-scatter.26
  5090.2 189.2 all-reduce.12
where the time goes:
time: 5300 us
  waiting for transfers between devices  4280 us (81%)
  matrix products  499 us (9%)
  local copies, waits for them, and re-layouts  170 us (3%)
  blocking collectives  157 us (3%)
  other arithmetic  131 us (2%)
    reduce_scatter x2, waiting for transfers between devices, shards(): lax.psum_scatter(contract_rows(mlp_in, pre_grad).astype(jnp.bfloat16), 'f...  1090 us
    reduce_scatter x2, waiting for transfers between devices, shards(): lax.psum_scatter(contract_rows(activ, cotangent).astype(jnp.bfloat16), 'f...  1090 us
    all_gather x1, waiting for transfers between devices, shards(): lax.all_gather(down_weight, 'fsdp', axis=0, tiled=True)  603 us
    all_gather x1, waiting for transfers between devices, shards(): lax.all_gather(fc_weight, 'fsdp', axis=0, tiled=True)  520 us
    reduce_scatter x2, waiting for transfers between devices, shards(): lax.psum_scatter(contract_rows(attn_in, qkv_grad_rows).astype(jnp.bfloat1...  329 us
    dot_general x72, matrix products, contract_cols(): lax.dot_general(left, right, (((1,), (1,)), ((), ())), preferred_element_...  241 us
    reduce_scatter x2, waiting for transfers between devices, shards(): lax.psum_scatter(key_grads, ('seq', 'fsdp'), scatter_dimension=0, tiled=T...  218 us
    reduce_scatter x2, waiting for transfers between devices, shards(): lax.psum_scatter(contract_rows(attn_out, branch_grad).astype(jnp.bfloat16...  210 us
  transfers between devices with their start and end apart: 23, of which 17 were waited for; matrix products, arithmetic and copies ran while one was open for 10% of the time, Pallas kernels for 0%

commit v1 on v0

v1 whole, which is shorter than its diff:
```python
import functools
import math

import jax
import jax.numpy as jnp
from jax import lax
from jax.experimental import pallas as pl
from jax.experimental.pallas import tpu as pltpu
from jax.sharding import PartitionSpec as P

HEADS = 16
HD = 128
MB = 2
BLOCK = 256
EPS = 1e-05
NEG_FILL = -1e30
SCALE = HD ** (-0.5)
LOG2E = math.log2(math.e)
BF = jnp.bfloat16
F32 = jnp.float32


def dot_rows(left, right):
    return lax.dot_general(left, right, (((0,), (0,)), ((), ())), preferred_element_type=F32)


def dot_cols(left, right):
    return lax.dot_general(left, right, (((1,), (1,)), ((), ())), preferred_element_type=F32)


def dot_plain(left, right):
    return lax.dot_general(left, right, (((1,), (0,)), ((), ())), preferred_element_type=F32)


def tie(value, after):
    return lax.optimization_barrier((value, after))[0]


def core_swap(value):
    return lax.ppermute(value, "seq", [(s, s ^ 1) for s in range(4)])


def chip_swap(value):
    return lax.ppermute(value, "seq", [(s, s ^ 2) for s in range(4)])


def seq_gather(value):
    across = chip_swap(value)
    pair = core_swap(value)
    pair_across = core_swap(across)
    return jnp.stack([value, pair, across, pair_across])


def seq_scatter(parts):
    far = core_swap(parts[3].astype(BF))
    near = core_swap(parts[1].astype(BF))
    across = chip_swap((parts[2] + far.astype(F32)).astype(BF))
    return parts[0] + near.astype(F32) + across.astype(F32)


def ring_order(count):
    return [2 * i for i in range(count // 2)] + [2 * i + 1 for i in reversed(range(count // 2))]


class Ring:
    def __init__(self, count):
        order = ring_order(count)
        self.count = count
        self.up = [(order[i], order[(i + 1) % count]) for i in range(count)]
        self.down = [(order[(i + 1) % count], order[i]) for i in range(count)]
        place = lax.axis_index("fsdp")
        half = count // 2
        self.place = place
        self.at = jnp.where(place % 2 == 0, place // 2, count - 1 - place // 2)

    def owner(self, step):
        count, half = self.count, self.count // 2
        at = lax.rem(self.at + (step + count), count)
        return jnp.where(at < half, 2 * at, 2 * (count - 1 - at) + 1)

    def gather(self, value):
        count = self.count
        rows = value.shape[0]
        out = jnp.zeros((count,) + value.shape, value.dtype)
        put = lambda out, piece, owner, row: lax.dynamic_update_slice(
            out, piece[None], (owner, row) + (0,) * (value.ndim - 1)
        )
        out = put(out, value, self.place, 0)
        low = high = value
        for step in range(1, count // 2):
            low = lax.ppermute(low, "fsdp", self.up)
            high = lax.ppermute(high, "fsdp", self.down)
            out = put(out, low, self.owner(-step), 0)
            out = put(out, high, self.owner(step), 0)
        half = rows // 2
        low = lax.ppermute(low[:half], "fsdp", self.up)
        high = lax.ppermute(high[half:], "fsdp", self.down)
        out = put(out, low, self.owner(-(count // 2)), 0)
        return put(out, high, self.owner(count // 2), half)

    def scatter(self, chunk):
        count = self.count
        middle = chunk(self.owner(count // 2))
        half = middle.shape[0] // 2
        up = middle[:half].astype(BF)
        down = middle[half:].astype(BF)
        for step in range(count // 2 - 1, -1, -1):
            up = lax.ppermute(up, "fsdp", self.up).astype(F32)
            down = lax.ppermute(down, "fsdp", self.down).astype(F32)
            if step == count // 2 - 1:
                mine = chunk(self.owner(step))
                up = jnp.concatenate([mine[:half] + up, mine[half:]], axis=0)
                mine = chunk(self.owner(-step))
                down = jnp.concatenate([mine[:half], mine[half:] + down], axis=0)
            elif step:
                up = chunk(self.owner(step)) + up
                down = chunk(self.owner(-step)) + down
            else:
                return chunk(self.place) + up + down
            up = up.astype(BF)
            down = down.astype(BF)


def attend_kernel(tables, q_ref, kv_ref, first_ref, out_ref, log_ref, stack, high, total, result, *, heads, blocks):
    batch, piece = pl.program_id(0), pl.program_id(1)
    count = q_ref.shape[2]
    base = (batch * pl.num_programs(1) + piece) * (blocks + 4)
    chunk, low_tile, high_tile = tables[base], tables[base + 1], tables[base + 2]
    for h in range(heads):
        stack[h * count : (h + 1) * count, :] = q_ref[0, 0, :, h * HD : (h + 1) * HD]
    high[...] = jnp.full_like(high, NEG_FILL)
    total[...] = jnp.zeros_like(total)
    result[...] = jnp.zeros_like(result)
    tokens = chunk * count + lax.broadcasted_iota(jnp.int32, (1, count), 1)
    first = first_ref[0, 0]

    def step(tile, carry):
        @pl.when(tables[base + 4 + tile] != 0)
        def _():
            part = kv_ref[pl.ds(2 * tile, 2), 0].reshape(BLOCK, 2 * HD)
            keys, values = part[:, :HD], part[:, HD:]
            scores = dot_cols(keys, stack[...])
            index = tile * BLOCK + lax.broadcasted_iota(jnp.int32, (BLOCK, count), 0)
            allowed = (index <= tokens) & (index >= first)
            weights, scales = [], []
            for h in range(heads):
                lanes = slice(h * count, (h + 1) * count)
                score = jnp.where(allowed, scores[:, lanes] * (SCALE * LOG2E), NEG_FILL)
                old = high[:, lanes]
                new = jnp.maximum(old, jnp.max(score, axis=0, keepdims=True))
                weight = jnp.exp2(score - new)
                scale = jnp.exp2(old - new)
                high[:, lanes] = new
                total[:, lanes] = total[:, lanes] * scale + jnp.sum(weight, axis=0, keepdims=True)
                weights.append(weight.astype(BF))
                scales.append(scale)
            added = dot_rows(values, jnp.concatenate(weights, axis=1))
            result[...] = result[...] * jnp.concatenate(scales, axis=1) + added

        return carry

    lax.fori_loop(low_tile, high_tile, step, 0)
    final = result[...] / total[...]
    logs = high[...] + jnp.log2(total[...])
    for h in range(heads):
        lanes = slice(h * count, (h + 1) * count)
        out_ref[0, 0, :, h * HD : (h + 1) * HD] = final[:, lanes].T.astype(BF)
        log_ref[0, 0, h : h + 1, :] = logs[:, lanes]


def attend_back_kernel(
    tables,
    q_ref,
    kv_ref,
    first_ref,
    out_ref,
    log_ref,
    grad_ref,
    dq_ref,
    dkv_ref,
    stack,
    grads,
    logs,
    deltas,
    dq_sum,
    dkv_sum,
    *,
    heads,
    blocks,
):
    batch, piece = pl.program_id(0), pl.program_id(1)
    count = q_ref.shape[2]
    base = (batch * pl.num_programs(1) + piece) * (blocks + 4)
    chunk, low_tile, high_tile = tables[base], tables[base + 1], tables[base + 2]

    @pl.when(piece == 0)
    def _():
        dkv_sum[...] = jnp.zeros_like(dkv_sum)

    for h in range(heads):
        rows = slice(h * count, (h + 1) * count)
        cols = slice(h * HD, (h + 1) * HD)
        stack[rows, :] = q_ref[0, 0, :, cols]
        grad = grad_ref[0, 0, :, cols]
        grads[rows, :] = grad
        product = grad.astype(F32) * out_ref[0, 0, :, cols].astype(F32)
        deltas[:, rows] = jnp.sum(product.T, axis=0, keepdims=True)
        logs[:, rows] = log_ref[0, 0, h : h + 1, :]
    dq_sum[...] = jnp.zeros_like(dq_sum)
    tokens = chunk * count + lax.broadcasted_iota(jnp.int32, (1, count), 1)
    first = first_ref[0, 0]

    def step(tile, carry):
        @pl.when(tables[base + 4 + tile] != 0)
        def _():
            part = kv_ref[pl.ds(2 * tile, 2), 0].reshape(BLOCK, 2 * HD)
            keys, values = part[:, :HD], part[:, HD:]
            scores = dot_cols(keys, stack[...])
            pulls = dot_cols(values, grads[...])
            index = tile * BLOCK + lax.broadcasted_iota(jnp.int32, (BLOCK, count), 0)
            allowed = (index <= tokens) & (index >= first)
            weights, score_grads = [], []
            for h in range(heads):
                lanes = slice(h * count, (h + 1) * count)
                score = jnp.where(allowed, scores[:, lanes] * (SCALE * LOG2E), NEG_FILL)
                weight = jnp.exp2(score - logs[:, lanes])
                weights.append(weight.astype(BF))
                score_grads.append((weight * (pulls[:, lanes] - deltas[:, lanes])).astype(BF))
            weight = jnp.concatenate(weights, axis=1)
            score_grad = jnp.concatenate(score_grads, axis=1)
            dv = dot_plain(weight, grads[...])
            dk = dot_plain(score_grad, stack[...])
            dq_sum[...] += dot_rows(keys, score_grad)
            both = jnp.concatenate([dk, dv], axis=1).reshape(2, BLOCK // 2, 2 * HD)
            dkv_sum[pl.ds(2 * tile, 2)] += both

        return carry

    lax.fori_loop(low_tile, high_tile, step, 0)
    for h in range(heads):
        lanes = slice(h * count, (h + 1) * count)
        dq_ref[0, 0, :, h * HD : (h + 1) * HD] = (dq_sum[:, lanes] * SCALE).T.astype(BF)

    @pl.when(piece == pl.num_programs(1) - 1)
    def _():
        dkv_ref[:, 0, :, :HD] = (dkv_sum[:, :, :HD] * SCALE).astype(BF)
        dkv_ref[:, 0, :, HD:] = dkv_sum[:, :, HD:].astype(BF)


def attend(tables, first, queries, key_values, blocks):
    pieces, batches, count, width = queries.shape
    heads = width // HD
    chunks = key_values.shape[0]
    row_spec = pl.BlockSpec((1, 1, count, width), lambda b, i, t: (i, b, 0, 0))
    kv_spec = pl.BlockSpec((chunks, 1, count, 2 * HD), lambda b, i, t: (0, b, 0, 0))
    first_spec = pl.BlockSpec((1, 1, 1, count), lambda b, i, t: (i, b, 0, 0))
    log_spec = pl.BlockSpec((1, 1, heads, count), lambda b, i, t: (i, b, 0, 0))
    rows = heads * count
    return pl.pallas_call(
        functools.partial(attend_kernel, heads=heads, blocks=blocks),
        out_shape=(
            jax.ShapeDtypeStruct(queries.shape, BF),
            jax.ShapeDtypeStruct((pieces, batches, heads, count), F32),
        ),
        grid_spec=pltpu.PrefetchScalarGridSpec(
            num_scalar_prefetch=1,
            grid=(batches, pieces),
            in_specs=[row_spec, kv_spec, first_spec],
            out_specs=[row_spec, log_spec],
            scratch_shapes=[
                pltpu.VMEM((rows, HD), BF),
                pltpu.VMEM((1, rows), F32),
                pltpu.VMEM((1, rows), F32),
                pltpu.VMEM((HD, rows), F32),
            ],
        ),
        compiler_params=pltpu.CompilerParams(vmem_limit_bytes=40 << 20),
        cost_estimate=pl.CostEstimate(flops=4 * rows * HD * chunks * count * pieces, bytes_accessed=16 << 20, transcendentals=rows * chunks * count * pieces),
        name="attend",
    )(tables, queries, key_values, first)


def attend_back(tables, first, queries, key_values, out, logs, grads, blocks):
    pieces, batches, count, width = queries.shape
    heads = width // HD
    chunks = key_values.shape[0]
    row_spec = pl.BlockSpec((1, 1, count, width), lambda b, i, t: (i, b, 0, 0))
    kv_spec = pl.BlockSpec((chunks, 1, count, 2 * HD), lambda b, i, t: (0, b, 0, 0))
    first_spec = pl.BlockSpec((1, 1, 1, count), lambda b, i, t: (i, b, 0, 0))
    log_spec = pl.BlockSpec((1, 1, heads, count), lambda b, i, t: (i, b, 0, 0))
    rows = heads * count
    return pl.pallas_call(
        functools.partial(attend_back_kernel, heads=heads, blocks=blocks),
        out_shape=(
            jax.ShapeDtypeStruct(queries.shape, BF),
            jax.ShapeDtypeStruct(key_values.shape, BF),
        ),
        grid_spec=pltpu.PrefetchScalarGridSpec(
            num_scalar_prefetch=1,
            grid=(batches, pieces),
            in_specs=[row_spec, kv_spec, first_spec, row_spec, log_spec, row_spec],
            out_specs=[row_spec, kv_spec],
            scratch_shapes=[
                pltpu.VMEM((rows, HD), BF),
                pltpu.VMEM((rows, HD), BF),
                pltpu.VMEM((1, rows), F32),
                pltpu.VMEM((1, rows), F32),
                pltpu.VMEM((HD, rows), F32),
                pltpu.VMEM((chunks, count, 2 * HD), F32),
            ],
        ),
        compiler_params=pltpu.CompilerParams(vmem_limit_bytes=60 << 20),
        cost_estimate=pl.CostEstimate(flops=10 * rows * HD * chunks * count * pieces, bytes_accessed=32 << 20, transcendentals=rows * chunks * count * pieces),
        name="attend_back",
    )(tables, queries, key_values, first, out, logs, grads)


def layer_norm(values):
    mean = jnp.mean(values, axis=-1, keepdims=True)
    center = values - mean
    inverse = lax.rsqrt(jnp.mean(center * center, axis=-1, keepdims=True) + EPS)
    return center * inverse, inverse


def norm_back(grad, normed, inverse):
    return inverse * (
        grad
        - jnp.mean(grad, axis=-1, keepdims=True)
        - normed * jnp.mean(grad * normed, axis=-1, keepdims=True)
    )


def gelu_tanh(values):
    return jax.nn.gelu(values, approximate=True)


def shards(
    hidden_in,
    out_cotangent,
    positions,
    block_mask,
    norm_gain,
    norm_bias,
    qkv_weight,
    proj_weight,
    mlp_gain,
    mlp_bias,
    fc_weight,
    down_weight,
):
    seq_count = lax.axis_size("seq")
    fsdp_count = lax.axis_size("fsdp")
    s = lax.axis_index("seq")
    f = lax.axis_index("fsdp")
    ring = Ring(fsdp_count)
    count = hidden_in.shape[1]
    width = hidden_in.shape[2]
    length = positions.shape[1]
    blocks = length // BLOCK
    shard = qkv_weight.shape[0]
    ff = fc_weight.shape[1]
    ff_shard = down_weight.shape[0]
    heads_here = HEADS // seq_count
    head_cols = heads_here * HD
    quarter = ff_shard // seq_count
    tokens_here = MB * count
    group = seq_count * tokens_here

    chunk_ids = jnp.stack([(s ^ i) * fsdp_count + f for i in range(seq_count)]).astype(jnp.int32)
    token_ids = chunk_ids[:, None] * count + jnp.arange(count, dtype=jnp.int32)[None]
    first = token_ids[:, None, :] - jnp.stack(
        [lax.dynamic_slice_in_dim(positions, chunk_ids[i] * count, count, 1) for i in range(seq_count)]
    )
    first = first[:, :, None, :]
    high_tiles = (chunk_ids * count + count - 1) // BLOCK + 1
    tables = jnp.concatenate(
        [
            jnp.broadcast_to(chunk_ids[None, :, None], (MB, seq_count, 1)),
            (first[:, :, 0, :1] // BLOCK).transpose(1, 0, 2),
            jnp.broadcast_to(high_tiles[None, :, None], (MB, seq_count, 1)),
            jnp.zeros((MB, seq_count, 1), jnp.int32),
            jnp.stack([block_mask[:, (chunk_ids[i] * count) // BLOCK] for i in range(seq_count)], axis=1),
        ],
        axis=2,
    ).reshape(-1)

    vectors = jnp.stack([norm_gain, norm_bias, mlp_gain, mlp_bias])
    own_qkv = jnp.concatenate(
        [lax.dynamic_slice_in_dim(qkv_weight, s * head_cols, head_cols, 1), qkv_weight[:, width:]], axis=1
    )
    qkv_cols = own_qkv.shape[1]
    span = 16
    padded = jnp.pad(vectors, ((0, span - 4), (0, qkv_cols - shard)))
    qkv_ring = ring.gather(jnp.concatenate([own_qkv, padded], axis=0))
    hidden_all = seq_gather(hidden_in)
    qkv_full = qkv_ring[:, :shard].reshape(width, qkv_cols)
    vectors = qkv_ring[:, shard : shard + 4, :shard].transpose(1, 0, 2).reshape(4, width).astype(F32)
    gain_one, bias_one, gain_two, bias_two = vectors[0], vectors[1], vectors[2], vectors[3]

    part = shard // seq_count
    pairs = [
        (j * fsdp_count + q * (fsdp_count // seq_count) + t // seq_count, q * fsdp_count + t)
        for q in range(seq_count)
        for t in range(fsdp_count)
        for j in [t % seq_count]
    ]
    back_pairs = [(b, a) for a, b in pairs]
    own_proj = lax.ppermute(
        lax.dynamic_slice_in_dim(proj_weight, s * part, part, 0), ("seq", "fsdp"), pairs
    )

    rows_all = hidden_all.reshape(group, width).astype(F32)
    normed_all, _ = layer_norm(rows_all)
    attn_in = (normed_all * gain_one + bias_one).astype(BF)
    own_attn_in = attn_in[:tokens_here]
    key_values = dot_plain(own_attn_in, qkv_full[:, head_cols:]).astype(BF)
    kv_ring = ring.gather(key_values)
    kv_rel = seq_gather(kv_ring)
    kv_all = jnp.zeros((seq_count,) + kv_ring.shape, BF)
    for i in range(seq_count):
        kv_all = lax.dynamic_update_slice(kv_all, kv_rel[i][None], (s ^ i, 0, 0, 0))
    kv_all = kv_all.reshape(seq_count * fsdp_count, MB, count, 2 * HD)
    queries = dot_plain(attn_in, qkv_full[:, :head_cols]).astype(BF).reshape(seq_count, MB, count, head_cols)

    own_proj = tie(own_proj, kv_ring)
    proj_full = ring.gather(own_proj).reshape(head_cols, width)
    fc_own = lax.dynamic_slice_in_dim(
        fc_weight.reshape(shard, fsdp_count, seq_count, quarter), s, 1, 2
    ).reshape(shard, fsdp_count * quarter)
    fc_own = tie(fc_own, proj_full)
    fc_full = ring.gather(fc_own).reshape(width, fsdp_count * quarter)
    down_own = lax.dynamic_slice_in_dim(down_weight, s * quarter, quarter, 0)
    down_own = tie(down_own, fc_full)
    down_full = ring.gather(down_own).reshape(fsdp_count * quarter, width)
    cotangent_all = seq_gather(tie(out_cotangent, hidden_all)).reshape(group, width)

    heads_out, logs = attend(tables, first, queries, kv_all, blocks)
    heads_rows = heads_out.reshape(group, head_cols)

    def partial_sums(left, right):
        return [
            dot_plain(left[i * tokens_here : (i + 1) * tokens_here], right) for i in range(seq_count)
        ]

    hidden_own = hidden_in.reshape(tokens_here, width).astype(F32)
    cotangent = out_cotangent.reshape(tokens_here, width)
    resid = hidden_own + seq_scatter(partial_sums(heads_rows, proj_full))
    normed_two, inverse_two = layer_norm(resid)
    mlp_in_own = (normed_two * gain_two + bias_two).astype(BF)
    mlp_in = seq_gather(mlp_in_own).reshape(group, width)
    pre_act = dot_plain(mlp_in, fc_full)
    activ, gelu_pull = jax.vjp(gelu_tanh, pre_act)
    activ = activ.astype(BF)
    activ_grad = dot_cols(cotangent_all, down_full)
    pre_grad = gelu_pull(activ_grad)[0].astype(BF)
    fc_turned = fc_full
    mlp_in_grad = seq_scatter(
        [
            dot_cols(pre_grad[i * tokens_here : (i + 1) * tokens_here], fc_turned)
            for i in range(seq_count)
        ]
    )
    result = (resid + seq_scatter(partial_sums(activ, down_full))).astype(BF)

    mlp_gain_part = jnp.sum(mlp_in_grad * normed_two, axis=0)
    mlp_bias_part = jnp.sum(mlp_in_grad, axis=0)
    resid_grad = cotangent.astype(F32) + norm_back(mlp_in_grad * gain_two, normed_two, inverse_two)
    branch_own = resid_grad.astype(BF)
    branch = seq_gather(branch_own).reshape(group, width)
    heads_grad = dot_cols(branch, proj_full).astype(BF).reshape(seq_count, MB, count, head_cols)

    down_sum = dot_rows(activ, cotangent_all).reshape(fsdp_count, quarter, width)
    down_grad = ring.scatter(lambda t: lax.dynamic_index_in_dim(down_sum, t, 0, keepdims=False)).astype(BF)
    fc_sum = dot_rows(mlp_in, pre_grad).reshape(fsdp_count, shard, fsdp_count * quarter)
    fc_sum = tie(fc_sum, down_grad)
    fc_grad = ring.scatter(lambda t: lax.dynamic_index_in_dim(fc_sum, t, 0, keepdims=False)).astype(BF)
    proj_sum = dot_rows(heads_rows, branch).reshape(fsdp_count, part, width)
    proj_sum = tie(proj_sum, fc_grad)
    proj_grad = ring.scatter(lambda t: lax.dynamic_index_in_dim(proj_sum, t, 0, keepdims=False)).astype(BF)
    proj_grad = lax.ppermute(proj_grad, ("seq", "fsdp"), back_pairs)

    query_grads, kv_grads = attend_back(
        tables, first, queries, kv_all, heads_out, logs, heads_grad, blocks
    )
    query_rows = query_grads.reshape(group, head_cols)
    query_sum = dot_rows(attn_in, query_rows).reshape(fsdp_count, shard, head_cols)
    query_weight_grad = ring.scatter(
        lambda t: lax.dynamic_index_in_dim(query_sum, t, 0, keepdims=False)
    ).astype(BF)
    attn_in_grad = seq_scatter(
        [
            dot_cols(query_rows[i * tokens_here : (i + 1) * tokens_here], qkv_full[:, :head_cols])
            for i in range(seq_count)
        ]
    )
    kv_grads = kv_grads.reshape(seq_count, fsdp_count, tokens_here, 2 * HD)
    kv_seq = seq_scatter(
        [
            lax.dynamic_index_in_dim(kv_grads, s ^ i, 0, keepdims=False).astype(F32)
            for i in range(seq_count)
        ]
    )
    kv_own = ring.scatter(lambda t: lax.dynamic_index_in_dim(kv_seq, t, 0, keepdims=False)).astype(BF)
    attn_in_grad = attn_in_grad + dot_cols(kv_own, qkv_full[:, head_cols:])
    normed_one, inverse_one = layer_norm(hidden_own)
    norm_gain_part = jnp.sum(attn_in_grad * normed_one, axis=0)
    norm_bias_part = jnp.sum(attn_in_grad, axis=0)
    grad_input = (resid_grad + norm_back(attn_in_grad * gain_one, normed_one, inverse_one)).astype(BF)

    kv_sum = dot_rows(own_attn_in, kv_own).reshape(fsdp_count, shard, 2 * HD)
    vector_sum = jnp.stack([norm_gain_part, norm_bias_part, mlp_gain_part, mlp_bias_part])
    vector_sum = vector_sum.reshape(4, fsdp_count, shard).transpose(1, 0, 2)
    tail_cols = max(2 * HD, shard)
    kv_sum = jnp.pad(kv_sum, ((0, 0), (0, 0), (0, tail_cols - 2 * HD)))
    vector_sum = jnp.pad(vector_sum, ((0, 0), (0, span - 4), (0, tail_cols - shard)))
    tail_sum = jnp.concatenate([kv_sum, vector_sum], axis=1)
    tail = ring.scatter(lambda t: lax.dynamic_index_in_dim(tail_sum, t, 0, keepdims=False)).astype(BF)
    tail = tail.astype(F32) + core_swap(tail).astype(F32)
    tail = tail.astype(BF)
    tail = tail.astype(F32) + chip_swap(tail).astype(F32)
    kv_weight_grad = tail[:shard, : 2 * HD]
    vector_grads = tail[shard : shard + 4, :shard]

    def spread(piece, axis):
        pieces = seq_gather(piece)
        shape = piece.shape[:axis] + (seq_count,) + piece.shape[axis:]
        out = jnp.zeros(shape, F32)
        for i in range(seq_count):
            start = [0] * len(shape)
            start[axis] = s ^ i
            out = lax.dynamic_update_slice(out, jnp.expand_dims(pieces[i], axis).astype(F32), start)
        return out

    grad_down = spread(down_grad, 0).reshape(ff_shard, width)
    grad_fc = spread(fc_grad.reshape(shard, fsdp_count, quarter), 2).reshape(shard, ff)
    grad_proj = spread(proj_grad, 0).reshape(shard, width)
    grad_query = spread(query_weight_grad, 1).reshape(shard, width)
    grad_qkv = jnp.concatenate([grad_query, kv_weight_grad], axis=1)
    return (
        result.reshape(hidden_in.shape),
        grad_input.reshape(hidden_in.shape),
        vector_grads[0],
        vector_grads[1],
        grad_qkv,
        grad_proj,
        vector_grads[2],
        vector_grads[3],
        grad_fc,
        grad_down,
    )


def solution(mesh):
    rows = P(None, ("seq", "fsdp"), None)
    vector = P("fsdp")
    matrix = P("fsdp", None)
    in_specs = (rows, rows, P(), P(), vector, vector, matrix, matrix, vector, vector, matrix, matrix)
    out_specs = (rows, rows, vector, vector, matrix, matrix, vector, vector, matrix, matrix)
    return jax.shard_map(shards, mesh=mesh, in_specs=in_specs, out_specs=out_specs, check_vma=False)
```

time: 5300 us -> 1110 us (0.21)
  waiting for transfers between devices: 4280 us -> 346 us
  matrix products: 499 us -> 157 us
  local copies, waits for them, and re-layouts: 170 us -> 335 us
  blocking collectives: 157 us -> 0 us
  starting transfers between devices: 23.6 us -> 141 us
  other arithmetic: 131 us -> 72.7 us
    reduce_scatter x10 -> x0, waiting for transfers between devices: 2930 us -> none  [the longest x2 1090 us: shards(): lax.psum_scatter(contract_rows(mlp_in, pre_grad).astype(jnp.bfloat16), 'f...]
    all_gather x6 -> x0, waiting for transfers between devices: 1230 us -> none  [the longest x1 603 us: shards(): lax.all_gather(down_weight, 'fsdp', axis=0, tiled=True)]
    ppermute x0 -> x134, waiting for transfers between devices: none -> 346 us  [the longest x15 95.2 us: gather(): low = lax.ppermute(low, 'fsdp', self.up)]
    dot_general x168 -> x27, matrix products: 499 us -> 157 us  [the longest x11 69.9 us: dot_cols(): lax.dot_general(left, right, (((1,), (1,)), ((), ())), preferred_element_...]
    dynamic_update_slice x0 -> x53, local copies, waits for them, and re-layouts: none -> 214 us  [the longest x6 191 us: spread(): lax.dynamic_update_slice(out, jnp.expand_dims(pieces[i], axis).astype(F32...]
    ppermute x0 -> x134, starting transfers between devices: none -> 141 us  [the longest x24 45.8 us: scatter(): up = lax.ppermute(up, 'fsdp', self.up).astype(F32)]
    psum x1 -> x0, waiting for transfers between devices: 106 us -> none  [shards(): lax.psum(totals[2].astype(jnp.bfloat16), 'seq').astype(jnp.float32)]
    all_gather x4 -> x0, blocking collectives: 91.8 us -> none  [the longest x1 34.1 us: shards(): lax.all_gather(mlp_gain, 'fsdp', axis=0, tiled=True)]
  transfers between devices with their start and end apart: 23 -> 134, of which waited for: 17 -> 56; matrix products, arithmetic and copies ran while one was open for 10% -> 46% of each run, Pallas kernels for 0% -> 4%
where the time goes in v1:
time: 1110 us; the launch traced here: 1100 us
  waiting for transfers between devices  346 us (31%)
  local copies, waits for them, and re-layouts  335 us (30%)
  matrix products  157 us (14%)
  starting transfers between devices  141 us (13%)
  other arithmetic  72.7 us (7%)
  Pallas kernels  43.9 us (4%)
    dynamic_update_slice x6, local copies, waits for them, and re-layouts, spread(): lax.dynamic_update_slice(out, jnp.expand_dims(pieces[i], axis).astype(F32...  191 us
    ppermute x15, waiting for transfers between devices, gather(): low = lax.ppermute(low, 'fsdp', self.up)  95.2 us
    ppermute x24, waiting for transfers between devices, scatter(): down = lax.ppermute(down, 'fsdp', self.down).astype(F32)  74.2 us
    dot_general x11, matrix products, dot_cols(): lax.dot_general(left, right, (((1,), (1,)), ((), ())), preferred_element_...  69.9 us
    ppermute x15, waiting for transfers between devices, chip_swap(): return lax.ppermute(value, 'seq', [(s, s ^ 2) for s in range(4)])  66 us
    ppermute x24, waiting for transfers between devices, scatter(): up = lax.ppermute(up, 'fsdp', self.up).astype(F32)  65.9 us
    dot_general x11, matrix products, dot_plain(): lax.dot_general(left, right, (((1,), (0,)), ((), ())), preferred_element_...  51.2 us
    ppermute x24, starting transfers between devices, scatter(): up = lax.ppermute(up, 'fsdp', self.up).astype(F32)  45.8 us
  transfers between devices with their start and end apart: 134, of which 56 were waited for; matrix products, arithmetic and copies ran while one was open for 46% of the time, Pallas kernels for 4%

profile of v1, /device:TPU:0, one launch (start us, length us, event | category | flops | bytes accessed | tf_op | source)
XLA Modules:
  0.0 1099.5 jit_solution(5303821615530472766)
XLA Ops:
  129.1 17.9 %collective-permute-done.37 = bf16[256,2048]{0,1:T(8,128)(2,1)} collective-permute-done((bf16[256,2048]{0,1:T(8,128)(2,1)S(1)}, bf16[256,2048]{0,1:T(8,128)(2,1)}, u32[]{:S(2)}, u32[]{:S(2)}) %collective-permute-start.37) | collective-permute-done | bytes 1048608 | tf_op jit(solution)/shard_map/ppermute | solution.py:91
  149.3 18.7 %attend.1 = (bf16[4,2,128,512]{3,2,1,0:T(8,128)(2,1)S(1)}, f32[4,2,4,128]{3,2,1,0:T(4,128)S(1)}) custom-call(s32[160]{0:T(256)S(1)} %reshape.602.tables, bf16[4,2,128,512]{3,2,1,0:T(8,128)(2,1)S(1)} %bitcast.575, bf16[32,2,128,256]{3,2,1,0:T(8,128)(2,1)S(1)} %bitcast.571, s32[4,2,1,128]{3,2,1,0:T(1,128)S(1)} %add_subtract_fusion.first_ref), custom_call_target="tpu_custom_call" | custom-call | flops 4294967296 | bytes 16777216 | tf_op jit(solution)/shard_map/attend/pallas_call | solution.py:259
  214.4 12.4 %collective-permute-done.41 = bf16[256,2048]{0,1:T(8,128)(2,1)} collective-permute-done((bf16[256,2048]{0,1:T(8,128)(2,1)}, bf16[256,2048]{0,1:T(8,128)(2,1)}, u32[]{:S(2)}, u32[]{:S(2)}) %collective-permute-start.41) | collective-permute-done | bytes 1048608 | tf_op jit(solution)/shard_map/ppermute | solution.py:91
  272.1 13.9 %collective-permute-done.45 = bf16[256,2048]{1,0:T(8,128)(2,1)} collective-permute-done((bf16[256,2048]{1,0:T(8,128)(2,1)}, bf16[256,2048]{1,0:T(8,128)(2,1)}, u32[]{:S(2)}, u32[]{:S(2)}) %collective-permute-start.45) | collective-permute-done | bytes 1048608 | tf_op jit(solution)/shard_map/ppermute | solution.py:91
  294.7 16.7 %fusion.14 = (bf16[2048,1024]{0,1:T(8,128)(2,1)}, f32[1024,2048]{1,0:T(8,128)}) fusion(bf16[1024,2048]{1,0:T(8,128)(2,1)S(1)} %bitcast.585, bf16[2048,2048]{1,0:T(8,128)(2,1)} %bitcast.78), kind=kOutput, calls=%fused_computation.17 | convolution fusion | flops 8608808960 | bytes 25165824 | tf_op jit(solution)/shard_map/dot_general | solution.py:32
  317.9 15.3 %fusion.155 = f32[8,256,2048]{2,1,0:T(8,128)} fusion(bf16[8,256,1024]{2,1,0:T(8,128)(2,1)} %bitcast.618, bf16[1024,2048,1]{1,0,2:T(8,128)(2,1)} %bitcast.613), kind=kOutput, calls=%fused_computation.391 | convolution fusion | flops 8589934592 | bytes 25165824 | tf_op jit(solution)/shard_map/dot_general | solution.py:24
  363.5 15.2 %collective-permute-done.49 = bf16[256,2048]{1,0:T(8,128)(2,1)S(1)} collective-permute-done((bf16[256,2048]{1,0:T(8,128)(2,1)}, bf16[256,2048]{1,0:T(8,128)(2,1)S(1)}, u32[]{:S(2)}, u32[]{:S(2)}) %collective-permute-start.49) | collective-permute-done | bytes 1048608 | tf_op jit(solution)/shard_map/ppermute | solution.py:91
  381.2 20.0 %collective-permute-done.101 = bf16[256,2048]{1,0:T(8,128)(2,1)S(1)} collective-permute-done((bf16[256,2048]{1,0:T(8,128)(2,1)S(1)}, bf16[256,2048]{1,0:T(8,128)(2,1)S(1)}, u32[]{:S(2)}, u32[]{:S(2)}) %collective-permute-start.101) | collective-permute-done | bytes 1048608 | tf_op jit(solution)/shard_map/ppermute | solution.py:108
  412.6 21.5 %fusion.6 = (bf16[1024,2048]{1,0:T(8,128)(2,1)}, bf16[1024,2048]{1,0:T(8,128)(2,1)}) fusion(f32[1024,2048]{1,0:T(8,128)} %get-tuple-element.133, bf16[1024,2048]{1,0:T(8,128)(2,1)} %bitcast.614, bf16[2048,2048]{1,0:T(8,128)(2,1)S(1)} %bitcast.595), kind=kOutput, calls=%fused_computation.9 | convolution fusion | flops 8636071936 | bytes 29360128 | tf_op jit(solution)/shard_map/dot_general | solution.py:28
  450.8 12.3 %fusion.19 = f32[8,256,2048]{2,1,0:T(8,128)S(1)} fusion(bf16[8,256,1024]{2,1,0:T(8,128)(2,1)} %bitcast.615, bf16[1024,2048]{1,0:T(8,128)(2,1)} %get-tuple-element.60), kind=kOutput, calls=%fused_computation.29 | convolution fusion | flops 8589934592 | bytes 25165824 | tf_op jit(solution)/shard_map/dot_general | solution.py:24
  463.2 12.1 %convolution_convert_fusion.5 = bf16[256,2048]{1,0:T(8,128)(2,1)S(1)} fusion(bf16[2048,2048]{1,0:T(8,128)(2,1)} %bitcast.78, bf16[1024,2048]{1,0:T(8,128)(2,1)} %get-tuple-element.60), kind=kOutput, calls=%fused_computation.52 | convolution fusion | flops 2148007936 | bytes 10485760 | tf_op jit(solution)/shard_map/dot_general | solution.py:28
  565.1 16.0 %collective-permute-done.132 = bf16[256,2048]{1,0:T(8,128)(2,1)} collective-permute-done((bf16[256,2048]{1,0:T(8,128)(2,1)S(1)}, bf16[256,2048]{1,0:T(8,128)(2,1)}, u32[]{:S(2)}, u32[]{:S(2)}) %collective-permute-start.132) | collective-permute-done | bytes 1048608 | tf_op jit(solution)/shard_map/ppermute | solution.py:44
  590.4 25.2 %attend_back.1 = (bf16[4,2,128,512]{3,2,1,0:T(8,128)(2,1)}, bf16[32,2,128,256]{3,2,1,0:T(8,128)(2,1)}) custom-call(s32[160]{0:T(256)} %copy-done.5, bf16[4,2,128,512]{3,2,1,0:T(8,128)(2,1)} %bitcast.576, bf16[32,2,128,256]{3,2,1,0:T(8,128)(2,1)} %bitcast.572, s32[4,2,1,128]{3,2,1,0:T(1,128)} %copy-done.4, bf16[4,2,128,512]{3,2,1,0:T(8,128)(2,1)} %copy-done.3, ...), custom_call_target="tpu_custom_call" | custom-call | flops 10737418240 | bytes 33554432 | tf_op jit(solution)/shard_map/attend_back/pallas_call | solution.py:292
  684.1 13.7 %collective-permute-done.71 = bf16[128,256]{1,0:T(8,128)(2,1)S(1)} collective-permute-done((bf16[128,256]{1,0:T(8,128)(2,1)S(1)}, bf16[128,256]{1,0:T(8,128)(2,1)S(1)}, u32[]{:S(2)}, u32[]{:S(2)}) %collective-permute-start.71) | collective-permute-done | bytes 65568 | tf_op jit(solution)/shard_map/ppermute | solution.py:108
  708.0 18.9 %collective-permute-done.98 = bf16[256,512]{1,0:T(8,128)(2,1)S(1)} collective-permute-done((bf16[256,512]{1,0:T(8,128)(2,1)S(1)}, bf16[256,512]{1,0:T(8,128)(2,1)S(1)}, u32[]{:S(2)}, u32[]{:S(2)}) %collective-permute-start.98) | collective-permute-done | bytes 262176 | tf_op jit(solution)/shard_map/ppermute | solution.py:44
  734.4 19.5 %collective-permute-done.77 = bf16[256,256]{1,0:T(8,128)(2,1)S(1)} collective-permute-done((bf16[256,256]{1,0:T(8,128)(2,1)S(1)}, bf16[256,256]{1,0:T(8,128)(2,1)S(1)}, u32[]{:S(2)}, u32[]{:S(2)}) %collective-permute-start.77) | collective-permute-done | bytes 131104 | tf_op jit(solution)/shard_map/ppermute | solution.py:109
  757.9 11.1 %dynamic_update_slice.247 = f32[256,4,512]{2,1,0:T(4,128)} dynamic-update-slice(f32[256,4,512]{2,1,0:T(4,128)} %copy.68, f32[256,1,512]{2,1,0:T(1,128)} %copy.69, s32[]{:T(128)} %constant.274.clone.1, s32[]{:T(128)S(6)} %select_n.368, s32[]{:T(128)} %constant.274.clone.1) | dynamic-update-slice | bytes 1048580 | tf_op jit(solution)/shard_map/dynamic_update_slice | solution.py:531
  782.7 15.0 %collective-permute-done.79 = bf16[136,256]{1,0:T(8,128)(2,1)S(1)} collective-permute-done((bf16[136,256]{1,0:T(8,128)(2,1)S(1)}, bf16[136,256]{1,0:T(8,128)(2,1)S(1)}, u32[]{:S(2)}, u32[]{:S(2)}) %collective-permute-start.79) | collective-permute-done | bytes 69664 | tf_op jit(solution)/shard_map/ppermute | solution.py:108
  805.3 22.0 %collective-permute-done.84 = bf16[272,256]{1,0:T(8,128)(2,1)S(1)} collective-permute-done((bf16[272,256]{1,0:T(8,128)(2,1)S(1)}, bf16[272,256]{1,0:T(8,128)(2,1)S(1)}, u32[]{:S(2)}, u32[]{:S(2)}) %collective-permute-start.84) | collective-permute-done | bytes 139296 | tf_op jit(solution)/shard_map/ppermute | solution.py:109
  868.3 44.5 %dynamic_update_slice.252 = f32[256,8,4,256]{3,2,1,0:T(4,128)} dynamic-update-slice(f32[256,8,4,256]{3,2,1,0:T(4,128)} %broadcast_in_dim.238, f32[256,8,1,256]{3,2,1,0:T(1,128)} %reshape.651, s32[]{:T(128)} %constant.274.clone.1, s32[]{:T(128)} %constant.274.clone.1, s32[]{:T(128)S(6)} %select_n.365, s32[]{:T(128)} %constant.274.clone.1) | dynamic-update-slice | bytes 4194308 | tf_op jit(solution)/shard_map/dynamic_update_slice | solution.py:531
  938.9 44.2 %dynamic_update_slice.253 = f32[256,8,4,256]{3,2,1,0:T(4,128)} dynamic-update-slice(f32[256,8,4,256]{3,2,1,0:T(4,128)} %dynamic_update_slice.252, f32[256,8,1,256]{3,2,1,0:T(1,128)S(1)} %copy.74, s32[]{:T(128)} %constant.274.clone.1, s32[]{:T(128)} %constant.274.clone.1, s32[]{:T(128)S(6)} %select_n.366, s32[]{:T(128)} %constant.274.clone.1) | dynamic-update-slice | bytes 4194308 | tf_op jit(solution)/shard_map/dynamic_update_slice | solution.py:531
  983.0 44.3 %dynamic_update_slice.254 = f32[256,8,4,256]{3,2,1,0:T(4,128)} dynamic-update-slice(f32[256,8,4,256]{3,2,1,0:T(4,128)} %dynamic_update_slice.253, f32[256,8,1,256]{3,2,1,0:T(1,128)} %copy.75, s32[]{:T(128)} %constant.274.clone.1, s32[]{:T(128)} %constant.274.clone.1, s32[]{:T(128)S(6)} %select_n.367, s32[]{:T(128)} %constant.274.clone.1) | dynamic-update-slice | bytes 4194308 | tf_op jit(solution)/shard_map/dynamic_update_slice | solution.py:531
  1044.1 44.2 %dynamic_update_slice.255 = f32[256,8,4,256]{3,2,1,0:T(4,128)} dynamic-update-slice(f32[256,8,4,256]{3,2,1,0:T(4,128)} %dynamic_update_slice.254, f32[256,8,1,256]{3,2,1,0:T(1,128)S(1)} %copy.76, s32[]{:T(128)} %constant.274.clone.1, s32[]{:T(128)} %constant.274.clone.1, s32[]{:T(128)S(6)} %select_n.368, s32[]{:T(128)} %constant.274.clone.1) | dynamic-update-slice | bytes 4194308 | tf_op jit(solution)/shard_map/dynamic_update_slice | solution.py:531
  1088.3 10.8 reshape.624
  (610 shorter events, 590.9 us)
Async XLA Ops:
  3.7 63.1 %collective-permute-start = (bf16[2,128,2048]{2,1,0:T(8,128)(2,1)}, bf16[2,128,2048]{2,1,0:T(8,128)(2,1)S(1)}, u32[]{:S(2)}, u32[]{:S(2)}) collective-permute-start(bf16[2,128,2048]{2,1,0:T(8,128)(2,1)} %param.12), channel_id=1, source_target_pairs={{0,8},{8,0},{16,24},{24,16},{1,9},{9,1},{17,25},{25,17},{2,10},{10... | collective-permute-start | bytes 3145736 | tf_op jit(solution)/shard_map/ppermute | solution.py:40
  12.4 82.2 %collective-permute-start.22 = (bf16[64,2048]{1,0:T(8,128)(2,1)}, bf16[64,2048]{1,0:T(8,128)(2,1)S(1)}, u32[]{:S(2)}, u32[]{:S(2)}) collective-permute-start(bf16[64,2048]{1,0:T(8,128)(2,1)} %constant_dynamic-slice_fusion.2), channel_id=1, source_target_pairs={{0,0},{8,1},{16,2},{24,3},{1,4},{9,5},{17,6},{25,7},{2,8},{10,9},{... | collective-permute-start | bytes 786440 | tf_op jit(solution)/shard_map/ppermute | solution.py:408
  147.0 50.9 %collective-permute-start.39 = (bf16[256,2048]{0,1:T(8,128)(2,1)}, bf16[256,2048]{0,1:T(8,128)(2,1)}, u32[]{:S(2)}, u32[]{:S(2)}) collective-permute-start(bf16[256,2048]{0,1:T(8,128)(2,1)} %collective-permute-done.37), channel_id=1, source_target_pairs={{0,2},{2,4},{4,6},{6,7},{7,5},{5,3},{3,1},{1,0},{8,10},{10,12},{12... | collective-permute-start | bytes 3145736 | tf_op jit(solution)/shard_map/ppermute | solution.py:91
  148.8 54.9 %collective-permute-start.40 = (bf16[256,2048]{0,1:T(8,128)(2,1)}, bf16[256,2048]{0,1:T(8,128)(2,1)}, u32[]{:S(2)}, u32[]{:S(2)}) collective-permute-start(bf16[256,2048]{0,1:T(8,128)(2,1)} %collective-permute-done.38), channel_id=1, source_target_pairs={{2,0},{4,2},{6,4},{7,6},{5,7},{3,5},{1,3},{0,1},{10,8},{12,10},{14... | collective-permute-start | bytes 3145736 | tf_op jit(solution)/shard_map/ppermute | solution.py:92
  214.4 49.3 %collective-permute-start.56 = (bf16[2,128,2048]{2,1,0:T(8,128)(2,1)}, bf16[2,128,2048]{2,1,0:T(8,128)(2,1)}, u32[]{:S(2)}, u32[]{:S(2)}) collective-permute-start(bf16[2,128,2048]{2,1,0:T(8,128)(2,1)} %param.13), channel_id=1, source_target_pairs={{0,8},{8,0},{16,24},{24,16},{1,9},{9,1},{17,25},{25,17},{2,10},{10... | collective-permute-start | bytes 3145736 | tf_op jit(solution)/shard_map/ppermute | solution.py:40
  285.9 59.2 %collective-permute-start.47 = (bf16[256,2048]{1,0:T(8,128)(2,1)}, bf16[256,2048]{1,0:T(8,128)(2,1)}, u32[]{:S(2)}, u32[]{:S(2)}) collective-permute-start(bf16[256,2048]{1,0:T(8,128)(2,1)} %collective-permute-done.45), channel_id=1, source_target_pairs={{0,2},{2,4},{4,6},{6,7},{7,5},{5,3},{3,1},{1,0},{8,10},{10,12},{12... | collective-permute-start | bytes 3145736 | tf_op jit(solution)/shard_map/ppermute | solution.py:91
  288.4 61.1 %collective-permute-start.48 = (bf16[256,2048]{1,0:T(8,128)(2,1)}, bf16[256,2048]{1,0:T(8,128)(2,1)}, u32[]{:S(2)}, u32[]{:S(2)}) collective-permute-start(bf16[256,2048]{1,0:T(8,128)(2,1)} %collective-permute-done.46), channel_id=1, source_target_pairs={{2,0},{4,2},{6,4},{7,6},{5,7},{3,5},{1,3},{0,1},{10,8},{12,10},{14... | collective-permute-start | bytes 3145736 | tf_op jit(solution)/shard_map/ppermute | solution.py:92
  363.3 112.0 %collective-permute-start.105 = (bf16[256,2048]{1,0:T(8,128)(2,1)}, bf16[256,2048]{1,0:T(8,128)(2,1)}, u32[]{:S(2)}, u32[]{:S(2)}) collective-permute-start(bf16[256,2048]{1,0:T(8,128)(2,1)} %pad_maximum_fusion.6), channel_id=1, source_target_pairs={{2,0},{4,2},{6,4},{7,6},{5,7},{3,5},{1,3},{0,1},{10,8},{12,10},{14... | collective-permute-start | bytes 3145736 | tf_op jit(solution)/shard_map/ppermute | solution.py:109
  403.2 72.7 %collective-permute-start.102 = (bf16[256,2048]{1,0:T(8,128)(2,1)S(1)}, bf16[256,2048]{1,0:T(8,128)(2,1)S(1)}, u32[]{:S(2)}, u32[]{:S(2)}) collective-permute-start(bf16[256,2048]{1,0:T(8,128)(2,1)S(1)} %fusion.40), channel_id=1, source_target_pairs={{0,2},{2,4},{4,6},{6,7},{7,5},{5,3},{3,1},{1,0},{8,10},{10,12},{12... | collective-permute-start | bytes 3145736 | tf_op jit(solution)/shard_map/ppermute | solution.py:108
  443.2 99.7 %collective-permute-start.53 = (bf16[256,2048]{1,0:T(8,128)(2,1)}, bf16[256,2048]{1,0:T(8,128)(2,1)}, u32[]{:S(2)}, u32[]{:S(2)}) collective-permute-start(bf16[256,2048]{1,0:T(8,128)(2,1)} %convolution_convert_fusion.7), channel_id=1, source_target_pairs={{0,8},{8,0},{16,24},{24,16},{1,9},{9,1},{17,25},{25,17},{2,10},{10... | collective-permute-start | bytes 3145736 | tf_op jit(solution)/shard_map/ppermute | solution.py:40
  479.1 49.8 %collective-permute-start.103 = (bf16[256,2048]{1,0:T(8,128)(2,1)S(1)}, bf16[256,2048]{1,0:T(8,128)(2,1)}, u32[]{:S(2)}, u32[]{:S(2)}) collective-permute-start(bf16[256,2048]{1,0:T(8,128)(2,1)S(1)} %get-tuple-element.54), channel_id=1, source_target_pairs={{0,2},{2,4},{4,6},{6,7},{7,5},{5,3},{3,1},{1,0},{8,10},{10,12},{12... | collective-permute-start | bytes 3145736 | tf_op jit(solution)/shard_map/ppermute | solution.py:108
  561.6 83.4 %collective-permute-start.109 = (bf16[256,2048]{1,0:T(8,128)(2,1)}, bf16[256,2048]{1,0:T(8,128)(2,1)}, u32[]{:S(2)}, u32[]{:S(2)}) collective-permute-start(bf16[256,2048]{1,0:T(8,128)(2,1)} %pad_maximum_fusion.7), channel_id=1, source_target_pairs={{0,2},{2,4},{4,6},{6,7},{7,5},{5,3},{3,1},{1,0},{8,10},{10,12},{12... | collective-permute-start | bytes 3145736 | tf_op jit(solution)/shard_map/ppermute | solution.py:108
  564.6 135.0 %collective-permute-start.113 = (bf16[256,2048]{1,0:T(8,128)(2,1)}, bf16[256,2048]{1,0:T(8,128)(2,1)}, u32[]{:S(2)}, u32[]{:S(2)}) collective-permute-start(bf16[256,2048]{1,0:T(8,128)(2,1)} %pad_maximum_fusion.8), channel_id=1, source_target_pairs={{2,0},{4,2},{6,4},{7,6},{5,7},{3,5},{1,3},{0,1},{10,8},{12,10},{14... | collective-permute-start | bytes 3145736 | tf_op jit(solution)/shard_map/ppermute | solution.py:109
  581.1 75.2 %collective-permute-start.133 = (bf16[256,2048]{1,0:T(8,128)(2,1)}, bf16[256,2048]{1,0:T(8,128)(2,1)}, u32[]{:S(2)}, u32[]{:S(2)}) collective-permute-start(bf16[256,2048]{1,0:T(8,128)(2,1)} %collective-permute-done.132), channel_id=1, source_target_pairs={{0,8},{8,0},{16,24},{24,16},{1,9},{9,1},{17,25},{25,17},{2,10},{10... | collective-permute-start | bytes 3145736 | tf_op jit(solution)/shard_map/ppermute | solution.py:40
  670.8 105.4 %collective-permute-start.65 = (bf16[256,2048]{1,0:T(8,128)(2,1)}, bf16[256,2048]{1,0:T(8,128)(2,1)}, u32[]{:S(2)}, u32[]{:S(2)}) collective-permute-start(bf16[256,2048]{1,0:T(8,128)(2,1)} %convolution_convert_fusion.1), channel_id=1, source_target_pairs={{0,8},{8,0},{16,24},{24,16},{1,9},{9,1},{17,25},{25,17},{2,10},{10... | collective-permute-start | bytes 3145736 | tf_op jit(solution)/shard_map/ppermute | solution.py:40
  697.8 78.5 %collective-permute-start.67 = (bf16[256,2048]{1,0:T(8,128)(2,1)}, bf16[256,2048]{1,0:T(8,128)(2,1)}, u32[]{:S(2)}, u32[]{:S(2)}) collective-permute-start(bf16[256,2048]{1,0:T(8,128)(2,1)} %add_convert_fusion.1), channel_id=1, source_target_pairs={{0,16},{8,24},{16,0},{24,8},{1,17},{9,25},{17,1},{25,9},{2,18},{10... | collective-permute-start | bytes 3145736 | tf_op jit(solution)/shard_map/ppermute | solution.py:44
  726.9 71.9 %collective-permute-start.114 = (bf16[256,2048]{1,0:T(8,128)(2,1)}, bf16[256,2048]{1,0:T(8,128)(2,1)}, u32[]{:S(2)}, u32[]{:S(2)}) collective-permute-start(bf16[256,2048]{1,0:T(8,128)(2,1)} %get-tuple-element.49), channel_id=1, source_target_pairs={{2,0},{4,2},{6,4},{7,6},{5,7},{3,5},{1,3},{0,1},{10,8},{12,10},{14... | collective-permute-start | bytes 3145736 | tf_op jit(solution)/shard_map/ppermute | solution.py:109
  773.0 60.0 %collective-permute-start.111 = (bf16[256,2048]{1,0:T(8,128)(2,1)S(1)}, bf16[256,2048]{1,0:T(8,128)(2,1)S(1)}, u32[]{:S(2)}, u32[]{:S(2)}) collective-permute-start(bf16[256,2048]{1,0:T(8,128)(2,1)S(1)} %copy-done.35), channel_id=1, source_target_pairs={{0,2},{2,4},{4,6},{6,7},{7,5},{5,3},{3,1},{1,0},{8,10},{10,12},{12... | collective-permute-start | bytes 3145736 | tf_op jit(solution)/shard_map/ppermute | solution.py:108
  845.9 67.8 %collective-permute-start.121 = (bf16[64,2048]{1,0:T(8,128)(2,1)S(1)}, bf16[64,2048]{1,0:T(8,128)(2,1)}, u32[]{:S(2)}, u32[]{:S(2)}) collective-permute-start(bf16[64,2048]{1,0:T(8,128)(2,1)S(1)} %pad_maximum_fusion.13), channel_id=1, source_target_pairs={{2,0},{4,2},{6,4},{7,6},{5,7},{3,5},{1,3},{0,1},{10,8},{12,10},{14... | collective-permute-start | bytes 786440 | tf_op jit(solution)/shard_map/ppermute | solution.py:109
  846.7 66.1 %collective-permute-start.88 = (bf16[272,256]{1,0:T(8,128)(2,1)S(1)}, bf16[272,256]{1,0:T(8,128)(2,1)}, u32[]{:S(2)}, u32[]{:S(2)}) collective-permute-start(bf16[272,256]{1,0:T(8,128)(2,1)S(1)} %add_convert_fusion.3), channel_id=1, source_target_pairs={{0,16},{8,24},{16,0},{24,8},{1,17},{9,25},{17,1},{25,9},{2,18},{10... | collective-permute-start | bytes 417800 | tf_op jit(solution)/shard_map/ppermute | solution.py:44
  852.5 61.2 %collective-permute-start.118 = (bf16[64,2048]{1,0:T(8,128)(2,1)}, bf16[64,2048]{1,0:T(8,128)(2,1)}, u32[]{:S(2)}, u32[]{:S(2)}) collective-permute-start(bf16[64,2048]{1,0:T(8,128)(2,1)} %fusion.84), channel_id=1, source_target_pairs={{0,2},{2,4},{4,6},{6,7},{7,5},{5,3},{3,1},{1,0},{8,10},{10,12},{12... | collective-permute-start | bytes 786440 | tf_op jit(solution)/shard_map/ppermute | solution.py:108
  861.0 64.3 %collective-permute-start.128 = (bf16[256,8,256]{2,1,0:T(8,128)(2,1)}, bf16[256,8,256]{2,1,0:T(8,128)(2,1)}, u32[]{:S(2)}, u32[]{:S(2)}) collective-permute-start(bf16[256,8,256]{2,1,0:T(8,128)(2,1)} %bitcast.247), channel_id=1, source_target_pairs={{0,8},{8,0},{16,24},{24,16},{1,9},{9,1},{17,25},{25,17},{2,10},{10... | collective-permute-start | bytes 3145736 | tf_op jit(solution)/shard_map/ppermute | solution.py:40
  861.0 74.2 %collective-permute-start.129 = (bf16[256,8,256]{2,1,0:T(8,128)(2,1)}, bf16[256,8,256]{2,1,0:T(8,128)(2,1)S(1)}, u32[]{:S(2)}, u32[]{:S(2)}) collective-permute-start(bf16[256,8,256]{2,1,0:T(8,128)(2,1)} %bitcast.247), channel_id=1, source_target_pairs={{0,16},{8,24},{16,0},{24,8},{1,17},{9,25},{17,1},{25,9},{2,18},{10... | collective-permute-start | bytes 3145736 | tf_op jit(solution)/shard_map/ppermute | solution.py:44
  933.6 95.9 %collective-permute-start.124 = (bf16[64,2048]{1,0:T(8,128)(2,1)S(1)}, bf16[64,2048]{1,0:T(8,128)(2,1)}, u32[]{:S(2)}, u32[]{:S(2)}) collective-permute-start(bf16[64,2048]{1,0:T(8,128)(2,1)S(1)} %fusion.87), channel_id=1, source_target_pairs={{0,0},{1,8},{2,16},{3,24},{4,1},{5,9},{6,17},{7,25},{8,2},{9,10},{... | collective-permute-start | bytes 786440 | tf_op jit(solution)/shard_map/ppermute | solution.py:480
  (162 other events, 3169.9 us)

commit v2 on v1

--- a/solution.py
+++ b/solution.py
@@ -48,7 +48,7 @@
     across = chip_swap(value)
     pair = core_swap(value)
     pair_across = core_swap(across)
-    return jnp.stack([value, pair, across, pair_across])
+    return [value, pair, across, pair_across]
 
 
 def seq_scatter(parts):
@@ -78,47 +78,76 @@
         at = lax.rem(self.at + (step + count), count)
         return jnp.where(at < half, 2 * at, 2 * (count - 1 - at) + 1)
 
-    def gather(self, value):
+    def gather(self, value, out):
         count = self.count
-        rows = value.shape[0]
-        out = jnp.zeros((count,) + value.shape, value.dtype)
-        put = lambda out, piece, owner, row: lax.dynamic_update_slice(
-            out, piece[None], (owner, row) + (0,) * (value.ndim - 1)
-        )
-        out = put(out, value, self.place, 0)
+        half = value.shape[0] // 2
+
+        def put(piece, owner, row):
+            return lax.dynamic_update_slice(out, piece[None], (owner, row) + (0,) * (value.ndim - 1))
+
         low = high = value
-        for step in range(1, count // 2):
+        for step in range(1, count // 2 + 1):
+            last = step == count // 2
+            if last:
+                low, high = low[:half], high[half:]
             low = lax.ppermute(low, "fsdp", self.up)
             high = lax.ppermute(high, "fsdp", self.down)
-            out = put(out, low, self.owner(-step), 0)
-            out = put(out, high, self.owner(step), 0)
-        half = rows // 2
-        low = lax.ppermute(low[:half], "fsdp", self.up)
-        high = lax.ppermute(high[half:], "fsdp", self.down)
-        out = put(out, low, self.owner(-(count // 2)), 0)
-        return put(out, high, self.owner(count // 2), half)
+            low, high = yield low, high
+            out = put(low, self.owner(-step), 0)
+            out = put(high, self.owner(step), half if last else 0)
+        return out
+
+    def steps(self):
+        half = self.count // 2
+        return [half] + [sign * n for n in range(half - 1, 0, -1) for sign in (1, -1)] + [0]
+
+    def order(self):
+        return jnp.stack([self.owner(n) for n in self.steps()]).astype(jnp.int32)
 
     def scatter(self, chunk):
         count = self.count
-        middle = chunk(self.owner(count // 2))
+        middle = chunk(count // 2)
         half = middle.shape[0] // 2
         up = middle[:half].astype(BF)
         down = middle[half:].astype(BF)
         for step in range(count // 2 - 1, -1, -1):
-            up = lax.ppermute(up, "fsdp", self.up).astype(F32)
-            down = lax.ppermute(down, "fsdp", self.down).astype(F32)
+            up = lax.ppermute(up, "fsdp", self.up)
+            down = lax.ppermute(down, "fsdp", self.down)
+            up, down = yield up, down
+            up, down = up.astype(F32), down.astype(F32)
             if step == count // 2 - 1:
-                mine = chunk(self.owner(step))
+                mine = chunk(step)
                 up = jnp.concatenate([mine[:half] + up, mine[half:]], axis=0)
-                mine = chunk(self.owner(-step))
+                mine = chunk(-step)
                 down = jnp.concatenate([mine[:half], mine[half:] + down], axis=0)
             elif step:
-                up = chunk(self.owner(step)) + up
-                down = chunk(self.owner(-step)) + down
+                up = chunk(step) + up
+                down = chunk(-step) + down
             else:
-                return chunk(self.place) + up + down
+                return chunk(0) + up + down
             up = up.astype(BF)
             down = down.astype(BF)
+
+
+class Flow:
+    def __init__(self, ring, steps):
+        self.ring, self.steps, self.result = ring, steps, None
+        self.pending = next(steps)
+
+    def advance(self, values=()):
+        for _ in range(max(1, self.ring.count // 8)):
+            if self.result is None:
+                self.pending, values = lax.optimization_barrier((self.pending, values))
+                try:
+                    self.pending = self.steps.send(self.pending)
+                except StopIteration as end:
+                    self.result = end.value
+        return values
+
+    def finish(self):
+        while self.result is None:
+            self.advance()
+        return self.result
 
 
 def attend_kernel(tables, q_ref, kv_ref, first_ref, out_ref, log_ref, stack, high, total, result, *, heads, blocks):
@@ -313,6 +342,423 @@
         cost_estimate=pl.CostEstimate(flops=10 * rows * HD * chunks * count * pieces, bytes_accessed=32 << 20, transcendentals=rows * chunks * count * pieces),
         name="attend_back",
     )(tables, queries, key_values, first, out, logs, grads)
+
+
+def neighbours(count):
+    s, f = lax.axis_index("seq"), lax.axis_index("fsdp")
+    half = count // 2
+    at = jnp.where(lax.rem(f, 2) == 0, f // 2, count - 1 - f // 2)
+
+    def owner(step):
+        place = lax.rem(at + (step + count), count)
+        return jnp.where(place < half, 2 * place, 2 * (count - 1 - place) + 1)
+
+    chip = lax.rem(s + 2, 4)
+    core = s + 1 - 2 * lax.rem(s, 2)
+    return s, f, owner, (s, owner(1)), (s, owner(-1)), (chip, f), (core, f)
+
+
+def greet(*devices):
+    barrier = pltpu.get_barrier_semaphore()
+    for device in devices:
+        pl.semaphore_signal(barrier, inc=1, device_id=device, device_id_type=pl.DeviceIdType.MESH)
+    pl.semaphore_wait(barrier, len(devices))
+
+
+def send(source, target, sems, index, device):
+    copy = pltpu.make_async_remote_copy(
+        src_ref=source,
+        dst_ref=target,
+        send_sem=sems.at[(0,) + index],
+        recv_sem=sems.at[(1,) + index],
+        device_id=device,
+        device_id_type=pl.DeviceIdType.MESH,
+    )
+    copy.start()
+    return copy
+
+
+class KernelRing:
+    def __init__(self, count, own, slots, sems, owner, up, down):
+        self.count, self.own, self.slots, self.sems = count, own, slots, sems
+        self.owner, self.up, self.down = owner, up, down
+        self.copies = {}
+
+    def start(self, step):
+        half = self.slots.shape[1] // 2
+        for way, device in enumerate((self.up, self.down)):
+            slot = self.slots.at[self.owner((1 - step) if way == 0 else (step - 1))]
+            source = self.own if step == 1 else slot
+            if step == self.count // 2:
+                rows = pl.ds(way * half, half)
+                source, slot = source.at[rows], slot.at[rows]
+            self.copies[way, step] = send(source, slot, self.sems, (way, step - 1), device)
+
+    def arrived(self, step):
+        self.copies[0, step].wait_recv()
+        self.copies[1, step].wait_recv()
+
+    def finish(self):
+        for copy in self.copies.values():
+            copy.wait_send()
+
+
+def opening_kernel(
+    hidden,
+    kv_own,
+    q_own,
+    proj_own,
+    hidden_out,
+    kvw_out,
+    qw_out,
+    proj_out,
+    kv_out,
+    weights,
+    mine,
+    hid_chip,
+    hid_core,
+    kvw_sems,
+    q_sems,
+    proj_sems,
+    kv_sems,
+    kv_chip,
+    kv_core,
+    kv_far,
+    local,
+    *,
+    count,
+    shard,
+):
+    s, f, owner, up, down, chip, core = neighbours(count)
+    greet(up, down, chip, core)
+    steps = count // 2
+    rings = [
+        KernelRing(count, own, slots, sems, owner, up, down)
+        for own, slots, sems in ((kv_own, kvw_out, kvw_sems), (q_own, qw_out, q_sems), (proj_own, proj_out, proj_sems))
+    ]
+    kvw, qw, proj = rings
+    kvw.start(1)
+    rows = hidden.shape[0] // 2
+    halves = [pl.ds(i * rows, rows) for i in range(2)]
+    across = [send(hidden.at[half], hidden_out.at[2, half], hid_chip, (i,), chip) for i, half in enumerate(halves)]
+    pair = [send(hidden, hidden_out.at[1], hid_core, (2,), core)]
+    stays = [
+        pltpu.make_async_copy(source, target, local.at[i])
+        for i, (source, target) in enumerate(
+            (
+                (hidden, hidden_out.at[0]),
+                (kv_own, kvw_out.at[f]),
+                (q_own, qw_out.at[f]),
+                (proj_own, proj_out.at[f]),
+            )
+        )
+    ]
+    for copy in stays:
+        copy.start()
+    values = hidden[...].astype(F32)
+    mean = jnp.mean(values, axis=-1, keepdims=True)
+    center = values - mean
+    inverse = lax.rsqrt(jnp.mean(center * center, axis=-1, keepdims=True) + EPS)
+    for step in range(2, steps + 1):
+        kvw.arrived(step - 1)
+        kvw.start(step)
+    qw.start(1)
+    kvw.arrived(steps)
+    stays[1].wait()
+    load = pltpu.make_async_copy(kvw_out, weights, local.at[4])
+    load.start()
+    load.wait()
+    total = jnp.zeros((hidden.shape[0], kvw_out.shape[2]), F32)
+    for t in range(count):
+        cols = slice(t * shard, (t + 1) * shard)
+        normed = (hidden[:, cols].astype(F32) - mean) * inverse
+        gain = weights[t, shard : shard + 1, :shard].astype(F32)
+        bias = weights[t, shard + 1 : shard + 2, :shard].astype(F32)
+        total += dot_plain((normed * gain + bias).astype(BF), weights[t, :shard, :])
+    mine[...] = total.astype(BF)
+
+    spread = KernelRing(count, mine, kv_out.at[s], kv_sems, owner, up, down)
+    spread.start(1)
+    keep = pltpu.make_async_copy(mine, kv_out.at[s, f], local.at[5])
+    keep.start()
+    kv_across, kv_pair = [], []
+
+    def pass_on(source, place):
+        index = (len(kv_across),)
+        kv_across.append((place, send(source, kv_out.at[s, place], kv_chip, index, chip)))
+        kv_pair.append(send(source, kv_out.at[s, place], kv_core, index, core))
+
+    pass_on(mine, f)
+    for i, half in enumerate(halves):
+        across[i].wait_recv()
+        pair.append(send(hidden_out.at[2, half], hidden_out.at[2 + 1, half], hid_core, (i,), core))
+    for step in range(1, steps + 1):
+        spread.arrived(step)
+        qw.arrived(step)
+        if step < steps:
+            spread.start(step + 1)
+            qw.start(step + 1)
+            for place in (owner(-step), owner(step)):
+                pass_on(kv_out.at[s, place], place)
+        else:
+            pass_on(kv_out.at[s, owner(steps)], owner(steps))
+        if step == 1:
+            proj.start(1)
+        else:
+            proj.arrived(step - 1)
+            proj.start(step)
+    other = lax.rem(s + 2, 4)
+    far = []
+    for i, (place, copy) in enumerate(kv_across):
+        copy.wait_recv()
+        slot = kv_out.at[other, place]
+        far.append(send(slot, slot, kv_far, (i,), core))
+    proj.arrived(steps)
+    for ring in rings + [spread]:
+        ring.finish()
+    for copy in [keep, stays[0], stays[2], stays[3]]:
+        copy.wait()
+    for copy in across + [copy for _, copy in kv_across]:
+        copy.wait_send()
+    for copy in pair + kv_pair + far:
+        copy.wait()
+
+
+def opening(hidden, kv_own, q_own, proj_own, fsdp_count, shard):
+    count, width = hidden.shape
+    dma = pltpu.SemaphoreType.DMA
+    ring = dma((2, 2, fsdp_count // 2))
+    anywhere = pl.BlockSpec(memory_space=pl.ANY)
+    inside = pl.BlockSpec(memory_space=pltpu.VMEM)
+    return pl.pallas_call(
+        functools.partial(opening_kernel, count=fsdp_count, shard=shard),
+        out_shape=(
+            jax.ShapeDtypeStruct((4,) + hidden.shape, BF),
+            jax.ShapeDtypeStruct((fsdp_count,) + kv_own.shape, BF),
+            jax.ShapeDtypeStruct((fsdp_count,) + q_own.shape, BF),
+            jax.ShapeDtypeStruct((fsdp_count,) + proj_own.shape, BF),
+            jax.ShapeDtypeStruct((4, fsdp_count, count, 2 * HD), BF),
+        ),
+        in_specs=[inside, anywhere, anywhere, anywhere],
+        out_specs=(anywhere,) * 5,
+        scratch_shapes=[
+            pltpu.VMEM((fsdp_count,) + kv_own.shape, BF),
+            pltpu.VMEM((count, 2 * HD), BF),
+            dma((2, 2)),
+            dma((2, 3)),
+            ring,
+            ring,
+            ring,
+            ring,
+            dma((2, fsdp_count)),
+            dma((2, fsdp_count)),
+            dma((2, fsdp_count)),
+            dma((6,)),
+        ],
+        compiler_params=pltpu.CompilerParams(
+            collective_id=1, has_side_effects=True, vmem_limit_bytes=40 << 20
+        ),
+        name="opening",
+    )(hidden, kv_own, q_own, proj_own)
+
+
+def pack_kernel(place, fc_ref, down_ref, own_ref, all_ref):
+    rows = fc_ref.shape[0]
+    own_ref[:rows] = fc_ref[...]
+    own_ref[rows:] = down_ref[...]
+    all_ref[0] = own_ref[...]
+
+
+def pack(place, fc_weight, down_weight, parts, quarter):
+    rows, width = fc_weight.shape[0], down_weight.shape[1]
+    if quarter % 128:
+        fc_own = lax.dynamic_slice_in_dim(fc_weight.reshape(rows, parts, 4, quarter), place[0], 1, 2)
+        down_own = lax.dynamic_slice_in_dim(down_weight, place[0] * quarter, quarter, 0)
+        own = jnp.concatenate([fc_own.reshape(rows, parts * quarter), down_own], axis=0)
+        return own, lax.dynamic_update_slice(jnp.zeros((parts,) + own.shape, BF), own[None], (place[1], 0, 0))
+    return pl.pallas_call(
+        pack_kernel,
+        out_shape=(
+            jax.ShapeDtypeStruct((rows + quarter, width), BF),
+            jax.ShapeDtypeStruct((parts, rows + quarter, width), BF),
+        ),
+        grid_spec=pltpu.PrefetchScalarGridSpec(
+            num_scalar_prefetch=1,
+            grid=(parts,),
+            in_specs=[
+                pl.BlockSpec((rows, quarter), lambda g, p: (0, g * 4 + p[0])),
+                pl.BlockSpec((quarter, quarter), lambda g, p: (p[0], g)),
+            ],
+            out_specs=(
+                pl.BlockSpec((rows + quarter, quarter), lambda g, p: (0, g)),
+                pl.BlockSpec((1, rows + quarter, quarter), lambda g, p: (p[1], 0, g)),
+            ),
+        ),
+        compiler_params=pltpu.CompilerParams(vmem_limit_bytes=30 << 20),
+        name="pack",
+    )(place, fc_weight, down_weight)
+
+
+GELU_A = math.sqrt(2 / math.pi)
+GELU_B = 0.044715
+
+
+def middle_kernel(rows_ref, cot_ref, fc_ref, down_ref, activ_ref, pre_ref, grad_ref, total, *, step):
+    tile = pl.program_id(0)
+    fc = fc_ref[...].reshape(-1, fc_ref.shape[2])
+    down = down_ref[...].reshape(-1, down_ref.shape[2])
+
+    @pl.when(tile == 0)
+    def _():
+        total[...] = jnp.zeros_like(total)
+
+    for at in range(0, rows_ref.shape[0], step):
+        part = slice(at, at + step)
+        value = dot_plain(rows_ref[part], fc)
+        pull = dot_cols(cot_ref[part], down)
+        square = value * value
+        bend = jnp.tanh(GELU_A * value * (1.0 + GELU_B * square))
+        half = 0.5 * (1.0 + bend)
+        activ_ref[part] = (value * half).astype(BF)
+        slope = half + 0.5 * value * (1.0 - bend * bend) * (GELU_A * (1.0 + 3.0 * GELU_B * square))
+        grad = (pull * slope).astype(BF)
+        pre_ref[part] = grad
+        total[part] += dot_cols(grad, fc)
+
+    @pl.when(tile == pl.num_programs(0) - 1)
+    def _():
+        grad_ref[...] = total[...].astype(BF)
+
+
+def middle(rows, cot, weights, shard, tile):
+    count, width = rows.shape
+    parts, quarter = weights.shape[0], weights.shape[1] - shard
+    hidden = parts * quarter
+    per = tile // quarter
+    whole = pl.BlockSpec((count, width), lambda n: (0, 0), pipeline_mode=pl.Buffered(1))
+    cols = pl.BlockSpec((count, tile), lambda n: (0, n))
+    return pl.pallas_call(
+        functools.partial(middle_kernel, step=256),
+        out_shape=(
+            jax.ShapeDtypeStruct((count, hidden), BF),
+            jax.ShapeDtypeStruct((count, hidden), BF),
+            jax.ShapeDtypeStruct((count, width), BF),
+        ),
+        grid=(hidden // tile,),
+        in_specs=[
+            whole,
+            whole,
+            pl.BlockSpec((parts, shard, tile), lambda n: (0, 0, n)),
+            pl.BlockSpec((per, quarter, width), lambda n: (n, 1, 0)),
+        ],
+        out_specs=(cols, cols, pl.BlockSpec((count, width), lambda n: (0, 0))),
+        scratch_shapes=[pltpu.VMEM((count, width), F32)],
+        compiler_params=pltpu.CompilerParams(vmem_limit_bytes=60 << 20),
+        name="middle",
+    )(rows, cot, weights, weights)
+
+
+def turned_kernel(order, left_ref, right_ref, left_two_ref, right_two_ref, out_ref):
+    rows = left_ref.shape[1]
+    out_ref[0, :rows] = dot_rows(left_ref[...], right_ref[...]).astype(BF)
+    out_ref[0, rows:] = dot_rows(left_two_ref[...], right_two_ref[...]).astype(BF)
+
+
+def turned(order, left, right, left_two, right_two, shard):
+    count, width = right.shape
+    chunks = order.shape[0]
+    if shard % 128:
+        one = dot_rows(left, right).astype(BF).reshape(-1, shard, width)
+        two = dot_rows(left_two, right_two).astype(BF).reshape(-1, shard, width)
+        both = jnp.concatenate([one, two], axis=1)
+        return jnp.stack([lax.dynamic_index_in_dim(both, order[i], 0, False) for i in range(chunks)])
+    whole = pl.BlockSpec((count, width), lambda n, o: (0, 0), pipeline_mode=pl.Buffered(1))
+    cols = pl.BlockSpec((count, shard), lambda n, o: (0, o[n]))
+    return pl.pallas_call(
+        turned_kernel,
+        out_shape=jax.ShapeDtypeStruct((chunks, 2 * shard, width), BF),
+        grid_spec=pltpu.PrefetchScalarGridSpec(
+            num_scalar_prefetch=1,
+            grid=(chunks,),
+            in_specs=[cols, whole, cols, whole],
+            out_specs=pl.BlockSpec((1, 2 * shard, width), lambda n, o: (n, 0, 0)),
+        ),
+        compiler_params=pltpu.CompilerParams(vmem_limit_bytes=60 << 20),
+        name="turned",
+    )(order, left, right, left_two, right_two)
+
+
+def lower_kernel(rows_ref, down_ref, out_ref):
+    down = down_ref[...].reshape(-1, down_ref.shape[2])
+    out_ref[...] = dot_plain(rows_ref[...], down).astype(BF)
+
+
+def lower(rows, weights, shard, tile):
+    count = rows.shape[0]
+    parts, quarter, width = weights.shape[0], weights.shape[1] - shard, weights.shape[2]
+    return pl.pallas_call(
+        lower_kernel,
+        out_shape=jax.ShapeDtypeStruct((count, width), BF),
+        grid=(width // tile,),
+        in_specs=[
+            pl.BlockSpec(rows.shape, lambda n: (0, 0), pipeline_mode=pl.Buffered(1)),
+            pl.BlockSpec((parts, quarter, tile), lambda n: (0, 1, n)),
+        ],
+        out_specs=pl.BlockSpec((count, tile), lambda n: (0, n)),
+        compiler_params=pltpu.CompilerParams(vmem_limit_bytes=60 << 20),
+        name="lower",
+    )(rows, weights)
+
+
+def rows_kernel(place, *refs):
+    *ins, out = refs
+    rows = ins[0].shape[0]
+    for i, ref in enumerate(ins):
+        out[pl.ds(pl.multiple_of((place[0] ^ i) * rows, rows), rows), :] = ref[...].astype(F32)
+
+
+def stack_rows(place, pieces, tile):
+    rows, width = pieces[0].shape
+    return pl.pallas_call(
+        rows_kernel,
+        out_shape=jax.ShapeDtypeStruct((len(pieces) * rows, width), F32),
+        grid_spec=pltpu.PrefetchScalarGridSpec(
+            num_scalar_prefetch=1,
+            grid=(width // tile,),
+            in_specs=[pl.BlockSpec((rows, tile), lambda n, p: (0, n))] * len(pieces),
+            out_specs=pl.BlockSpec((len(pieces) * rows, tile), lambda n, p: (0, n)),
+        ),
+        compiler_params=pltpu.CompilerParams(vmem_limit_bytes=40 << 20),
+        name="stack_rows",
+    )(place, *pieces)
+
+
+def cols_kernel(place, *refs):
+    *ins, out = refs
+    cols = ins[0].shape[1]
+    for i, ref in enumerate(ins):
+        out[:, pl.ds(pl.multiple_of((place[0] ^ i) * cols, cols), cols)] = ref[...].astype(F32)
+
+
+def stack_cols(place, pieces, cols):
+    rows, width = pieces[0].shape
+    count = len(pieces)
+    if cols % 128:
+        ordered = jnp.stack([lax.dynamic_index_in_dim(jnp.stack(pieces), place[0] ^ i, 0, False) for i in range(count)])
+        ordered = ordered.reshape(count, rows, width // cols, cols).transpose(1, 2, 0, 3)
+        return ordered.reshape(rows, count * width).astype(F32)
+    return pl.pallas_call(
+        cols_kernel,
+        out_shape=jax.ShapeDtypeStruct((rows, count * width), F32),
+        grid_spec=pltpu.PrefetchScalarGridSpec(
+            num_scalar_prefetch=1,
+            grid=(width // cols,),
+            in_specs=[pl.BlockSpec((rows, cols), lambda n, p: (0, n))] * count,
+            out_specs=pl.BlockSpec((rows, count * cols), lambda n, p: (0, n)),
+        ),
+        compiler_params=pltpu.CompilerParams(vmem_limit_bytes=40 << 20),
+        name="stack_cols",
+    )(place, *pieces)
 
 
 def layer_norm(values):
@@ -384,18 +830,9 @@
         axis=2,
     ).reshape(-1)
 
-    vectors = jnp.stack([norm_gain, norm_bias, mlp_gain, mlp_bias])
-    own_qkv = jnp.concatenate(
-        [lax.dynamic_slice_in_dim(qkv_weight, s * head_cols, head_cols, 1), qkv_weight[:, width:]], axis=1
-    )
-    qkv_cols = own_qkv.shape[1]
-    span = 16
-    padded = jnp.pad(vectors, ((0, span - 4), (0, qkv_cols - shard)))
-    qkv_ring = ring.gather(jnp.concatenate([own_qkv, padded], axis=0))
-    hidden_all = seq_gather(hidden_in)
-    qkv_full = qkv_ring[:, :shard].reshape(width, qkv_cols)
-    vectors = qkv_ring[:, shard : shard + 4, :shard].transpose(1, 0, 2).reshape(4, width).astype(F32)
-    gain_one, bias_one, gain_two, bias_two = vectors[0], vectors[1], vectors[2], vectors[3]
+    place = jnp.stack([s, f]).astype(jnp.int32)
+    ff_own, ff_slots = pack(place, fc_weight, down_weight, fsdp_count, quarter)
+    flow = Flow(ring, ring.gather(ff_own, ff_slots))
 
     part = shard // seq_count
     pairs = [
@@ -409,89 +846,92 @@
         lax.dynamic_slice_in_dim(proj_weight, s * part, part, 0), ("seq", "fsdp"), pairs
     )
 
-    rows_all = hidden_all.reshape(group, width).astype(F32)
-    normed_all, _ = layer_norm(rows_all)
+    span = 32
+    vectors = jnp.stack([norm_gain, norm_bias, mlp_gain, mlp_bias])
+    padded = jnp.pad(vectors, ((0, span - 4), (0, 2 * HD - shard)))
+    own_kv = jnp.concatenate([qkv_weight[:, width:], padded], axis=0)
+    own_q = lax.dynamic_slice_in_dim(qkv_weight, s * head_cols, head_cols, 1)
+    opened = opening(hidden_in.reshape(tokens_here, width), own_kv, own_q, own_proj, fsdp_count, shard)
+    hidden_all, kv_ring, q_ring, proj_ring, kv_all = flow.advance(opened)
+    kv_weight = kv_ring[:, :shard].reshape(width, 2 * HD)
+    vectors = kv_ring[:, shard : shard + 4, :shard].transpose(1, 0, 2).reshape(4, width).astype(F32)
+    gain_one, bias_one, gain_two, bias_two = vectors[0], vectors[1], vectors[2], vectors[3]
+    q_weight = q_ring.reshape(width, head_cols)
+    proj_full = proj_ring.reshape(head_cols, width)
+    kv_all = kv_all.reshape(seq_count * fsdp_count, MB, count, 2 * HD)
+    normed_all, _ = layer_norm(hidden_all.reshape(group, width).astype(F32))
     attn_in = (normed_all * gain_one + bias_one).astype(BF)
     own_attn_in = attn_in[:tokens_here]
-    key_values = dot_plain(own_attn_in, qkv_full[:, head_cols:]).astype(BF)
-    kv_ring = ring.gather(key_values)
-    kv_rel = seq_gather(kv_ring)
-    kv_all = jnp.zeros((seq_count,) + kv_ring.shape, BF)
-    for i in range(seq_count):
-        kv_all = lax.dynamic_update_slice(kv_all, kv_rel[i][None], (s ^ i, 0, 0, 0))
-    kv_all = kv_all.reshape(seq_count * fsdp_count, MB, count, 2 * HD)
-    queries = dot_plain(attn_in, qkv_full[:, :head_cols]).astype(BF).reshape(seq_count, MB, count, head_cols)
-
-    own_proj = tie(own_proj, kv_ring)
-    proj_full = ring.gather(own_proj).reshape(head_cols, width)
-    fc_own = lax.dynamic_slice_in_dim(
-        fc_weight.reshape(shard, fsdp_count, seq_count, quarter), s, 1, 2
-    ).reshape(shard, fsdp_count * quarter)
-    fc_own = tie(fc_own, proj_full)
-    fc_full = ring.gather(fc_own).reshape(width, fsdp_count * quarter)
-    down_own = lax.dynamic_slice_in_dim(down_weight, s * quarter, quarter, 0)
-    down_own = tie(down_own, fc_full)
-    down_full = ring.gather(down_own).reshape(fsdp_count * quarter, width)
-    cotangent_all = seq_gather(tie(out_cotangent, hidden_all)).reshape(group, width)
+    queries = dot_plain(attn_in, q_weight).astype(BF).reshape(seq_count, MB, count, head_cols)
+    cotangent = out_cotangent.reshape(tokens_here, width)
+    cotangent_all = jnp.concatenate(seq_gather(tie(cotangent, queries)), axis=0)
 
     heads_out, logs = attend(tables, first, queries, kv_all, blocks)
     heads_rows = heads_out.reshape(group, head_cols)
 
-    def partial_sums(left, right):
-        return [
-            dot_plain(left[i * tokens_here : (i + 1) * tokens_here], right) for i in range(seq_count)
-        ]
+    def pieces(rows):
+        return [rows[i * tokens_here : (i + 1) * tokens_here] for i in range(seq_count)]
 
     hidden_own = hidden_in.reshape(tokens_here, width).astype(F32)
-    cotangent = out_cotangent.reshape(tokens_here, width)
-    resid = hidden_own + seq_scatter(partial_sums(heads_rows, proj_full))
+    resid = hidden_own + seq_scatter([dot_plain(piece, proj_full) for piece in pieces(heads_rows)])
+    resid, cotangent_all = flow.advance((resid, cotangent_all))
     normed_two, inverse_two = layer_norm(resid)
     mlp_in_own = (normed_two * gain_two + bias_two).astype(BF)
-    mlp_in = seq_gather(mlp_in_own).reshape(group, width)
-    pre_act = dot_plain(mlp_in, fc_full)
-    activ, gelu_pull = jax.vjp(gelu_tanh, pre_act)
-    activ = activ.astype(BF)
-    activ_grad = dot_cols(cotangent_all, down_full)
-    pre_grad = gelu_pull(activ_grad)[0].astype(BF)
-    fc_turned = fc_full
-    mlp_in_grad = seq_scatter(
-        [
-            dot_cols(pre_grad[i * tokens_here : (i + 1) * tokens_here], fc_turned)
-            for i in range(seq_count)
-        ]
-    )
-    result = (resid + seq_scatter(partial_sums(activ, down_full))).astype(BF)
+    mlp_in = flow.advance(jnp.concatenate(seq_gather(mlp_in_own), axis=0))
+    weights = flow.finish()
+    activ, pre_grad, mlp_in_part = middle(mlp_in, cotangent_all, weights, shard, BLOCK)
+    mlp_in_grad = seq_scatter([piece.astype(F32) for piece in pieces(mlp_in_part)])
+
+    order = ring.order()
+    early = 3
+    ff_early = turned(order[:early], mlp_in, pre_grad, activ, cotangent_all, shard)
+    ff_late = turned(order[early:], mlp_in, pre_grad, activ, cotangent_all, shard)
+    steps = ring.steps()
+
+    def ff_chunk(n):
+        at = steps.index(n)
+        return (ff_early[at] if at < early else ff_late[at - early]).astype(F32)
+
+    flow = Flow(ring, ring.scatter(ff_chunk))
+    lowered = lower(activ, weights, shard, BLOCK)
+    mlp_in_grad, lowered = flow.advance((mlp_in_grad, lowered))
 
     mlp_gain_part = jnp.sum(mlp_in_grad * normed_two, axis=0)
     mlp_bias_part = jnp.sum(mlp_in_grad, axis=0)
     resid_grad = cotangent.astype(F32) + norm_back(mlp_in_grad * gain_two, normed_two, inverse_two)
     branch_own = resid_grad.astype(BF)
-    branch = seq_gather(branch_own).reshape(group, width)
+    branch, lowered = flow.advance((jnp.concatenate(seq_gather(branch_own), axis=0), lowered))
+    result = (resid + seq_scatter([piece.astype(F32) for piece in pieces(lowered)])).astype(BF)
     heads_grad = dot_cols(branch, proj_full).astype(BF).reshape(seq_count, MB, count, head_cols)
-
-    down_sum = dot_rows(activ, cotangent_all).reshape(fsdp_count, quarter, width)
-    down_grad = ring.scatter(lambda t: lax.dynamic_index_in_dim(down_sum, t, 0, keepdims=False)).astype(BF)
-    fc_sum = dot_rows(mlp_in, pre_grad).reshape(fsdp_count, shard, fsdp_count * quarter)
-    fc_sum = tie(fc_sum, down_grad)
-    fc_grad = ring.scatter(lambda t: lax.dynamic_index_in_dim(fc_sum, t, 0, keepdims=False)).astype(BF)
-    proj_sum = dot_rows(heads_rows, branch).reshape(fsdp_count, part, width)
-    proj_sum = tie(proj_sum, fc_grad)
-    proj_grad = ring.scatter(lambda t: lax.dynamic_index_in_dim(proj_sum, t, 0, keepdims=False)).astype(BF)
-    proj_grad = lax.ppermute(proj_grad, ("seq", "fsdp"), back_pairs)
-
     query_grads, kv_grads = attend_back(
         tables, first, queries, kv_all, heads_out, logs, heads_grad, blocks
     )
+    query_grads, kv_grads, result = flow.advance((query_grads, kv_grads, result))
     query_rows = query_grads.reshape(group, head_cols)
-    query_sum = dot_rows(attn_in, query_rows).reshape(fsdp_count, shard, head_cols)
-    query_weight_grad = ring.scatter(
-        lambda t: lax.dynamic_index_in_dim(query_sum, t, 0, keepdims=False)
-    ).astype(BF)
+
+    proj_sum = dot_rows(heads_rows, branch).astype(BF).reshape(fsdp_count, part, width)
+    query_sum = dot_rows(attn_in, query_rows).astype(BF).reshape(fsdp_count, shard, head_cols)
+    folds = width // head_cols
+    query_sum = (
+        query_sum.reshape(fsdp_count, folds, shard // folds, head_cols)
+        .transpose(0, 2, 1, 3)
+        .reshape(fsdp_count, shard // folds, width)
+    )
+    attn_sum = jnp.concatenate([proj_sum, query_sum], axis=1)
+    attn_flow = Flow(
+        ring,
+        ring.scatter(
+            lambda n: lax.dynamic_index_in_dim(attn_sum, ring.owner(n), 0, keepdims=False).astype(F32)
+        ),
+    )
+    attn_grad = attn_flow.finish().astype(BF)
+    proj_grad = lax.ppermute(attn_grad[:part], ("seq", "fsdp"), back_pairs)
+    query_weight_grad = (
+        attn_grad[part:].reshape(shard // folds, folds, head_cols).transpose(1, 0, 2).reshape(shard, head_cols)
+    )
+
     attn_in_grad = seq_scatter(
-        [
-            dot_cols(query_rows[i * tokens_here : (i + 1) * tokens_here], qkv_full[:, :head_cols])
-            for i in range(seq_count)
-        ]
+        [dot_cols(piece, q_weight) for piece in pieces(query_rows)]
     )
     kv_grads = kv_grads.reshape(seq_count, fsdp_count, tokens_here, 2 * HD)
     kv_seq = seq_scatter(
@@ -500,8 +940,14 @@
             for i in range(seq_count)
         ]
     )
-    kv_own = ring.scatter(lambda t: lax.dynamic_index_in_dim(kv_seq, t, 0, keepdims=False)).astype(BF)
-    attn_in_grad = attn_in_grad + dot_cols(kv_own, qkv_full[:, head_cols:])
+    kv_seq = flow.advance(kv_seq)
+    ff_grad = flow.finish().astype(BF)
+    kv_flow = Flow(
+        ring,
+        ring.scatter(lambda n: lax.dynamic_index_in_dim(kv_seq, ring.owner(n), 0, keepdims=False)),
+    )
+    kv_own = kv_flow.finish().astype(BF)
+    attn_in_grad = attn_in_grad + dot_cols(kv_own, kv_weight)
     normed_one, inverse_one = layer_norm(hidden_own)
     norm_gain_part = jnp.sum(attn_in_grad * normed_one, axis=0)
     norm_bias_part = jnp.sum(attn_in_grad, axis=0)
@@ -514,27 +960,22 @@
     kv_sum = jnp.pad(kv_sum, ((0, 0), (0, 0), (0, tail_cols - 2 * HD)))
     vector_sum = jnp.pad(vector_sum, ((0, 0), (0, span - 4), (0, tail_cols - shard)))
     tail_sum = jnp.concatenate([kv_sum, vector_sum], axis=1)
-    tail = ring.scatter(lambda t: lax.dynamic_index_in_dim(tail_sum, t, 0, keepdims=False)).astype(BF)
+    tail_flow = Flow(
+        ring,
+        ring.scatter(lambda n: lax.dynamic_index_in_dim(tail_sum, ring.owner(n), 0, keepdims=False)),
+    )
+    tail = tail_flow.finish().astype(BF)
     tail = tail.astype(F32) + core_swap(tail).astype(F32)
     tail = tail.astype(BF)
     tail = tail.astype(F32) + chip_swap(tail).astype(F32)
     kv_weight_grad = tail[:shard, : 2 * HD]
     vector_grads = tail[shard : shard + 4, :shard]
 
-    def spread(piece, axis):
-        pieces = seq_gather(piece)
-        shape = piece.shape[:axis] + (seq_count,) + piece.shape[axis:]
-        out = jnp.zeros(shape, F32)
-        for i in range(seq_count):
-            start = [0] * len(shape)
-            start[axis] = s ^ i
-            out = lax.dynamic_update_slice(out, jnp.expand_dims(pieces[i], axis).astype(F32), start)
-        return out
-
-    grad_down = spread(down_grad, 0).reshape(ff_shard, width)
-    grad_fc = spread(fc_grad.reshape(shard, fsdp_count, quarter), 2).reshape(shard, ff)
-    grad_proj = spread(proj_grad, 0).reshape(shard, width)
-    grad_query = spread(query_weight_grad, 1).reshape(shard, width)
+    ff_pieces = seq_gather(ff_grad)
+    grad_fc = stack_cols(place, [piece[:shard] for piece in ff_pieces], quarter)
+    grad_down = stack_rows(place, [piece[shard:] for piece in ff_pieces], BLOCK)
+    grad_proj = stack_rows(place, seq_gather(proj_grad), BLOCK)
+    grad_query = stack_cols(place, seq_gather(query_weight_grad), head_cols)
     grad_qkv = jnp.concatenate([grad_query, kv_weight_grad], axis=1)
     return (
         result.reshape(hidden_in.shape),

time: 1110 us -> 753 us (0.68)
  local copies, waits for them, and re-layouts: 335 us -> 50.8 us
  Pallas kernels: 43.9 us -> 273 us
  waiting for transfers between devices: 346 us -> 211 us
  matrix products: 157 us -> 29.8 us
  starting transfers between devices: 141 us -> 101 us
    pallas_call x0 -> x10, Pallas kernels: none -> 237 us  [the longest x1 130 us: opening(): pl.pallas_call(functools.partial(opening_kernel, count=fsdp_count, shard=...]
    dynamic_update_slice x53 -> x8, local copies, waits for them, and re-layouts: 214 us -> 17.9 us  [put(): lax.dynamic_update_slice(out, piece[None], (owner, row) + (0,) * (value.n...]
    ppermute x15 -> x4, waiting for transfers between devices: 95.2 us -> 27.5 us  [gather(): low = lax.ppermute(low, 'fsdp', self.up)]
    dot_general x11 -> x6, matrix products: 69.9 us -> 11.1 us  [dot_cols(): lax.dot_general(left, right, (((1,), (1,)), ((), ())), preferred_element_...]
    ppermute x59 -> x33, waiting for transfers between devices: 165 us -> 106 us  [the longest x16 84.3 us: scatter(): down = lax.ppermute(down, 'fsdp', self.down)]
    dot_general x11 -> x5, matrix products: 51.2 us -> 10.2 us  [dot_plain(): lax.dot_general(left, right, (((1,), (0,)), ((), ())), preferred_element_...]
    broadcast_in_dim x17 -> x0, local copies, waits for them, and re-layouts: 28.3 us -> none  [the longest x9 16.8 us: gather(): piece[None]]
    dot_general x5 -> x3, matrix products: 36 us -> 8.43 us  [dot_rows(): lax.dot_general(left, right, (((0,), (0,)), ((), ())), preferred_element_...]
  transfers between devices with their start and end apart: 134 -> 77, of which waited for: 56 -> 37; matrix products, arithmetic and copies ran while one was open for 46% -> 15% of each run, Pallas kernels for 4% -> 29%
where the time goes in v2:
time: 753 us; the launch traced here: 742 us
  Pallas kernels  273 us (36%)
  waiting for transfers between devices  211 us (28%)
  starting transfers between devices  101 us (13%)
  other arithmetic  73.3 us (10%)
  local copies, waits for them, and re-layouts  50.8 us (7%)
  matrix products  29.8 us (4%)
    pallas_call x1, Pallas kernels, opening(): pl.pallas_call(functools.partial(opening_kernel, count=fsdp_count, shard=...  130 us
    ppermute x16, waiting for transfers between devices, scatter(): down = lax.ppermute(down, 'fsdp', self.down)  84.3 us
    ppermute x12, waiting for transfers between devices, chip_swap(): return lax.ppermute(value, 'seq', [(s, s ^ 2) for s in range(4)])  53.5 us
    pallas_call x1, Pallas kernels, middle(): pl.pallas_call(functools.partial(middle_kernel, step=256), out_shape=(jax...  42.3 us
    ppermute x16, starting transfers between devices, scatter(): up = lax.ppermute(up, 'fsdp', self.up)  35.7 us
    pallas_call x2, Pallas kernels, turned(): pl.pallas_call(turned_kernel, out_shape=jax.ShapeDtypeStruct((chunks, 2 *...  30.9 us
    ppermute x4, waiting for transfers between devices, gather(): low = lax.ppermute(low, 'fsdp', self.up)  27.5 us
    ppermute x4, waiting for transfers between devices, gather(): high = lax.ppermute(high, 'fsdp', self.down)  22.3 us
  transfers between devices with their start and end apart: 77, of which 37 were waited for; matrix products, arithmetic and copies ran while one was open for 15% of the time, Pallas kernels for 29%

profile of v2, /device:TPU:0, one launch (start us, length us, event | category | flops | bytes accessed | tf_op | source)
XLA Modules:
  0.0 741.6 jit_solution(12197633417616432976)
XLA Ops:
  17.0 130.4 %opening.1 = (bf16[4,256,2048]{2,1,0:T(8,128)(2,1)S(1)}, bf16[8,288,256]{2,1,0:T(8,128)(2,1)S(1)}, bf16[8,256,512]{2,1,0:T(8,128)(2,1)S(1)}, bf16[8,64,2048]{2,1,0:T(8,128)(2,1)S(1)}, bf16[4,8,256,256]{3,2,1,0:T(8,128)(2,1)}) custom-call(bf16[256,2048]{1,0:T(8,128)(2,1)S(1)} %bitcast.313, bf16[288,256]{1,0:T(8,128)(2,1)S(1)} %pad_maximum_fusion.8.kv_own, ...), custom_call_target="tpu_custom_call" | custom-call | tf_op jit(solution)/shard_map/opening/pallas_call | solution.py:533
  157.2 14.8 %attend.1 = (bf16[4,2,128,512]{3,2,1,0:T(8,128)(2,1)S(1)}, f32[4,2,4,128]{3,2,1,0:T(4,128)S(1)}) custom-call(s32[160]{0:T(256)S(1)} %reshape.583.tables, bf16[4,2,128,512]{3,2,1,0:T(8,128)(2,1)S(1)} %bitcast.327, bf16[32,2,128,256]{3,2,1,0:T(8,128)(2,1)S(1)} %bitcast.326, s32[4,2,1,128]{3,2,1,0:T(1,128)S(1)} %add_subtract_fusion.first_ref), custom_call_target="tpu_custom_call" | custom-call | flops 4294967296 | bytes 16777216 | tf_op jit(solution)/shard_map/attend/pallas_call | solution.py:288
  173.5 8.9 %collective-permute-start.3 = (bf16[512,2048]{1,0:T(8,128)(2,1)}, bf16[512,2048]{1,0:T(8,128)(2,1)}, u32[]{:S(2)}, u32[]{:S(2)}) collective-permute-start(bf16[512,2048]{1,0:T(8,128)(2,1)} %collective-permute-done), channel_id=1, source_target_pairs={{0,2},{2,4},{4,6},{6,7},{7,5},{5,3},{3,1},{1,0},{8,10},{10,12},{12... | collective-permute-start | bytes 6291464 | tf_op jit(solution)/shard_map/ppermute | solution.py:93
  191.3 21.6 %collective-permute-done.7 = bf16[256,2048]{1,0:T(8,128)(2,1)} collective-permute-done((bf16[256,2048]{1,0:T(8,128)(2,1)}, bf16[256,2048]{1,0:T(8,128)(2,1)}, u32[]{:S(2)}, u32[]{:S(2)}) %collective-permute-start.7) | collective-permute-done | bytes 1048608 | tf_op jit(solution)/shard_map/ppermute | solution.py:44
  216.7 11.1 %collective-permute-done.3 = bf16[512,2048]{1,0:T(8,128)(2,1)} collective-permute-done((bf16[512,2048]{1,0:T(8,128)(2,1)}, bf16[512,2048]{1,0:T(8,128)(2,1)}, u32[]{:S(2)}, u32[]{:S(2)}) %collective-permute-start.3) | collective-permute-done | bytes 2097184 | tf_op jit(solution)/shard_map/ppermute | solution.py:93
  245.5 13.6 %collective-permute-done.14 = bf16[256,2048]{1,0:T(8,128)(2,1)S(1)} collective-permute-done((bf16[256,2048]{1,0:T(8,128)(2,1)S(1)}, bf16[256,2048]{1,0:T(8,128)(2,1)S(1)}, u32[]{:S(2)}, u32[]{:S(2)}) %collective-permute-start.14) | collective-permute-done | bytes 1048608 | tf_op jit(solution)/shard_map/ppermute | solution.py:44
  267.7 15.9 %collective-permute-done.11 = bf16[512,2048]{1,0:T(8,128)(2,1)S(1)} collective-permute-done((bf16[512,2048]{1,0:T(8,128)(2,1)}, bf16[512,2048]{1,0:T(8,128)(2,1)S(1)}, u32[]{:S(2)}, u32[]{:S(2)}) %collective-permute-start.11) | collective-permute-done | bytes 2097184 | tf_op jit(solution)/shard_map/ppermute | solution.py:93
  291.3 17.6 %collective-permute-done.17 = bf16[256,2048]{1,0:T(8,128)(2,1)S(1)} collective-permute-done((bf16[256,2048]{1,0:T(8,128)(2,1)S(1)}, bf16[256,2048]{1,0:T(8,128)(2,1)S(1)}, u32[]{:S(2)}, u32[]{:S(2)}) %collective-permute-start.17) | collective-permute-done | bytes 1048608 | tf_op jit(solution)/shard_map/ppermute | solution.py:94
  311.5 42.3 %middle.1 = (bf16[1024,2048]{1,0:T(8,128)(2,1)}, bf16[1024,2048]{1,0:T(8,128)(2,1)}, bf16[1024,2048]{1,0:T(8,128)(2,1)}) custom-call(bf16[1024,2048]{1,0:T(8,128)(2,1)} %pad_maximum_fusion.1.rows_ref.left_ref, bf16[1024,2048]{1,0:T(8,128)(2,1)} %pad_maximum_fusion.cot_ref.right_two_ref, ...), custom_call_target="tpu_custom_call" | custom-call | tf_op jit(solution)/shard_map/middle/pallas_call | solution.py:640
  358.1 13.0 %turned.3 = bf16[3,512,2048]{2,1,0:T(8,128)(2,1)} custom-call(s32[3]{0:T(128)} %pad_add_fusion.3.order, bf16[1024,2048]{1,0:T(8,128)(2,1)} %pad_maximum_fusion.1.rows_ref.left_ref, bf16[1024,2048]{1,0:T(8,128)(2,1)} %get-tuple-element.106.right_ref, bf16[1024,2048]{1,0:T(8,128)(2,1)} %get-tuple-element.107.left_two_ref.rows_ref, ...), custom_call_target="tpu_custom_call" | custom-call | tf_op jit(solution)/shard_map/turned/pallas_call | solution.py:677
  382.3 14.1 %lower.1 = bf16[1024,2048]{1,0:T(8,128)(2,1)} custom-call(bf16[1024,2048]{1,0:T(8,128)(2,1)} %get-tuple-element.107.left_two_ref.rows_ref, bf16[8,512,2048]{2,1,0:T(8,128)(2,1)} %bitcast_dynamic-update-slice_fusion.6.fc_ref.down_ref), custom_call_target="tpu_custom_call" | custom-call | tf_op jit(solution)/shard_map/lower/pallas_call | solution.py:699
  417.8 15.0 %collective-permute-done.26 = bf16[256,2048]{1,0:T(8,128)(2,1)} collective-permute-done((bf16[256,2048]{1,0:T(8,128)(2,1)}, bf16[256,2048]{1,0:T(8,128)(2,1)}, u32[]{:S(2)}, u32[]{:S(2)}) %collective-permute-start.26) | collective-permute-done | bytes 1048608 | tf_op jit(solution)/shard_map/ppermute | solution.py:44
  435.7 17.8 %turned.2 = bf16[5,512,2048]{2,1,0:T(8,128)(2,1)} custom-call(s32[5]{0:T(128)} %stack.106.order, bf16[1024,2048]{1,0:T(8,128)(2,1)} %pad_maximum_fusion.1.rows_ref.left_ref, bf16[1024,2048]{1,0:T(8,128)(2,1)} %get-tuple-element.106.right_ref, bf16[1024,2048]{1,0:T(8,128)(2,1)} %get-tuple-element.107.left_two_ref.rows_ref, ...), custom_call_target="tpu_custom_call" | custom-call | tf_op jit(solution)/shard_map/turned/pallas_call | solution.py:677
  465.1 7.7 %fusion.4 = (bf16[512,2048]{1,0:T(8,128)(2,1)}, bf16[512,2048]{1,0:T(8,128)(2,1)}) fusion(bf16[512,2048]{1,0:T(8,128)(2,1)} %collective-permute-done.24, bf16[5,512,2048]{2,1,0:T(8,128)(2,1)} %turned.2, bf16[512,2048]{1,0:T(8,128)(2,1)} %collective-permute-done.23), kind=kLoop, calls=%fused_computation.30 | loop fusion | flops 8388608 | bytes 12582912 | tf_op jit(solution)/shard_map/convert_element_type | solution.py:129
  484.7 21.2 %attend_back.1 = (bf16[4,2,128,512]{3,2,1,0:T(8,128)(2,1)}, bf16[32,2,128,256]{3,2,1,0:T(8,128)(2,1)}) custom-call(s32[160]{0:T(256)} %copy-done.16, bf16[4,2,128,512]{3,2,1,0:T(8,128)(2,1)} %bitcast.328, bf16[32,2,128,256]{3,2,1,0:T(8,128)(2,1)} %bitcast.325, s32[4,2,1,128]{3,2,1,0:T(1,128)} %copy-done.13, bf16[4,2,128,512]{3,2,1,0:T(8,128)(2,1)} %copy-done.9, ...), custom_call_target="tpu_custom_call" | custom-call | flops 10737418240 | bytes 33554432 | tf_op jit(solution)/shard_map/attend_back/pallas_call | solution.py:321
  509.6 11.1 %collective-permute-done.29 = bf16[512,2048]{1,0:T(8,128)(2,1)} collective-permute-done((bf16[512,2048]{1,0:T(8,128)(2,1)}, bf16[512,2048]{1,0:T(8,128)(2,1)}, u32[]{:S(2)}, u32[]{:S(2)}) %collective-permute-start.29) | collective-permute-done | bytes 2097184 | tf_op jit(solution)/shard_map/ppermute | solution.py:115
  545.1 6.1 collective-permute-done.62
  555.1 5.8 fusion.2
  578.5 41.0 %collective-permute-done.66 = bf16[128,2048]{1,0:T(8,128)(2,1)S(1)} collective-permute-done((bf16[128,2048]{1,0:T(8,128)(2,1)}, bf16[128,2048]{1,0:T(8,128)(2,1)S(1)}, u32[]{:S(2)}, u32[]{:S(2)}) %collective-permute-start.66) | collective-permute-done | bytes 524320 | tf_op jit(solution)/shard_map/ppermute | solution.py:115
  623.5 6.1 collective-permute-done.65
  683.1 8.1 %collective-permute-start.72 = (bf16[64,2048]{1,0:T(8,128)(2,1)S(1)}, bf16[64,2048]{1,0:T(8,128)(2,1)S(1)}, u32[]{:S(2)}, u32[]{:S(2)}) collective-permute-start(bf16[64,2048]{1,0:T(8,128)(2,1)S(1)} %collective-permute-done.70.refs_0_), channel_id=1, source_target_pairs={{0,16},{8,24},{16,0},{24,8},{1,17},{9,25},{17,1},{25,9},{2,18},{10... | collective-permute-start | bytes 786440 | tf_op jit(solution)/shard_map/ppermute | solution.py:44
  694.4 21.4 %collective-permute-start.55 = (bf16[288,256]{1,0:T(8,128)(2,1)S(1)}, bf16[288,256]{1,0:T(8,128)(2,1)S(1)}, u32[]{:S(2)}, u32[]{:S(2)}) collective-permute-start(bf16[288,256]{1,0:T(8,128)(2,1)S(1)} %get-tuple-element.188), channel_id=1, source_target_pairs={{0,2},{2,4},{4,6},{6,7},{7,5},{5,3},{3,1},{1,0},{8,10},{10,12},{12... | collective-permute-start | bytes 442376 | tf_op jit(solution)/shard_map/ppermute | solution.py:114
  730.3 5.4 stack_rows.3
  735.7 5.4 stack_cols.3
  (388 shorter events, 264.0 us)
Async XLA Ops:
  9.6 137.8 %collective-permute-start.1 = (bf16[512,2048]{1,0:T(8,128)(2,1)}, bf16[512,2048]{1,0:T(8,128)(2,1)}, u32[]{:S(2)}, u32[]{:S(2)}) collective-permute-start(bf16[512,2048]{1,0:T(8,128)(2,1)} %get-tuple-element.81), channel_id=1, source_target_pairs={{2,0},{4,2},{6,4},{7,6},{5,7},{3,5},{1,3},{0,1},{10,8},{12,10},{14... | collective-permute-start | bytes 6291464 | tf_op jit(solution)/shard_map/ppermute | solution.py:94
  12.6 134.8 %collective-permute-start = (bf16[512,2048]{1,0:T(8,128)(2,1)}, bf16[512,2048]{1,0:T(8,128)(2,1)}, u32[]{:S(2)}, u32[]{:S(2)}) collective-permute-start(bf16[512,2048]{1,0:T(8,128)(2,1)} %get-tuple-element.81), channel_id=1, source_target_pairs={{0,2},{2,4},{4,6},{6,7},{7,5},{5,3},{3,1},{1,0},{8,10},{10,12},{12... | collective-permute-start | bytes 6291464 | tf_op jit(solution)/shard_map/ppermute | solution.py:93
  153.8 28.7 %collective-permute-start.9 = (bf16[256,2048]{1,0:T(8,128)(2,1)S(1)}, bf16[256,2048]{1,0:T(8,128)(2,1)}, u32[]{:S(2)}, u32[]{:S(2)}) collective-permute-start(bf16[256,2048]{1,0:T(8,128)(2,1)S(1)} %bitcast.342), channel_id=1, source_target_pairs={{0,16},{8,24},{16,0},{24,8},{1,17},{9,25},{17,1},{25,9},{2,18},{10... | collective-permute-start | bytes 3145736 | tf_op jit(solution)/shard_map/ppermute | solution.py:44
  173.5 54.2 %collective-permute-start.3 = (bf16[512,2048]{1,0:T(8,128)(2,1)}, bf16[512,2048]{1,0:T(8,128)(2,1)}, u32[]{:S(2)}, u32[]{:S(2)}) collective-permute-start(bf16[512,2048]{1,0:T(8,128)(2,1)} %collective-permute-done), channel_id=1, source_target_pairs={{0,2},{2,4},{4,6},{6,7},{7,5},{5,3},{3,1},{1,0},{8,10},{10,12},{12... | collective-permute-start | bytes 6291464 | tf_op jit(solution)/shard_map/ppermute | solution.py:93
  182.4 48.0 %collective-permute-start.4 = (bf16[512,2048]{1,0:T(8,128)(2,1)}, bf16[512,2048]{1,0:T(8,128)(2,1)}, u32[]{:S(2)}, u32[]{:S(2)}) collective-permute-start(bf16[512,2048]{1,0:T(8,128)(2,1)} %collective-permute-done.1), channel_id=1, source_target_pairs={{2,0},{4,2},{6,4},{7,6},{5,7},{3,5},{1,3},{0,1},{10,8},{12,10},{14... | collective-permute-start | bytes 6291464 | tf_op jit(solution)/shard_map/ppermute | solution.py:94
  236.5 47.2 %collective-permute-start.11 = (bf16[512,2048]{1,0:T(8,128)(2,1)}, bf16[512,2048]{1,0:T(8,128)(2,1)S(1)}, u32[]{:S(2)}, u32[]{:S(2)}) collective-permute-start(bf16[512,2048]{1,0:T(8,128)(2,1)} %collective-permute-done.3), channel_id=1, source_target_pairs={{0,2},{2,4},{4,6},{6,7},{7,5},{5,3},{3,1},{1,0},{8,10},{10,12},{12... | collective-permute-start | bytes 6291464 | tf_op jit(solution)/shard_map/ppermute | solution.py:93
  239.1 46.6 %collective-permute-start.12 = (bf16[512,2048]{1,0:T(8,128)(2,1)}, bf16[512,2048]{1,0:T(8,128)(2,1)S(1)}, u32[]{:S(2)}, u32[]{:S(2)}) collective-permute-start(bf16[512,2048]{1,0:T(8,128)(2,1)} %collective-permute-done.4), channel_id=1, source_target_pairs={{2,0},{4,2},{6,4},{7,6},{5,7},{3,5},{1,3},{0,1},{10,8},{12,10},{14... | collective-permute-start | bytes 6291464 | tf_op jit(solution)/shard_map/ppermute | solution.py:94
  357.6 38.8 %collective-permute-start.20 = (bf16[256,2048]{1,0:T(8,128)(2,1)}, bf16[256,2048]{1,0:T(8,128)(2,1)}, u32[]{:S(2)}, u32[]{:S(2)}) collective-permute-start(bf16[256,2048]{1,0:T(8,128)(2,1)} %get-tuple-element.185), channel_id=1, source_target_pairs={{0,8},{8,0},{16,24},{24,16},{1,9},{9,1},{17,25},{25,17},{2,10},{10... | collective-permute-start | bytes 3145736 | tf_op jit(solution)/shard_map/ppermute | solution.py:40
  414.2 46.1 %collective-permute-start.23 = (bf16[512,2048]{1,0:T(8,128)(2,1)}, bf16[512,2048]{1,0:T(8,128)(2,1)}, u32[]{:S(2)}, u32[]{:S(2)}) collective-permute-start(bf16[512,2048]{1,0:T(8,128)(2,1)} %pad_maximum_fusion.4), channel_id=1, source_target_pairs={{0,2},{2,4},{4,6},{6,7},{7,5},{5,3},{3,1},{1,0},{8,10},{10,12},{12... | collective-permute-start | bytes 6291464 | tf_op jit(solution)/shard_map/ppermute | solution.py:114
  417.5 45.8 %collective-permute-start.24 = (bf16[512,2048]{1,0:T(8,128)(2,1)}, bf16[512,2048]{1,0:T(8,128)(2,1)}, u32[]{:S(2)}, u32[]{:S(2)}) collective-permute-start(bf16[512,2048]{1,0:T(8,128)(2,1)} %pad_maximum_fusion.5), channel_id=1, source_target_pairs={{2,0},{4,2},{6,4},{7,6},{5,7},{3,5},{1,3},{0,1},{10,8},{12,10},{14... | collective-permute-start | bytes 6291464 | tf_op jit(solution)/shard_map/ppermute | solution.py:115
  417.8 35.7 %collective-permute-start.25 = (bf16[256,2048]{1,0:T(8,128)(2,1)}, bf16[256,2048]{1,0:T(8,128)(2,1)}, u32[]{:S(2)}, u32[]{:S(2)}) collective-permute-start(bf16[256,2048]{1,0:T(8,128)(2,1)} %get-tuple-element.160), channel_id=1, source_target_pairs={{0,8},{8,0},{16,24},{24,16},{1,9},{9,1},{17,25},{25,17},{2,10},{10... | collective-permute-start | bytes 3145736 | tf_op jit(solution)/shard_map/ppermute | solution.py:40
  464.6 41.3 %collective-permute-start.30 = (bf16[256,2048]{1,0:T(8,128)(2,1)}, bf16[256,2048]{1,0:T(8,128)(2,1)}, u32[]{:S(2)}, u32[]{:S(2)}) collective-permute-start(bf16[256,2048]{1,0:T(8,128)(2,1)} %get-tuple-element.183), channel_id=1, source_target_pairs={{0,8},{8,0},{16,24},{24,16},{1,9},{9,1},{17,25},{25,17},{2,10},{10... | collective-permute-start | bytes 3145736 | tf_op jit(solution)/shard_map/ppermute | solution.py:40
  472.8 47.9 %collective-permute-start.29 = (bf16[512,2048]{1,0:T(8,128)(2,1)}, bf16[512,2048]{1,0:T(8,128)(2,1)}, u32[]{:S(2)}, u32[]{:S(2)}) collective-permute-start(bf16[512,2048]{1,0:T(8,128)(2,1)} %get-tuple-element.166), channel_id=1, source_target_pairs={{2,0},{4,2},{6,4},{7,6},{5,7},{3,5},{1,3},{0,1},{10,8},{12,10},{14... | collective-permute-start | bytes 6291464 | tf_op jit(solution)/shard_map/ppermute | solution.py:115
  473.1 47.7 %collective-permute-start.28 = (bf16[512,2048]{1,0:T(8,128)(2,1)}, bf16[512,2048]{1,0:T(8,128)(2,1)}, u32[]{:S(2)}, u32[]{:S(2)}) collective-permute-start(bf16[512,2048]{1,0:T(8,128)(2,1)} %get-tuple-element.167), channel_id=1, source_target_pairs={{0,2},{2,4},{4,6},{6,7},{7,5},{5,3},{3,1},{1,0},{8,10},{10,12},{12... | collective-permute-start | bytes 6291464 | tf_op jit(solution)/shard_map/ppermute | solution.py:114
  544.5 85.1 %collective-permute-start.38 = (bf16[8,256,256]{2,1,0:T(8,128)(2,1)S(1)}, bf16[8,256,256]{2,1,0:T(8,128)(2,1)S(1)}, u32[]{:S(2)}, u32[]{:S(2)}) collective-permute-start(bf16[8,256,256]{2,1,0:T(8,128)(2,1)S(1)} %get-tuple-element.181), channel_id=1, source_target_pairs={{0,8},{8,0},{16,24},{24,16},{1,9},{9,1},{17,25},{25,17},{2,10},{10... | collective-permute-start | bytes 3145736 | tf_op jit(solution)/shard_map/ppermute | solution.py:40
  560.9 70.2 %collective-permute-start.37 = (bf16[512,2048]{1,0:T(8,128)(2,1)S(1)}, bf16[512,2048]{1,0:T(8,128)(2,1)S(1)}, u32[]{:S(2)}, u32[]{:S(2)}) collective-permute-start(bf16[512,2048]{1,0:T(8,128)(2,1)S(1)} %get-tuple-element.164), channel_id=1, source_target_pairs={{2,0},{4,2},{6,4},{7,6},{5,7},{3,5},{1,3},{0,1},{10,8},{12,10},{14... | collective-permute-start | bytes 6291464 | tf_op jit(solution)/shard_map/ppermute | solution.py:115
  568.0 63.1 %collective-permute-start.36 = (bf16[512,2048]{1,0:T(8,128)(2,1)S(1)}, bf16[512,2048]{1,0:T(8,128)(2,1)S(1)}, u32[]{:S(2)}, u32[]{:S(2)}) collective-permute-start(bf16[512,2048]{1,0:T(8,128)(2,1)S(1)} %get-tuple-element.165), channel_id=1, source_target_pairs={{0,2},{2,4},{4,6},{6,7},{7,5},{5,3},{3,1},{1,0},{8,10},{10,12},{12... | collective-permute-start | bytes 6291464 | tf_op jit(solution)/shard_map/ppermute | solution.py:114
  568.6 62.1 %collective-permute-start.40 = (bf16[8,256,256]{2,1,0:T(8,128)(2,1)S(1)}, bf16[8,256,256]{2,1,0:T(8,128)(2,1)S(1)}, u32[]{:S(2)}, u32[]{:S(2)}) collective-permute-start(bf16[8,256,256]{2,1,0:T(8,128)(2,1)S(1)} %fusion.28), channel_id=1, source_target_pairs={{0,16},{8,24},{16,0},{24,8},{1,17},{9,25},{17,1},{25,9},{2,18},{10... | collective-permute-start | bytes 3145736 | tf_op jit(solution)/shard_map/ppermute | solution.py:44
  572.2 47.3 %collective-permute-start.66 = (bf16[128,2048]{1,0:T(8,128)(2,1)}, bf16[128,2048]{1,0:T(8,128)(2,1)S(1)}, u32[]{:S(2)}, u32[]{:S(2)}) collective-permute-start(bf16[128,2048]{1,0:T(8,128)(2,1)} %get-tuple-element.174), channel_id=1, source_target_pairs={{2,0},{4,2},{6,4},{7,6},{5,7},{3,5},{1,3},{0,1},{10,8},{12,10},{14... | collective-permute-start | bytes 1572872 | tf_op jit(solution)/shard_map/ppermute | solution.py:115
  629.6 32.9 %collective-permute-start.33 = (bf16[256,2048]{1,0:T(8,128)(2,1)}, bf16[256,2048]{1,0:T(8,128)(2,1)}, u32[]{:S(2)}, u32[]{:S(2)}) collective-permute-start(bf16[256,2048]{1,0:T(8,128)(2,1)} %convolution_convert_fusion.3), channel_id=1, source_target_pairs={{0,8},{8,0},{16,24},{24,16},{1,9},{9,1},{17,25},{25,17},{2,10},{10... | collective-permute-start | bytes 3145736 | tf_op jit(solution)/shard_map/ppermute | solution.py:40
  629.6 32.9 %collective-permute-start.35 = (bf16[256,2048]{1,0:T(8,128)(2,1)}, bf16[256,2048]{1,0:T(8,128)(2,1)}, u32[]{:S(2)}, u32[]{:S(2)}) collective-permute-start(bf16[256,2048]{1,0:T(8,128)(2,1)} %fusion.11), channel_id=1, source_target_pairs={{0,16},{8,24},{16,0},{24,8},{1,17},{9,25},{17,1},{25,9},{2,18},{10... | collective-permute-start | bytes 3145736 | tf_op jit(solution)/shard_map/ppermute | solution.py:44
  657.9 63.7 %collective-permute-start.75 = (bf16[512,2048]{1,0:T(8,128)(2,1)S(1)}, bf16[512,2048]{1,0:T(8,128)(2,1)S(1)}, u32[]{:S(2)}, u32[]{:S(2)}) collective-permute-start(bf16[512,2048]{1,0:T(8,128)(2,1)S(1)} %fusion.1), channel_id=1, source_target_pairs={{0,16},{8,24},{16,0},{24,8},{1,17},{9,25},{17,1},{25,9},{2,18},{10... | collective-permute-start | bytes 6291464 | tf_op jit(solution)/shard_map/ppermute | solution.py:44
  680.3 49.5 %collective-permute-start.74 = (bf16[512,2048]{1,0:T(8,128)(2,1)S(1)}, bf16[512,2048]{1,0:T(8,128)(2,1)S(1)}, u32[]{:S(2)}, u32[]{:S(2)}) collective-permute-start(bf16[512,2048]{1,0:T(8,128)(2,1)S(1)} %fusion.1), channel_id=1, source_target_pairs={{0,8},{8,0},{16,24},{24,16},{1,9},{9,1},{17,25},{25,17},{2,10},{10... | collective-permute-start | bytes 6291464 | tf_op jit(solution)/shard_map/ppermute | solution.py:40
  683.1 32.7 %collective-permute-start.72 = (bf16[64,2048]{1,0:T(8,128)(2,1)S(1)}, bf16[64,2048]{1,0:T(8,128)(2,1)S(1)}, u32[]{:S(2)}, u32[]{:S(2)}) collective-permute-start(bf16[64,2048]{1,0:T(8,128)(2,1)S(1)} %collective-permute-done.70.refs_0_), channel_id=1, source_target_pairs={{0,16},{8,24},{16,0},{24,8},{1,17},{9,25},{17,1},{25,9},{2,18},{10... | collective-permute-start | bytes 786440 | tf_op jit(solution)/shard_map/ppermute | solution.py:44
  (104 other events, 1345.1 us)

commit v3 on v2

--- a/solution.py
+++ b/solution.py
@@ -17,6 +17,7 @@
 SCALE = HD ** (-0.5)
 LOG2E = math.log2(math.e)
 BF = jnp.bfloat16
+COST = pl.CostEstimate(flops=0, bytes_accessed=0, transcendentals=0)
 F32 = jnp.float32
 
 
@@ -104,13 +105,15 @@
     def order(self):
         return jnp.stack([self.owner(n) for n in self.steps()]).astype(jnp.int32)
 
-    def scatter(self, chunk):
+    def scatter(self, chunk, last=True):
         count = self.count
         middle = chunk(count // 2)
         half = middle.shape[0] // 2
         up = middle[:half].astype(BF)
         down = middle[half:].astype(BF)
         for step in range(count // 2 - 1, -1, -1):
+            if step == 0 and not last:
+                return up, down
             up = lax.ppermute(up, "fsdp", self.up)
             down = lax.ppermute(down, "fsdp", self.down)
             up, down = yield up, down
@@ -304,7 +307,7 @@
             ],
         ),
         compiler_params=pltpu.CompilerParams(vmem_limit_bytes=40 << 20),
-        cost_estimate=pl.CostEstimate(flops=4 * rows * HD * chunks * count * pieces, bytes_accessed=16 << 20, transcendentals=rows * chunks * count * pieces),
+        cost_estimate=COST,
         name="attend",
     )(tables, queries, key_values, first)
 
@@ -339,7 +342,7 @@
             ],
         ),
         compiler_params=pltpu.CompilerParams(vmem_limit_bytes=60 << 20),
-        cost_estimate=pl.CostEstimate(flops=10 * rows * HD * chunks * count * pieces, bytes_accessed=32 << 20, transcendentals=rows * chunks * count * pieces),
+        cost_estimate=COST,
         name="attend_back",
     )(tables, queries, key_values, first, out, logs, grads)
 
@@ -558,6 +561,7 @@
         compiler_params=pltpu.CompilerParams(
             collective_id=1, has_side_effects=True, vmem_limit_bytes=40 << 20
         ),
+        cost_estimate=COST,
         name="opening",
     )(hidden, kv_own, q_own, proj_own)
 
@@ -595,6 +599,7 @@
             ),
         ),
         compiler_params=pltpu.CompilerParams(vmem_limit_bytes=30 << 20),
+        cost_estimate=COST,
         name="pack",
     )(place, fc_weight, down_weight)
 
@@ -654,6 +659,7 @@
         out_specs=(cols, cols, pl.BlockSpec((count, width), lambda n: (0, 0))),
         scratch_shapes=[pltpu.VMEM((count, width), F32)],
         compiler_params=pltpu.CompilerParams(vmem_limit_bytes=60 << 20),
+        cost_estimate=COST,
         name="middle",
     )(rows, cot, weights, weights)
 
@@ -684,6 +690,7 @@
             out_specs=pl.BlockSpec((1, 2 * shard, width), lambda n, o: (n, 0, 0)),
         ),
         compiler_params=pltpu.CompilerParams(vmem_limit_bytes=60 << 20),
+        cost_estimate=COST,
         name="turned",
     )(order, left, right, left_two, right_two)
 
@@ -706,8 +713,390 @@
         ],
         out_specs=pl.BlockSpec((count, tile), lambda n: (0, n)),
         compiler_params=pltpu.CompilerParams(vmem_limit_bytes=60 << 20),
+        cost_estimate=COST,
         name="lower",
     )(rows, weights)
+
+
+class KernelScatter:
+    def __init__(self, count, chunk, outs, ins, sems, up, down):
+        self.steps, self.chunk, self.outs, self.ins, self.sems = count // 2, chunk, outs, ins, sems
+        self.devices = (up, down)
+        self.half = outs.shape[2] // 2
+        self.copies = {}
+
+    def start(self, step):
+        half = self.half
+        for way, sign in ((0, 1), (1, -1)):
+            mine = self.chunk(sign * (self.steps - step))
+            if step > 1:
+                self.copies[way, step - 2].wait_send()
+            out, into = self.outs.at[way, step % 2], self.ins.at[way, step]
+            rows = slice(way * half, (way + 1) * half)
+            rest = slice((1 - way) * half, (2 - way) * half)
+            if step == 0:
+                out, into = out.at[pl.ds(0, half)], into.at[pl.ds(0, half)]
+                out[...] = mine[rows].astype(BF)
+            elif step == 1:
+                out[rows] = (mine[rows] + self.ins[way, 0, :half].astype(F32)).astype(BF)
+                out[rest] = mine[rest].astype(BF)
+            else:
+                out[...] = (mine + self.ins[way, step - 1].astype(F32)).astype(BF)
+            self.copies[way, step] = send(out, into, self.sems, (way, step), self.devices[way])
+
+    def arrived(self, step):
+        self.copies[0, step].wait_recv()
+        self.copies[1, step].wait_recv()
+
+    def total(self):
+        last = self.steps - 1
+        return self.chunk(0) + self.ins[0, last].astype(F32) + self.ins[1, last].astype(F32)
+
+    def finish(self):
+        for (_, step), copy in self.copies.items():
+            if step >= self.steps - 2:
+                copy.wait_send()
+
+
+def closing_kernel(
+    kv_parts,
+    query_rows,
+    q_weight,
+    attn_parts,
+    ff_up,
+    ff_down,
+    ff_last,
+    resid_grad,
+    hidden,
+    kv_weight,
+    attn_in,
+    mlp_vectors,
+    grad_out,
+    attn_out,
+    ff_out,
+    tail_out,
+    kv_here,
+    kv_near,
+    kv_far,
+    kv_chip_in,
+    kv_outs,
+    kv_ins,
+    q_far_out,
+    q_far,
+    q_near,
+    q_chip_in,
+    q_here,
+    attn_here,
+    attn_outs,
+    attn_ins,
+    ff_here,
+    ff_ins,
+    ff_sum,
+    kv_total,
+    tail_here,
+    tail_outs,
+    tail_ins,
+    swap_out,
+    swap_in,
+    local,
+    kv_core_sems,
+    kv_chip_sems,
+    kv_sems,
+    q_core_sems,
+    q_chip_sems,
+    attn_sems,
+    ff_sems,
+    ff_chip_sems,
+    ff_core_sems,
+    tail_sems,
+    swap_sems,
+    *,
+    count,
+    shard,
+):
+    s, f, owner, up, down, chip, core = neighbours(count)
+    steps = count // 2
+    order = [steps] + [sign * n for n in range(steps - 1, 0, -1) for sign in (1, -1)] + [0]
+    other, sibling = lax.rem(s + 2, 4), core[0]
+    far = lax.rem(sibling + 2, 4)
+    tokens = hidden.shape[0]
+    greet(up, down, chip, core)
+
+    kv_pair = [
+        send(kv_parts.at[far], kv_far, kv_core_sems, (0,), core),
+        send(kv_parts.at[sibling], kv_near, kv_core_sems, (1,), core),
+    ]
+    loads = [
+        pltpu.make_async_copy(kv_parts.at[other], kv_here.at[1], local.at[0]),
+        pltpu.make_async_copy(kv_parts.at[s], kv_here.at[0], local.at[1]),
+        pltpu.make_async_copy(attn_parts, attn_here, local.at[2]),
+        pltpu.make_async_copy(ff_last, ff_here, local.at[3]),
+    ]
+    for copy in loads:
+        copy.start()
+    ff_rows = ff_last.shape[0] // 2
+    ff_parts = [pl.ds(i * ff_rows, ff_rows) for i in range(2)]
+    ff_ring = []
+
+    def ff_start(i):
+        for way, (source, device) in enumerate(((ff_up, up), (ff_down, down))):
+            copy = send(source.at[ff_parts[i]], ff_ins.at[way, ff_parts[i]], ff_sems, (way, i), device)
+            ff_ring.append(copy)
+
+    ff_start(0)
+
+    def query_part(i):
+        return dot_cols(query_rows[i * tokens : (i + 1) * tokens], q_weight[...])
+
+    q_far_out[...] = query_part(3).astype(BF)
+    q_pair = [send(q_far_out, q_far, q_core_sems, (0,), core)]
+    grad_out[...] = query_part(1).astype(BF)
+    loads[0].wait()
+    kv_pair[0].wait_recv()
+    kv_across = {}
+    for i, n in enumerate(order):
+        place = owner(n)
+        kv_here[1, place] = (kv_here[1, place].astype(F32) + kv_far[place].astype(F32)).astype(BF)
+        kv_across[n] = send(kv_here.at[1, place], kv_chip_in.at[i], kv_chip_sems, (i,), chip)
+    part = query_part(2)
+    q_pair[0].wait()
+    q_chip_out = q_far_out
+    q_chip_out[...] = (part + q_far[...].astype(F32)).astype(BF)
+    rows = tokens // 2
+    q_halves = [pl.ds(i * rows, rows) for i in range(2)]
+    q_across = [
+        send(q_chip_out.at[half], q_chip_in.at[half], q_chip_sems, (i,), chip) for i, half in enumerate(q_halves)
+    ]
+    q_pair.append(send(grad_out, q_near, q_core_sems, (1,), core))
+    q_here[...] = query_part(0)
+    loads[1].wait()
+    kv_pair[1].wait_recv()
+
+    def kv_chunk(n):
+        n = steps if n == -steps else n
+        place = owner(n)
+        here = kv_here[0, place].astype(F32) + kv_near[place].astype(F32)
+        return here + kv_chip_in[order.index(n)].astype(F32)
+
+    kv = KernelScatter(count, kv_chunk, kv_outs, kv_ins, kv_sems, up, down)
+    for step in range(steps):
+        for n in {steps - step, -(steps - step)} & set(order):
+            kv_across[n].wait_recv()
+        if step:
+            kv.arrived(step - 1)
+        kv.start(step)
+    ff_start(1)
+    loads[2].wait()
+
+    def attn_chunk(n):
+        return attn_here[order.index(steps if n == -steps else n)].astype(F32)
+
+    attn = KernelScatter(count, attn_chunk, attn_outs, attn_ins, attn_sems, up, down)
+    attn.start(0)
+
+    loads[3].wait()
+    ff_pair, ff_across = [], []
+
+    def ff_close(i):
+        rows = ff_parts[i]
+        for copy in ff_ring[2 * i : 2 * i + 2]:
+            copy.wait_recv()
+        arrived = ff_ins[0, rows].astype(F32) + ff_ins[1, rows].astype(F32)
+        ff_sum[rows] = (ff_here[rows].astype(F32) + arrived).astype(BF)
+        ff_across.append(send(ff_sum.at[rows], ff_out.at[2, rows], ff_chip_sems, (i,), chip))
+        ff_pair.append(send(ff_sum.at[rows], ff_out.at[1, rows], ff_core_sems, (i,), core))
+
+    ff_close(0)
+    kv_across[0].wait_recv()
+    kv.arrived(steps - 1)
+    kv_total[...] = kv.total().astype(BF)
+
+    q_pair[1].wait()
+    for copy in q_across:
+        copy.wait_recv()
+    q_here[...] += q_near[...].astype(F32) + q_chip_in[...].astype(F32)
+    for t in range(count):
+        cols = slice(t * shard, (t + 1) * shard)
+        q_here[:, cols] += dot_cols(kv_total[...], kv_weight[t, :shard, :])
+    gain = jnp.concatenate([kv_weight[t, shard : shard + 1, :shard] for t in range(count)], axis=1).astype(F32)
+    block = 64
+    gain_grad = jnp.zeros((1, hidden.shape[1]), F32)
+    bias_grad = jnp.zeros((1, hidden.shape[1]), F32)
+    for at in range(0, tokens, block):
+        here = slice(at, at + block)
+        normed, inverse = layer_norm(hidden[here].astype(F32))
+        grad = q_here[here]
+        gain_grad += jnp.sum(grad * normed, axis=0, keepdims=True)
+        bias_grad += jnp.sum(grad, axis=0, keepdims=True)
+        grad_out[here] = (resid_grad[here] + norm_back(grad * gain, normed, inverse)).astype(BF)
+
+    tail_here[...] = jnp.zeros_like(tail_here)
+    vectors = (gain_grad, bias_grad, mlp_vectors[0:1], mlp_vectors[1:2])
+    for t in range(count):
+        cols = slice(t * shard, (t + 1) * shard)
+        tail_here[t, :shard, :] = dot_rows(attn_in[:, cols], kv_total[...])
+        for j, vector in enumerate(vectors):
+            tail_here[t, shard + j : shard + j + 1, :shard] = vector[:, cols]
+    tail = KernelScatter(count, lambda n: tail_here[owner(n)], tail_outs, tail_ins, tail_sems, up, down)
+    for step in range(steps):
+        if step:
+            tail.arrived(step - 1)
+        tail.start(step)
+        if step == 0:
+            ff_close(1)
+        attn.arrived(step)
+        if step < steps - 1:
+            attn.start(step + 1)
+    attn_out[...] = attn.total().astype(BF)
+    tail.arrived(steps - 1)
+    total = tail.total()
+    swap_out[0] = total.astype(BF)
+    swaps = [send(swap_out.at[0], swap_in.at[0], swap_sems, (0,), core)]
+    for i, rows in enumerate(ff_parts):
+        ff_across[i].wait_recv()
+        ff_pair.append(send(ff_out.at[2, rows], ff_out.at[3, rows], ff_core_sems, (2 + i,), core))
+    keep = pltpu.make_async_copy(ff_sum, ff_out.at[0], local.at[4])
+    keep.start()
+    swaps[0].wait_recv()
+    swap_out[1] = (swap_out[0].astype(F32) + swap_in[0].astype(F32)).astype(BF)
+    swaps.append(send(swap_out.at[1], swap_in.at[1], swap_sems, (1,), chip))
+    swaps[1].wait_recv()
+    tail_out[...] = swap_out[1].astype(F32) + swap_in[1].astype(F32)
+    keep.wait()
+    for ring in (kv, attn, tail):
+        ring.finish()
+    for copy in kv_pair + q_across + list(kv_across.values()) + ff_ring + ff_across + swaps:
+        copy.wait_send()
+    for copy in ff_pair:
+        copy.wait()
+
+
+def closing(kv_parts, query_rows, q_weight, attn_parts, ff_flow, resid_grad, hidden, kv_weight, attn_in, mlp_vectors, shard):
+    ff_up, ff_down, ff_last = ff_flow
+    fsdp_count, tokens, kv_cols = kv_parts.shape[1:]
+    width = hidden.shape[1]
+    steps = fsdp_count // 2
+    dma = pltpu.SemaphoreType.DMA
+    anywhere = pl.BlockSpec(memory_space=pl.ANY)
+    inside = pl.BlockSpec(memory_space=pltpu.VMEM)
+    attn_shape = attn_parts.shape[1:]
+    tail_shape = kv_weight.shape[1:]
+    wide = pltpu.VMEM((tokens, width), BF)
+    kv_all = pltpu.VMEM((fsdp_count, tokens, kv_cols), BF)
+
+    def ring(shape):
+        return pltpu.VMEM((2, steps) + tuple(shape), BF)
+
+    def pair(shape):
+        return pltpu.VMEM((2, 2) + tuple(shape), BF)
+
+    ring_sems = dma((2, 2, steps))
+    return pl.pallas_call(
+        functools.partial(closing_kernel, count=fsdp_count, shard=shard),
+        out_shape=(
+            jax.ShapeDtypeStruct((tokens, width), BF),
+            jax.ShapeDtypeStruct(attn_shape, BF),
+            jax.ShapeDtypeStruct((4,) + ff_last.shape, BF),
+            jax.ShapeDtypeStruct(tail_shape, F32),
+        ),
+        in_specs=[anywhere, inside, inside, anywhere, anywhere, anywhere, anywhere] + [inside] * 5,
+        out_specs=(inside, inside, anywhere, inside),
+        scratch_shapes=[
+            pltpu.VMEM((2, fsdp_count, tokens, kv_cols), BF),
+            kv_all,
+            kv_all,
+            kv_all,
+            pair((tokens, kv_cols)),
+            ring((tokens, kv_cols)),
+            wide,
+            wide,
+            wide,
+            wide,
+            pltpu.VMEM((tokens, width), F32),
+            pltpu.VMEM(attn_parts.shape, BF),
+            pair(attn_shape),
+            ring(attn_shape),
+            pltpu.VMEM(ff_last.shape, BF),
+            pltpu.VMEM((2,) + ff_last.shape, BF),
+            pltpu.VMEM(ff_last.shape, BF),
+            pltpu.VMEM((tokens, kv_cols), BF),
+            pltpu.VMEM((fsdp_count,) + tail_shape, F32),
+            pair(tail_shape),
+            ring(tail_shape),
+            pltpu.VMEM((2,) + tail_shape, BF),
+            pltpu.VMEM((2,) + tail_shape, BF),
+            dma((5,)),
+            dma((2, 2)),
+            dma((2, fsdp_count)),
+            ring_sems,
+            dma((2, 2)),
+            dma((2, 2)),
+            ring_sems,
+            dma((2, 2, 2)),
+            dma((2, 2)),
+            dma((2, 4)),
+            ring_sems,
+            dma((2, 2)),
+        ],
+        compiler_params=pltpu.CompilerParams(
+            collective_id=2, has_side_effects=True, vmem_limit_bytes=61 << 20
+        ),
+        cost_estimate=COST,
+        name="closing",
+    )(
+        kv_parts,
+        query_rows,
+        q_weight,
+        attn_parts,
+        ff_up,
+        ff_down,
+        ff_last,
+        resid_grad,
+        hidden,
+        kv_weight,
+        attn_in,
+        mlp_vectors,
+    )
+
+
+def attn_turned_kernel(order, rows_ref, query_ref, proj_ref, out_ref):
+    part, cols = proj_ref.shape[0], query_ref.shape[1]
+    grad = dot_rows(rows_ref[...], query_ref[...]).astype(BF)
+    lines = out_ref.shape[1] - part
+    out_ref[0, :part] = proj_ref[...]
+    for k in range(grad.shape[0] // lines):
+        out_ref[0, part:, k * cols : (k + 1) * cols] = grad[k * lines : (k + 1) * lines]
+
+
+def attn_turned(order, rows, query_rows, proj_sum, shard):
+    count, width = rows.shape
+    cols = query_rows.shape[1]
+    chunks = order.shape[0]
+    part = proj_sum.shape[0] // chunks
+    folds = width // cols
+    lines = shard // folds
+    if shard % 128:
+        grad = dot_rows(rows, query_rows).astype(BF).reshape(chunks, folds, lines, cols)
+        grad = grad.transpose(0, 2, 1, 3).reshape(chunks, lines, width)
+        both = jnp.concatenate([proj_sum.reshape(chunks, part, width), grad], axis=1)
+        return jnp.stack([lax.dynamic_index_in_dim(both, order[i], 0, False) for i in range(chunks)])
+    return pl.pallas_call(
+        attn_turned_kernel,
+        out_shape=jax.ShapeDtypeStruct((chunks, part + lines, width), BF),
+        grid_spec=pltpu.PrefetchScalarGridSpec(
+            num_scalar_prefetch=1,
+            grid=(chunks,),
+            in_specs=[
+                pl.BlockSpec((count, shard), lambda n, o: (0, o[n])),
+                pl.BlockSpec((count, cols), lambda n, o: (0, 0)),
+                pl.BlockSpec((part, width), lambda n, o: (o[n], 0)),
+            ],
+            out_specs=pl.BlockSpec((1, part + lines, width), lambda n, o: (n, 0, 0)),
+        ),
+        compiler_params=pltpu.CompilerParams(vmem_limit_bytes=30 << 20),
+        cost_estimate=COST,
+        name="attn_turned",
+    )(order, rows, query_rows, proj_sum)
 
 
 def rows_kernel(place, *refs):
@@ -729,6 +1118,7 @@
             out_specs=pl.BlockSpec((len(pieces) * rows, tile), lambda n, p: (0, n)),
         ),
         compiler_params=pltpu.CompilerParams(vmem_limit_bytes=40 << 20),
+        cost_estimate=COST,
         name="stack_rows",
     )(place, *pieces)
 
@@ -757,6 +1147,7 @@
             out_specs=pl.BlockSpec((rows, count * cols), lambda n, p: (0, n)),
         ),
         compiler_params=pltpu.CompilerParams(vmem_limit_bytes=40 << 20),
+        cost_estimate=COST,
         name="stack_cols",
     )(place, *pieces)
 
@@ -892,9 +1283,9 @@
         at = steps.index(n)
         return (ff_early[at] if at < early else ff_late[at - early]).astype(F32)
 
-    flow = Flow(ring, ring.scatter(ff_chunk))
-    lowered = lower(activ, weights, shard, BLOCK)
-    mlp_in_grad, lowered = flow.advance((mlp_in_grad, lowered))
+    flow = Flow(ring, ring.scatter(ff_chunk, last=False))
+    mlp_in_grad, ff_late, activ_later = flow.advance((mlp_in_grad, ff_late, activ))
+    lowered = lower(activ_later, weights, shard, BLOCK)
 
     mlp_gain_part = jnp.sum(mlp_in_grad * normed_two, axis=0)
     mlp_bias_part = jnp.sum(mlp_in_grad, axis=0)
@@ -909,69 +1300,30 @@
     query_grads, kv_grads, result = flow.advance((query_grads, kv_grads, result))
     query_rows = query_grads.reshape(group, head_cols)
 
-    proj_sum = dot_rows(heads_rows, branch).astype(BF).reshape(fsdp_count, part, width)
-    query_sum = dot_rows(attn_in, query_rows).astype(BF).reshape(fsdp_count, shard, head_cols)
+    proj_sum = dot_rows(heads_rows, branch).astype(BF)
+    attn_parts = attn_turned(order, attn_in, query_rows, proj_sum, shard)
+    ff_up, ff_down = flow.finish()
+    grad_input, attn_grad, ff_all, tail = closing(
+        kv_grads.reshape(seq_count, fsdp_count, tokens_here, 2 * HD),
+        query_rows,
+        q_weight,
+        attn_parts,
+        (ff_up, ff_down, ff_late[-1]),
+        resid_grad,
+        hidden_in.reshape(tokens_here, width),
+        kv_ring,
+        own_attn_in,
+        jnp.stack([mlp_gain_part, mlp_bias_part]),
+        shard,
+    )
+    kv_weight_grad = tail[:shard, : 2 * HD]
+    vector_grads = tail[shard : shard + 4, :shard]
     folds = width // head_cols
-    query_sum = (
-        query_sum.reshape(fsdp_count, folds, shard // folds, head_cols)
-        .transpose(0, 2, 1, 3)
-        .reshape(fsdp_count, shard // folds, width)
-    )
-    attn_sum = jnp.concatenate([proj_sum, query_sum], axis=1)
-    attn_flow = Flow(
-        ring,
-        ring.scatter(
-            lambda n: lax.dynamic_index_in_dim(attn_sum, ring.owner(n), 0, keepdims=False).astype(F32)
-        ),
-    )
-    attn_grad = attn_flow.finish().astype(BF)
     proj_grad = lax.ppermute(attn_grad[:part], ("seq", "fsdp"), back_pairs)
     query_weight_grad = (
         attn_grad[part:].reshape(shard // folds, folds, head_cols).transpose(1, 0, 2).reshape(shard, head_cols)
     )
-
-    attn_in_grad = seq_scatter(
-        [dot_cols(piece, q_weight) for piece in pieces(query_rows)]
-    )
-    kv_grads = kv_grads.reshape(seq_count, fsdp_count, tokens_here, 2 * HD)
-    kv_seq = seq_scatter(
-        [
-            lax.dynamic_index_in_dim(kv_grads, s ^ i, 0, keepdims=False).astype(F32)
-            for i in range(seq_count)
-        ]
-    )
-    kv_seq = flow.advance(kv_seq)
-    ff_grad = flow.finish().astype(BF)
-    kv_flow = Flow(
-        ring,
-        ring.scatter(lambda n: lax.dynamic_index_in_dim(kv_seq, ring.owner(n), 0, keepdims=False)),
-    )
-    kv_own = kv_flow.finish().astype(BF)
-    attn_in_grad = attn_in_grad + dot_cols(kv_own, kv_weight)
-    normed_one, inverse_one = layer_norm(hidden_own)
-    norm_gain_part = jnp.sum(attn_in_grad * normed_one, axis=0)
-    norm_bias_part = jnp.sum(attn_in_grad, axis=0)
-    grad_input = (resid_grad + norm_back(attn_in_grad * gain_one, normed_one, inverse_one)).astype(BF)
-
-    kv_sum = dot_rows(own_attn_in, kv_own).reshape(fsdp_count, shard, 2 * HD)
-    vector_sum = jnp.stack([norm_gain_part, norm_bias_part, mlp_gain_part, mlp_bias_part])
-    vector_sum = vector_sum.reshape(4, fsdp_count, shard).transpose(1, 0, 2)
-    tail_cols = max(2 * HD, shard)
-    kv_sum = jnp.pad(kv_sum, ((0, 0), (0, 0), (0, tail_cols - 2 * HD)))
-    vector_sum = jnp.pad(vector_sum, ((0, 0), (0, span - 4), (0, tail_cols - shard)))
-    tail_sum = jnp.concatenate([kv_sum, vector_sum], axis=1)
-    tail_flow = Flow(
-        ring,
-        ring.scatter(lambda n: lax.dynamic_index_in_dim(tail_sum, ring.owner(n), 0, keepdims=False)),
-    )
-    tail = tail_flow.finish().astype(BF)
-    tail = tail.astype(F32) + core_swap(tail).astype(F32)
-    tail = tail.astype(BF)
-    tail = tail.astype(F32) + chip_swap(tail).astype(F32)
-    kv_weight_grad = tail[:shard, : 2 * HD]
-    vector_grads = tail[shard : shard + 4, :shard]
-
-    ff_pieces = seq_gather(ff_grad)
+    ff_pieces = [ff_all[i] for i in range(seq_count)]
     grad_fc = stack_cols(place, [piece[:shard] for piece in ff_pieces], quarter)
     grad_down = stack_rows(place, [piece[shard:] for piece in ff_pieces], BLOCK)
     grad_proj = stack_rows(place, seq_gather(proj_grad), BLOCK)

time: 753 us -> 716 us (0.951)
  Pallas kernels: 273 us -> 408 us
  waiting for transfers between devices: 211 us -> 126 us
  starting transfers between devices: 101 us -> 39 us
  other arithmetic: 73.3 us -> 58.1 us
  matrix products: 29.8 us -> 18.2 us
    pallas_call x0 -> x2, Pallas kernels: none -> 126 us  [the longest x1 121 us: closing(): pl.pallas_call(functools.partial(closing_kernel, count=fsdp_count, shard=...]
    ppermute x16 -> x3, waiting for transfers between devices: 84.3 us -> 7.23 us  [scatter(): down = lax.ppermute(down, 'fsdp', self.down)]
    ppermute x16 -> x3, starting transfers between devices: 35.7 us -> 3.55 us  [scatter(): up = lax.ppermute(up, 'fsdp', self.up)]
    ppermute x16 -> x3, starting transfers between devices: 20.2 us -> 2.86 us  [scatter(): down = lax.ppermute(down, 'fsdp', self.down)]
    ppermute x4, waiting for transfers between devices: 27.5 us -> 44.8 us  [gather(): low = lax.ppermute(low, 'fsdp', self.up)]
    ppermute x4, waiting for transfers between devices: 22.3 us -> 8.35 us  [gather(): high = lax.ppermute(high, 'fsdp', self.down)]
    convert_element_type x7 -> x0, other arithmetic: 12 us -> none  [the longest x1 4.75 us: shards(): normed_all, _ = layer_norm(hidden_all.reshape(group, width).astype(F32))]
    ppermute x16 -> x3, waiting for transfers between devices: 22 us -> 12 us  [scatter(): up = lax.ppermute(up, 'fsdp', self.up)]
  transfers between devices with their start and end apart: 77 -> 40, of which waited for: 37 -> 16; matrix products, arithmetic and copies ran while one was open for 15% -> 12% of each run, Pallas kernels for 29% -> 33%
where the time goes in v3:
time: 716 us; the launch traced here: 704 us
  Pallas kernels  408 us (57%)
  waiting for transfers between devices  126 us (18%)
  other arithmetic  58.1 us (8%)
  local copies, waits for them, and re-layouts  52.8 us (7%)
  starting transfers between devices  39 us (5%)
  matrix products  18.2 us (3%)
    pallas_call x1, Pallas kernels, opening(): pl.pallas_call(functools.partial(opening_kernel, count=fsdp_count, shard=...  132 us
    pallas_call x1, Pallas kernels, closing(): pl.pallas_call(functools.partial(closing_kernel, count=fsdp_count, shard=...  121 us
    ppermute x8, waiting for transfers between devices, chip_swap(): return lax.ppermute(value, 'seq', [(s, s ^ 2) for s in range(4)])  53.8 us
    ppermute x4, waiting for transfers between devices, gather(): low = lax.ppermute(low, 'fsdp', self.up)  44.8 us
    pallas_call x1, Pallas kernels, middle(): pl.pallas_call(functools.partial(middle_kernel, step=256), out_shape=(jax...  42.4 us
    pallas_call x2, Pallas kernels, turned(): pl.pallas_call(turned_kernel, out_shape=jax.ShapeDtypeStruct((chunks, 2 *...  30.8 us
    pallas_call x1, Pallas kernels, attend_back(): pl.pallas_call(functools.partial(attend_back_kernel, heads=heads, blocks=...  24.6 us
    dynamic_update_slice x8, local copies, waits for them, and re-layouts, put(): lax.dynamic_update_slice(out, piece[None], (owner, row) + (0,) * (value.n...  18.2 us
  transfers between devices with their start and end apart: 40, of which 16 were waited for; matrix products, arithmetic and copies ran while one was open for 12% of the time, Pallas kernels for 33%

profile of v3, /device:TPU:0, one launch (start us, length us, event | category | flops | bytes accessed | tf_op | source)
XLA Modules:
  0.0 704.5 jit_solution(3843104535420656640)
XLA Ops:
  17.2 132.2 %opening.1 = (bf16[4,256,2048]{2,1,0:T(8,128)(2,1)S(1)}, bf16[8,288,256]{2,1,0:T(8,128)(2,1)S(1)}, bf16[8,256,512]{2,1,0:T(8,128)(2,1)S(1)}, bf16[8,64,2048]{2,1,0:T(8,128)(2,1)S(1)}, bf16[4,8,256,256]{3,2,1,0:T(8,128)(2,1)}) custom-call(bf16[256,2048]{1,0:T(8,128)(2,1)S(1)} %bitcast.171, bf16[288,256]{1,0:T(8,128)(2,1)S(1)} %pad_maximum_fusion.6.kv_own, ...), custom_call_target="tpu_custom_call" | custom-call | tf_op jit(solution)/shard_map/opening/pallas_call | solution.py:536
  158.5 18.2 %attend.1 = (bf16[4,2,128,512]{3,2,1,0:T(8,128)(2,1)S(1)}, f32[4,2,4,128]{3,2,1,0:T(4,128)S(1)}) custom-call(s32[160]{0:T(256)S(1)} %reshape.455.tables, bf16[4,2,128,512]{3,2,1,0:T(8,128)(2,1)S(1)} %bitcast.173, bf16[32,2,128,256]{3,2,1,0:T(8,128)(2,1)S(1)} %bitcast.169, s32[4,2,1,128]{3,2,1,0:T(1,128)S(1)} %add_subtract_fusion.first_ref), custom_call_target="tpu_custom_call" | custom-call | tf_op jit(solution)/shard_map/attend/pallas_call | solution.py:291
  190.1 21.4 %collective-permute-done.7 = bf16[256,2048]{1,0:T(8,128)(2,1)} collective-permute-done((bf16[256,2048]{1,0:T(8,128)(2,1)}, bf16[256,2048]{1,0:T(8,128)(2,1)}, u32[]{:S(2)}, u32[]{:S(2)}) %collective-permute-start.7) | collective-permute-done | bytes 1048608 | tf_op jit(solution)/shard_map/ppermute | solution.py:45
  215.3 11.6 %collective-permute-done.3 = bf16[512,2048]{1,0:T(8,128)(2,1)} collective-permute-done((bf16[512,2048]{1,0:T(8,128)(2,1)}, bf16[512,2048]{1,0:T(8,128)(2,1)}, u32[]{:S(2)}, u32[]{:S(2)}) %collective-permute-start.3) | collective-permute-done | bytes 2097184 | tf_op jit(solution)/shard_map/ppermute | solution.py:94
  226.9 4.8 collective-permute-done.4
  236.2 4.9 collective-permute-start.11
  247.5 12.9 %collective-permute-done.14 = bf16[256,2048]{1,0:T(8,128)(2,1)S(1)} collective-permute-done((bf16[256,2048]{1,0:T(8,128)(2,1)S(1)}, bf16[256,2048]{1,0:T(8,128)(2,1)S(1)}, u32[]{:S(2)}, u32[]{:S(2)}) %collective-permute-start.14) | collective-permute-done | bytes 1048608 | tf_op jit(solution)/shard_map/ppermute | solution.py:45
  269.2 16.3 %collective-permute-done.11 = bf16[512,2048]{1,0:T(8,128)(2,1)S(1)} collective-permute-done((bf16[512,2048]{1,0:T(8,128)(2,1)}, bf16[512,2048]{1,0:T(8,128)(2,1)S(1)}, u32[]{:S(2)}, u32[]{:S(2)}) %collective-permute-start.11) | collective-permute-done | bytes 2097184 | tf_op jit(solution)/shard_map/ppermute | solution.py:94
  293.6 16.9 %collective-permute-done.16 = bf16[256,2048]{1,0:T(8,128)(2,1)S(1)} collective-permute-done((bf16[256,2048]{1,0:T(8,128)(2,1)S(1)}, bf16[256,2048]{1,0:T(8,128)(2,1)S(1)}, u32[]{:S(2)}, u32[]{:S(2)}) %collective-permute-start.16) | collective-permute-done | bytes 1048608 | tf_op jit(solution)/shard_map/ppermute | solution.py:94
  314.1 42.4 %middle.1 = (bf16[1024,2048]{1,0:T(8,128)(2,1)}, bf16[1024,2048]{1,0:T(8,128)(2,1)}, bf16[1024,2048]{1,0:T(8,128)(2,1)}) custom-call(bf16[1024,2048]{1,0:T(8,128)(2,1)} %pad_maximum_fusion.1.rows_ref.left_ref, bf16[1024,2048]{1,0:T(8,128)(2,1)} %pad_maximum_fusion.cot_ref.right_two_ref, ...), custom_call_target="tpu_custom_call" | custom-call | tf_op jit(solution)/shard_map/middle/pallas_call | solution.py:645
  360.7 13.0 %turned.2 = bf16[3,512,2048]{2,1,0:T(8,128)(2,1)} custom-call(s32[3]{0:T(128)} %pad_add_fusion.1.order, bf16[1024,2048]{1,0:T(8,128)(2,1)} %pad_maximum_fusion.1.rows_ref.left_ref, bf16[1024,2048]{1,0:T(8,128)(2,1)} %get-tuple-element.84.right_ref, bf16[1024,2048]{1,0:T(8,128)(2,1)} %get-tuple-element.91.left_two_ref.rows_ref, ...), custom_call_target="tpu_custom_call" | custom-call | tf_op jit(solution)/shard_map/turned/pallas_call | solution.py:683
  384.2 17.8 %turned.3 = bf16[5,512,2048]{2,1,0:T(8,128)(2,1)} custom-call(s32[5]{0:T(128)} %stack.125.order, bf16[1024,2048]{1,0:T(8,128)(2,1)} %pad_maximum_fusion.1.rows_ref.left_ref, bf16[1024,2048]{1,0:T(8,128)(2,1)} %get-tuple-element.84.right_ref, bf16[1024,2048]{1,0:T(8,128)(2,1)} %get-tuple-element.91.left_two_ref.rows_ref, ...), custom_call_target="tpu_custom_call" | custom-call | tf_op jit(solution)/shard_map/turned/pallas_call | solution.py:683
  420.7 14.6 %collective-permute-done.26 = bf16[256,2048]{1,0:T(8,128)(2,1)} collective-permute-done((bf16[256,2048]{1,0:T(8,128)(2,1)}, bf16[256,2048]{1,0:T(8,128)(2,1)}, u32[]{:S(2)}, u32[]{:S(2)}) %collective-permute-start.26) | collective-permute-done | bytes 1048608 | tf_op jit(solution)/shard_map/ppermute | solution.py:45
  441.8 14.1 %lower.1 = bf16[1024,2048]{1,0:T(8,128)(2,1)} custom-call(bf16[1024,2048]{1,0:T(8,128)(2,1)} %get-tuple-element.91.left_two_ref.rows_ref, bf16[8,512,2048]{2,1,0:T(8,128)(2,1)} %bitcast_dynamic-update-slice_fusion.6.fc_ref.down_ref), custom_call_target="tpu_custom_call" | custom-call | tf_op jit(solution)/shard_map/lower/pallas_call | solution.py:706
  458.2 4.9 collective-permute-done.24
  471.0 7.8 %fusion.6 = (bf16[512,2048]{1,0:T(8,128)(2,1)}, bf16[512,2048]{1,0:T(8,128)(2,1)}) fusion(bf16[512,2048]{1,0:T(8,128)(2,1)} %collective-permute-done.24, bf16[5,512,2048]{2,1,0:T(8,128)(2,1)} %turned.3, bf16[512,2048]{1,0:T(8,128)(2,1)} %collective-permute-done.23), kind=kLoop, calls=%fused_computation.16 | loop fusion | flops 8388608 | bytes 12582912 | tf_op jit(solution)/shard_map/convert_element_type | solution.py:132
  486.3 24.6 %attend_back.1 = (bf16[4,2,128,512]{3,2,1,0:T(8,128)(2,1)}, bf16[32,2,128,256]{3,2,1,0:T(8,128)(2,1)}) custom-call(s32[160]{0:T(256)} %copy-done.19, bf16[4,2,128,512]{3,2,1,0:T(8,128)(2,1)} %bitcast.174, bf16[32,2,128,256]{3,2,1,0:T(8,128)(2,1)} %bitcast.168, s32[4,2,1,128]{3,2,1,0:T(1,128)} %copy-done.17, bf16[4,2,128,512]{3,2,1,0:T(8,128)(2,1)} %copy-done.11, ...), custom_call_target="tpu_custom_call" | custom-call | tf_op jit(solution)/shard_map/attend_back/pallas_call | solution.py:324
  519.2 7.4 %collective-permute-done.28 = bf16[512,2048]{1,0:T(8,128)(2,1)} collective-permute-done((bf16[512,2048]{1,0:T(8,128)(2,1)}, bf16[512,2048]{1,0:T(8,128)(2,1)}, u32[]{:S(2)}, u32[]{:S(2)}) %collective-permute-start.28) | collective-permute-done | bytes 2097184 | tf_op jit(solution)/shard_map/ppermute | solution.py:117
  527.6 7.9 %fusion.4 = (bf16[512,2048]{1,0:T(8,128)(2,1)}, bf16[512,2048]{1,0:T(8,128)(2,1)}) fusion(bf16[512,2048]{1,0:T(8,128)(2,1)} %collective-permute-done.29, bf16[5,512,2048]{2,1,0:T(8,128)(2,1)} %turned.3, bf16[512,2048]{1,0:T(8,128)(2,1)} %collective-permute-done.28), kind=kLoop, calls=%fused_computation.12 | loop fusion | flops 8388608 | bytes 12582912 | tf_op jit(solution)/shard_map/convert_element_type | solution.py:132
  535.5 5.2 attn_turned.1.attn_parts
  542.8 121.0 %closing.1 = (bf16[256,2048]{1,0:T(8,128)(2,1)}, bf16[128,2048]{1,0:T(8,128)(2,1)}, bf16[4,512,2048]{2,1,0:T(8,128)(2,1)}, f32[288,256]{1,0:T(8,128)}) custom-call(bf16[4,8,256,256]{3,2,1,0:T(8,128)(2,1)} %bitcast.184, bf16[1024,512]{1,0:T(8,128)(2,1)} %bitcast.175, bf16[2048,512]{1,0:T(8,128)(2,1)} %bitcast.179, bf16[8,128,2048]{2,1,0:T(8,128)(2,1)} %copy-done.6, ...), custom_call_target="tpu_custom_call" | custom-call | tf_op jit(solution)/shard_map/closing/pallas_call | solution.py:994
  670.1 6.2 collective-permute-start.38
  685.2 5.4 stack_rows.3
  690.6 5.4 stack_cols.3
  (236 shorter events, 165.4 us)
Async XLA Ops:
  9.6 139.8 %collective-permute-start = (bf16[512,2048]{1,0:T(8,128)(2,1)}, bf16[512,2048]{1,0:T(8,128)(2,1)}, u32[]{:S(2)}, u32[]{:S(2)}) collective-permute-start(bf16[512,2048]{1,0:T(8,128)(2,1)} %get-tuple-element.59), channel_id=1, source_target_pairs={{0,2},{2,4},{4,6},{6,7},{7,5},{5,3},{3,1},{1,0},{8,10},{10,12},{12... | collective-permute-start | bytes 6291464 | tf_op jit(solution)/shard_map/ppermute | solution.py:94
  12.7 136.8 %collective-permute-start.1 = (bf16[512,2048]{1,0:T(8,128)(2,1)}, bf16[512,2048]{1,0:T(8,128)(2,1)}, u32[]{:S(2)}, u32[]{:S(2)}) collective-permute-start(bf16[512,2048]{1,0:T(8,128)(2,1)} %get-tuple-element.59), channel_id=1, source_target_pairs={{2,0},{4,2},{6,4},{7,6},{5,7},{3,5},{1,3},{0,1},{10,8},{12,10},{14... | collective-permute-start | bytes 6291464 | tf_op jit(solution)/shard_map/ppermute | solution.py:95
  155.9 25.4 %collective-permute-start.9 = (bf16[256,2048]{1,0:T(8,128)(2,1)S(1)}, bf16[256,2048]{1,0:T(8,128)(2,1)}, u32[]{:S(2)}, u32[]{:S(2)}) collective-permute-start(bf16[256,2048]{1,0:T(8,128)(2,1)S(1)} %bitcast.187), channel_id=1, source_target_pairs={{0,16},{8,24},{16,0},{24,8},{1,17},{9,25},{17,1},{25,9},{2,18},{10... | collective-permute-start | bytes 3145736 | tf_op jit(solution)/shard_map/ppermute | solution.py:45
  178.9 47.9 %collective-permute-start.3 = (bf16[512,2048]{1,0:T(8,128)(2,1)}, bf16[512,2048]{1,0:T(8,128)(2,1)}, u32[]{:S(2)}, u32[]{:S(2)}) collective-permute-start(bf16[512,2048]{1,0:T(8,128)(2,1)} %collective-permute-done), channel_id=1, source_target_pairs={{0,2},{2,4},{4,6},{6,7},{7,5},{5,3},{3,1},{1,0},{8,10},{10,12},{12... | collective-permute-start | bytes 6291464 | tf_op jit(solution)/shard_map/ppermute | solution.py:94
  179.0 52.6 %collective-permute-start.4 = (bf16[512,2048]{1,0:T(8,128)(2,1)}, bf16[512,2048]{1,0:T(8,128)(2,1)}, u32[]{:S(2)}, u32[]{:S(2)}) collective-permute-start(bf16[512,2048]{1,0:T(8,128)(2,1)} %collective-permute-done.1), channel_id=1, source_target_pairs={{2,0},{4,2},{6,4},{7,6},{5,7},{3,5},{1,3},{0,1},{10,8},{12,10},{14... | collective-permute-start | bytes 6291464 | tf_op jit(solution)/shard_map/ppermute | solution.py:95
  186.1 25.4 %collective-permute-start.7 = (bf16[256,2048]{1,0:T(8,128)(2,1)}, bf16[256,2048]{1,0:T(8,128)(2,1)}, u32[]{:S(2)}, u32[]{:S(2)}) collective-permute-start(bf16[256,2048]{1,0:T(8,128)(2,1)} %fusion.10), channel_id=1, source_target_pairs={{0,16},{8,24},{16,0},{24,8},{1,17},{9,25},{17,1},{25,9},{2,18},{10... | collective-permute-start | bytes 3145736 | tf_op jit(solution)/shard_map/ppermute | solution.py:45
  236.1 24.4 %collective-permute-start.14 = (bf16[256,2048]{1,0:T(8,128)(2,1)S(1)}, bf16[256,2048]{1,0:T(8,128)(2,1)S(1)}, u32[]{:S(2)}, u32[]{:S(2)}) collective-permute-start(bf16[256,2048]{1,0:T(8,128)(2,1)S(1)} %add_convert_fusion.4), channel_id=1, source_target_pairs={{0,16},{8,24},{16,0},{24,8},{1,17},{9,25},{17,1},{25,9},{2,18},{10... | collective-permute-start | bytes 3145736 | tf_op jit(solution)/shard_map/ppermute | solution.py:45
  236.2 49.2 %collective-permute-start.11 = (bf16[512,2048]{1,0:T(8,128)(2,1)}, bf16[512,2048]{1,0:T(8,128)(2,1)S(1)}, u32[]{:S(2)}, u32[]{:S(2)}) collective-permute-start(bf16[512,2048]{1,0:T(8,128)(2,1)} %collective-permute-done.3), channel_id=1, source_target_pairs={{0,2},{2,4},{4,6},{6,7},{7,5},{5,3},{3,1},{1,0},{8,10},{10,12},{12... | collective-permute-start | bytes 6291464 | tf_op jit(solution)/shard_map/ppermute | solution.py:94
  241.1 46.4 %collective-permute-start.12 = (bf16[512,2048]{1,0:T(8,128)(2,1)}, bf16[512,2048]{1,0:T(8,128)(2,1)S(1)}, u32[]{:S(2)}, u32[]{:S(2)}) collective-permute-start(bf16[512,2048]{1,0:T(8,128)(2,1)} %collective-permute-done.4), channel_id=1, source_target_pairs={{2,0},{4,2},{6,4},{7,6},{5,7},{3,5},{1,3},{0,1},{10,8},{12,10},{14... | collective-permute-start | bytes 6291464 | tf_op jit(solution)/shard_map/ppermute | solution.py:95
  287.6 22.9 %collective-permute-start.16 = (bf16[256,2048]{1,0:T(8,128)(2,1)S(1)}, bf16[256,2048]{1,0:T(8,128)(2,1)S(1)}, u32[]{:S(2)}, u32[]{:S(2)}) collective-permute-start(bf16[256,2048]{1,0:T(8,128)(2,1)S(1)} %slice.253), channel_id=1, source_target_pairs={{0,2},{2,4},{4,6},{6,7},{7,5},{5,3},{3,1},{1,0},{8,10},{10,12},{12... | collective-permute-start | bytes 3145736 | tf_op jit(solution)/shard_map/ppermute | solution.py:94
  360.2 41.9 %collective-permute-start.20 = (bf16[256,2048]{1,0:T(8,128)(2,1)}, bf16[256,2048]{1,0:T(8,128)(2,1)S(1)}, u32[]{:S(2)}, u32[]{:S(2)}) collective-permute-start(bf16[256,2048]{1,0:T(8,128)(2,1)} %get-tuple-element.136), channel_id=1, source_target_pairs={{0,8},{8,0},{16,24},{24,16},{1,9},{9,1},{17,25},{25,17},{2,10},{10... | collective-permute-start | bytes 3145736 | tf_op jit(solution)/shard_map/ppermute | solution.py:41
  376.6 25.5 %collective-permute-start.22 = (bf16[256,2048]{1,0:T(8,128)(2,1)}, bf16[256,2048]{1,0:T(8,128)(2,1)}, u32[]{:S(2)}, u32[]{:S(2)}) collective-permute-start(bf16[256,2048]{1,0:T(8,128)(2,1)} %add_convert_fusion.3), channel_id=1, source_target_pairs={{0,16},{8,24},{16,0},{24,8},{1,17},{9,25},{17,1},{25,9},{2,18},{10... | collective-permute-start | bytes 3145736 | tf_op jit(solution)/shard_map/ppermute | solution.py:45
  381.5 25.1 %collective-permute-start.18 = (bf16[256,2048]{1,0:T(8,128)(2,1)}, bf16[256,2048]{1,0:T(8,128)(2,1)}, u32[]{:S(2)}, u32[]{:S(2)}) collective-permute-start(bf16[256,2048]{1,0:T(8,128)(2,1)} %get-tuple-element.131), channel_id=1, source_target_pairs={{0,2},{2,4},{4,6},{6,7},{7,5},{5,3},{3,1},{1,0},{8,10},{10,12},{12... | collective-permute-start | bytes 3145736 | tf_op jit(solution)/shard_map/ppermute | solution.py:117
  383.0 25.0 %collective-permute-start.19 = (bf16[256,2048]{1,0:T(8,128)(2,1)}, bf16[256,2048]{1,0:T(8,128)(2,1)}, u32[]{:S(2)}, u32[]{:S(2)}) collective-permute-start(bf16[256,2048]{1,0:T(8,128)(2,1)} %get-tuple-element.130), channel_id=1, source_target_pairs={{2,0},{4,2},{6,4},{7,6},{5,7},{3,5},{1,3},{0,1},{10,8},{12,10},{14... | collective-permute-start | bytes 3145736 | tf_op jit(solution)/shard_map/ppermute | solution.py:118
  411.4 23.9 %collective-permute-start.26 = (bf16[256,2048]{1,0:T(8,128)(2,1)}, bf16[256,2048]{1,0:T(8,128)(2,1)}, u32[]{:S(2)}, u32[]{:S(2)}) collective-permute-start(bf16[256,2048]{1,0:T(8,128)(2,1)} %get-tuple-element.112), channel_id=1, source_target_pairs={{0,16},{8,24},{16,0},{24,8},{1,17},{9,25},{17,1},{25,9},{2,18},{10... | collective-permute-start | bytes 3145736 | tf_op jit(solution)/shard_map/ppermute | solution.py:45
  417.0 46.1 %collective-permute-start.24 = (bf16[512,2048]{1,0:T(8,128)(2,1)}, bf16[512,2048]{1,0:T(8,128)(2,1)}, u32[]{:S(2)}, u32[]{:S(2)}) collective-permute-start(bf16[512,2048]{1,0:T(8,128)(2,1)} %pad_maximum_fusion.5), channel_id=1, source_target_pairs={{2,0},{4,2},{6,4},{7,6},{5,7},{3,5},{1,3},{0,1},{10,8},{12,10},{14... | collective-permute-start | bytes 6291464 | tf_op jit(solution)/shard_map/ppermute | solution.py:118
  419.7 45.8 %collective-permute-start.23 = (bf16[512,2048]{1,0:T(8,128)(2,1)}, bf16[512,2048]{1,0:T(8,128)(2,1)}, u32[]{:S(2)}, u32[]{:S(2)}) collective-permute-start(bf16[512,2048]{1,0:T(8,128)(2,1)} %pad_maximum_fusion.4), channel_id=1, source_target_pairs={{0,2},{2,4},{4,6},{6,7},{7,5},{5,3},{3,1},{1,0},{8,10},{10,12},{12... | collective-permute-start | bytes 6291464 | tf_op jit(solution)/shard_map/ppermute | solution.py:117
  420.7 35.2 %collective-permute-start.25 = (bf16[256,2048]{1,0:T(8,128)(2,1)}, bf16[256,2048]{1,0:T(8,128)(2,1)S(1)}, u32[]{:S(2)}, u32[]{:S(2)}) collective-permute-start(bf16[256,2048]{1,0:T(8,128)(2,1)} %get-tuple-element.112), channel_id=1, source_target_pairs={{0,8},{8,0},{16,24},{24,16},{1,9},{9,1},{17,25},{25,17},{2,10},{10... | collective-permute-start | bytes 3145736 | tf_op jit(solution)/shard_map/ppermute | solution.py:41
  470.5 45.2 %collective-permute-start.30 = (bf16[256,2048]{1,0:T(8,128)(2,1)}, bf16[256,2048]{1,0:T(8,128)(2,1)}, u32[]{:S(2)}, u32[]{:S(2)}) collective-permute-start(bf16[256,2048]{1,0:T(8,128)(2,1)} %get-tuple-element.134), channel_id=1, source_target_pairs={{0,8},{8,0},{16,24},{24,16},{1,9},{9,1},{17,25},{25,17},{2,10},{10... | collective-permute-start | bytes 3145736 | tf_op jit(solution)/shard_map/ppermute | solution.py:41
  478.8 47.9 %collective-permute-start.28 = (bf16[512,2048]{1,0:T(8,128)(2,1)}, bf16[512,2048]{1,0:T(8,128)(2,1)}, u32[]{:S(2)}, u32[]{:S(2)}) collective-permute-start(bf16[512,2048]{1,0:T(8,128)(2,1)} %get-tuple-element.119), channel_id=1, source_target_pairs={{0,2},{2,4},{4,6},{6,7},{7,5},{5,3},{3,1},{1,0},{8,10},{10,12},{12... | collective-permute-start | bytes 6291464 | tf_op jit(solution)/shard_map/ppermute | solution.py:117
  479.8 47.8 %collective-permute-start.29 = (bf16[512,2048]{1,0:T(8,128)(2,1)}, bf16[512,2048]{1,0:T(8,128)(2,1)}, u32[]{:S(2)}, u32[]{:S(2)}) collective-permute-start(bf16[512,2048]{1,0:T(8,128)(2,1)} %get-tuple-element.118), channel_id=1, source_target_pairs={{2,0},{4,2},{6,4},{7,6},{5,7},{3,5},{1,3},{0,1},{10,8},{12,10},{14... | collective-permute-start | bytes 6291464 | tf_op jit(solution)/shard_map/ppermute | solution.py:118
  482.4 33.3 %collective-permute-start.32 = (bf16[256,2048]{1,0:T(8,128)(2,1)}, bf16[256,2048]{1,0:T(8,128)(2,1)}, u32[]{:S(2)}, u32[]{:S(2)}) collective-permute-start(bf16[256,2048]{1,0:T(8,128)(2,1)} %add_convert_fusion.2), channel_id=1, source_target_pairs={{0,16},{8,24},{16,0},{24,8},{1,17},{9,25},{17,1},{25,9},{2,18},{10... | collective-permute-start | bytes 3145736 | tf_op jit(solution)/shard_map/ppermute | solution.py:45
  669.8 27.3 %collective-permute-start.33 = (bf16[256,512]{1,0:T(8,128)(2,1)S(1)}, bf16[256,512]{1,0:T(8,128)(2,1)S(1)}, u32[]{:S(2)}, u32[]{:S(2)}) collective-permute-start(bf16[256,512]{1,0:T(8,128)(2,1)S(1)} %bitcast.181), channel_id=1, source_target_pairs={{0,8},{8,0},{16,24},{24,16},{1,9},{9,1},{17,25},{25,17},{2,10},{10... | collective-permute-start | bytes 786440 | tf_op jit(solution)/shard_map/ppermute | solution.py:41
  670.1 27.0 %collective-permute-start.38 = (bf16[64,2048]{1,0:T(8,128)(2,1)S(1)}, bf16[64,2048]{1,0:T(8,128)(2,1)S(1)}, u32[]{:S(2)}, u32[]{:S(2)}) collective-permute-start(bf16[64,2048]{1,0:T(8,128)(2,1)S(1)} %collective-permute-done.36.refs_0_), channel_id=1, source_target_pairs={{0,16},{8,24},{16,0},{24,8},{1,17},{9,25},{17,1},{25,9},{2,18},{10... | collective-permute-start | bytes 786440 | tf_op jit(solution)/shard_map/ppermute | solution.py:45
  (55 other events, 733.0 us)

commit v4 on v3

--- a/solution.py
+++ b/solution.py
@@ -33,32 +33,6 @@
     return lax.dot_general(left, right, (((1,), (0,)), ((), ())), preferred_element_type=F32)
 
 
-def tie(value, after):
-    return lax.optimization_barrier((value, after))[0]
-
-
-def core_swap(value):
-    return lax.ppermute(value, "seq", [(s, s ^ 1) for s in range(4)])
-
-
-def chip_swap(value):
-    return lax.ppermute(value, "seq", [(s, s ^ 2) for s in range(4)])
-
-
-def seq_gather(value):
-    across = chip_swap(value)
-    pair = core_swap(value)
-    pair_across = core_swap(across)
-    return [value, pair, across, pair_across]
-
-
-def seq_scatter(parts):
-    far = core_swap(parts[3].astype(BF))
-    near = core_swap(parts[1].astype(BF))
-    across = chip_swap((parts[2] + far.astype(F32)).astype(BF))
-    return parts[0] + near.astype(F32) + across.astype(F32)
-
-
 def ring_order(count):
     return [2 * i for i in range(count // 2)] + [2 * i + 1 for i in reversed(range(count // 2))]
 
@@ -79,25 +53,6 @@
         at = lax.rem(self.at + (step + count), count)
         return jnp.where(at < half, 2 * at, 2 * (count - 1 - at) + 1)
 
-    def gather(self, value, out):
-        count = self.count
-        half = value.shape[0] // 2
-
-        def put(piece, owner, row):
-            return lax.dynamic_update_slice(out, piece[None], (owner, row) + (0,) * (value.ndim - 1))
-
-        low = high = value
-        for step in range(1, count // 2 + 1):
-            last = step == count // 2
-            if last:
-                low, high = low[:half], high[half:]
-            low = lax.ppermute(low, "fsdp", self.up)
-            high = lax.ppermute(high, "fsdp", self.down)
-            low, high = yield low, high
-            out = put(low, self.owner(-step), 0)
-            out = put(high, self.owner(step), half if last else 0)
-        return out
-
     def steps(self):
         half = self.count // 2
         return [half] + [sign * n for n in range(half - 1, 0, -1) for sign in (1, -1)] + [0]
@@ -105,31 +60,14 @@
     def order(self):
         return jnp.stack([self.owner(n) for n in self.steps()]).astype(jnp.int32)
 
-    def scatter(self, chunk, last=True):
-        count = self.count
-        middle = chunk(count // 2)
-        half = middle.shape[0] // 2
-        up = middle[:half].astype(BF)
-        down = middle[half:].astype(BF)
-        for step in range(count // 2 - 1, -1, -1):
-            if step == 0 and not last:
-                return up, down
+    def scatter(self, up, down, chunk):
+        for step in range(self.count // 2 - 3, 0, -1):
             up = lax.ppermute(up, "fsdp", self.up)
             down = lax.ppermute(down, "fsdp", self.down)
             up, down = yield up, down
-            up, down = up.astype(F32), down.astype(F32)
-            if step == count // 2 - 1:
-                mine = chunk(step)
-                up = jnp.concatenate([mine[:half] + up, mine[half:]], axis=0)
-                mine = chunk(-step)
-                down = jnp.concatenate([mine[:half], mine[half:] + down], axis=0)
-            elif step:
-                up = chunk(step) + up
-                down = chunk(-step) + down
-            else:
-                return chunk(0) + up + down
-            up = up.astype(BF)
-            down = down.astype(BF)
+            up = (chunk(step).astype(F32) + up.astype(F32)).astype(BF)
+            down = (chunk(-step).astype(F32) + down.astype(F32)).astype(BF)
+        return up, down
 
 
 class Flow:
@@ -368,6 +306,54 @@
     pl.semaphore_wait(barrier, len(devices))
 
 
+def met(device, s, f):
+    return (device[0] == s) & (device[1] == f)
+
+
+def greet_also(devices, sources, own, s, f):
+    barrier = pltpu.get_barrier_semaphore()
+    for device in devices:
+        pl.semaphore_signal(barrier, inc=1, device_id=device, device_id_type=pl.DeviceIdType.MESH)
+    for device in sources:
+
+        @pl.when(jnp.logical_not(met(device, s, f)))
+        def _():
+            pl.semaphore_signal(barrier, inc=1, device_id=device, device_id_type=pl.DeviceIdType.MESH)
+
+    pl.semaphore_wait(barrier, len(devices) + len(sources) - own)
+
+
+class Maybe:
+    def __init__(self, source, target, landing, send_sem, recv_sem, landing_sem, local_sem, device, sender, s, f):
+        self.here, self.from_here = met(device, s, f), met(sender, s, f)
+        kind = dict(device_id_type=pl.DeviceIdType.MESH)
+        self.copy = pltpu.make_async_remote_copy(source, target, send_sem, recv_sem, device_id=device, **kind)
+        self.into = pltpu.make_async_remote_copy(source, landing, send_sem, landing_sem, device_id=device, **kind)
+        self.stay = pltpu.make_async_copy(source, target, local_sem)
+
+        @pl.when(self.here)
+        def _():
+            self.stay.start()
+
+        @pl.when(jnp.logical_not(self.here))
+        def _():
+            self.copy.start()
+
+    def arrived(self):
+        @pl.when(jnp.logical_not(self.from_here))
+        def _():
+            self.into.wait_recv()
+
+    def left(self):
+        @pl.when(self.here)
+        def _():
+            self.stay.wait()
+
+        @pl.when(jnp.logical_not(self.here))
+        def _():
+            self.copy.wait_send()
+
+
 def send(source, target, sems, index, device):
     copy = pltpu.make_async_remote_copy(
         src_ref=source,
@@ -409,13 +395,17 @@
 def opening_kernel(
     hidden,
     kv_own,
-    q_own,
-    proj_own,
+    qkv_weight,
+    proj_weight,
+    fc_weight,
+    cot,
     hidden_out,
     kvw_out,
     qw_out,
     proj_out,
     kv_out,
+    fc_out,
+    cot_out,
     weights,
     mine,
     hid_chip,
@@ -427,20 +417,64 @@
     kv_chip,
     kv_core,
     kv_far,
+    fc_sems,
+    cot_sems,
+    move_sems,
+    cut_sems,
     local,
     *,
     count,
     shard,
 ):
     s, f, owner, up, down, chip, core = neighbours(count)
-    greet(up, down, chip, core)
     steps = count // 2
+    per = count // 4
+    target = (f // per, 4 * lax.rem(f, per) + s)
+    source = (lax.rem(f, 4), s * per + f // 4)
+    own_goes = met(target, s, f).astype(jnp.int32)
+    greet_also((up, down, chip, core), (source,), own_goes, s, f)
+    part = proj_out.shape[1]
+    q_cols = qw_out.shape[2]
+    q_own = qkv_weight.at[:, pl.ds(pl.multiple_of(s * q_cols, q_cols), q_cols)]
+    proj_own, fc_own = proj_out.at[f], fc_out.at[f]
     rings = [
         KernelRing(count, own, slots, sems, owner, up, down)
-        for own, slots, sems in ((kv_own, kvw_out, kvw_sems), (q_own, qw_out, q_sems), (proj_own, proj_out, proj_sems))
+        for own, slots, sems in (
+            (kv_own, kvw_out, kvw_sems),
+            (q_own, qw_out, q_sems),
+            (proj_own, proj_out, proj_sems),
+            (fc_own, fc_out, fc_sems),
+        )
     ]
-    kvw, qw, proj = rings
+    kvw, qw, proj, fc = rings
     kvw.start(1)
+    moved = Maybe(
+        proj_weight.at[pl.ds(pl.multiple_of(s * part, part), part)],
+        proj_out.at[target[1]],
+        proj_own,
+        move_sems.at[0],
+        move_sems.at[1],
+        move_sems.at[1],
+        move_sems.at[2],
+        target,
+        source,
+        s,
+        f,
+    )
+    if fc_weight.shape[1] == fc_out.shape[2]:
+        cuts = [pltpu.make_async_copy(fc_weight, fc_own, cut_sems.at[0])]
+    else:
+        cols = fc_out.shape[2] // count
+        cuts = [
+            pltpu.make_async_copy(
+                fc_weight.at[:, pl.ds(pl.multiple_of((g * 4 + s) * cols, cols), cols)],
+                fc_own.at[:, pl.ds(g * cols, cols)],
+                cut_sems.at[g],
+            )
+            for g in range(count)
+        ]
+    for copy in cuts:
+        copy.start()
     rows = hidden.shape[0] // 2
     halves = [pl.ds(i * rows, rows) for i in range(2)]
     across = [send(hidden.at[half], hidden_out.at[2, half], hid_chip, (i,), chip) for i, half in enumerate(halves)]
@@ -452,7 +486,7 @@
                 (hidden, hidden_out.at[0]),
                 (kv_own, kvw_out.at[f]),
                 (q_own, qw_out.at[f]),
-                (proj_own, proj_out.at[f]),
+                (cot, cot_out.at[0]),
             )
         )
     ]
@@ -466,9 +500,12 @@
         kvw.arrived(step - 1)
         kvw.start(step)
     qw.start(1)
+    for copy in cuts:
+        copy.wait()
+    fc.start(1)
     kvw.arrived(steps)
     stays[1].wait()
-    load = pltpu.make_async_copy(kvw_out, weights, local.at[4])
+    load = pltpu.make_async_copy(kvw_out, weights, local.at[6])
     load.start()
     load.wait()
     total = jnp.zeros((hidden.shape[0], kvw_out.shape[2]), F32)
@@ -482,7 +519,7 @@
 
     spread = KernelRing(count, mine, kv_out.at[s], kv_sems, owner, up, down)
     spread.start(1)
-    keep = pltpu.make_async_copy(mine, kv_out.at[s, f], local.at[5])
+    keep = pltpu.make_async_copy(mine, kv_out.at[s, f], local.at[7])
     keep.start()
     kv_across, kv_pair = [], []
 
@@ -506,20 +543,29 @@
         else:
             pass_on(kv_out.at[s, owner(steps)], owner(steps))
         if step == 1:
+            moved.arrived()
+            moved.left()
             proj.start(1)
+            cot_across = send(cot, cot_out.at[2], cot_sems, (0,), chip)
+            cot_pair = send(cot, cot_out.at[1], cot_sems, (1,), core)
         else:
             proj.arrived(step - 1)
             proj.start(step)
+        fc.arrived(step)
+        if step < steps:
+            fc.start(step + 1)
     other = lax.rem(s + 2, 4)
     far = []
     for i, (place, copy) in enumerate(kv_across):
         copy.wait_recv()
         slot = kv_out.at[other, place]
         far.append(send(slot, slot, kv_far, (i,), core))
+    cot_across.wait()
+    cot_far = send(cot_out.at[2], cot_out.at[3], cot_sems, (2,), core)
     proj.arrived(steps)
     for ring in rings + [spread]:
         ring.finish()
-    for copy in [keep, stays[0], stays[2], stays[3]]:
+    for copy in [keep, cot_pair, cot_far, stays[0]] + stays[2:]:
         copy.wait()
     for copy in across + [copy for _, copy in kv_across]:
         copy.wait_send()
@@ -527,23 +573,26 @@
         copy.wait()
 
 
-def opening(hidden, kv_own, q_own, proj_own, fsdp_count, shard):
+def opening(hidden, kv_own, qkv_weight, proj_weight, fc_weight, cot, fsdp_count, q_cols):
     count, width = hidden.shape
+    shard = qkv_weight.shape[0]
     dma = pltpu.SemaphoreType.DMA
     ring = dma((2, 2, fsdp_count // 2))
-    anywhere = pl.BlockSpec(memory_space=pl.ANY)
+    anywhere = pl.BlockSpec(memory_space=pltpu.HBM)
     inside = pl.BlockSpec(memory_space=pltpu.VMEM)
     return pl.pallas_call(
         functools.partial(opening_kernel, count=fsdp_count, shard=shard),
         out_shape=(
             jax.ShapeDtypeStruct((4,) + hidden.shape, BF),
             jax.ShapeDtypeStruct((fsdp_count,) + kv_own.shape, BF),
-            jax.ShapeDtypeStruct((fsdp_count,) + q_own.shape, BF),
-            jax.ShapeDtypeStruct((fsdp_count,) + proj_own.shape, BF),
+            jax.ShapeDtypeStruct((fsdp_count, shard, q_cols), BF),
+            jax.ShapeDtypeStruct((fsdp_count, shard // 4, width), BF),
             jax.ShapeDtypeStruct((4, fsdp_count, count, 2 * HD), BF),
+            jax.ShapeDtypeStruct((fsdp_count, shard, width), BF),
+            jax.ShapeDtypeStruct((4,) + hidden.shape, BF),
         ),
-        in_specs=[inside, anywhere, anywhere, anywhere],
-        out_specs=(anywhere,) * 5,
+        in_specs=[inside] + [anywhere] * 5,
+        out_specs=(anywhere,) * 7,
         scratch_shapes=[
             pltpu.VMEM((fsdp_count,) + kv_own.shape, BF),
             pltpu.VMEM((count, 2 * HD), BF),
@@ -556,52 +605,18 @@
             dma((2, fsdp_count)),
             dma((2, fsdp_count)),
             dma((2, fsdp_count)),
-            dma((6,)),
+            ring,
+            dma((2, 3)),
+            dma((3,)),
+            dma((fsdp_count,)),
+            dma((8,)),
         ],
         compiler_params=pltpu.CompilerParams(
             collective_id=1, has_side_effects=True, vmem_limit_bytes=40 << 20
         ),
         cost_estimate=COST,
         name="opening",
-    )(hidden, kv_own, q_own, proj_own)
-
-
-def pack_kernel(place, fc_ref, down_ref, own_ref, all_ref):
-    rows = fc_ref.shape[0]
-    own_ref[:rows] = fc_ref[...]
-    own_ref[rows:] = down_ref[...]
-    all_ref[0] = own_ref[...]
-
-
-def pack(place, fc_weight, down_weight, parts, quarter):
-    rows, width = fc_weight.shape[0], down_weight.shape[1]
-    if quarter % 128:
-        fc_own = lax.dynamic_slice_in_dim(fc_weight.reshape(rows, parts, 4, quarter), place[0], 1, 2)
-        down_own = lax.dynamic_slice_in_dim(down_weight, place[0] * quarter, quarter, 0)
-        own = jnp.concatenate([fc_own.reshape(rows, parts * quarter), down_own], axis=0)
-        return own, lax.dynamic_update_slice(jnp.zeros((parts,) + own.shape, BF), own[None], (place[1], 0, 0))
-    return pl.pallas_call(
-        pack_kernel,
-        out_shape=(
-            jax.ShapeDtypeStruct((rows + quarter, width), BF),
-            jax.ShapeDtypeStruct((parts, rows + quarter, width), BF),
-        ),
-        grid_spec=pltpu.PrefetchScalarGridSpec(
-            num_scalar_prefetch=1,
-            grid=(parts,),
-            in_specs=[
-                pl.BlockSpec((rows, quarter), lambda g, p: (0, g * 4 + p[0])),
-                pl.BlockSpec((quarter, quarter), lambda g, p: (p[0], g)),
-            ],
-            out_specs=(
-                pl.BlockSpec((rows + quarter, quarter), lambda g, p: (0, g)),
-                pl.BlockSpec((1, rows + quarter, quarter), lambda g, p: (p[1], 0, g)),
-            ),
-        ),
-        compiler_params=pltpu.CompilerParams(vmem_limit_bytes=30 << 20),
-        cost_estimate=COST,
-        name="pack",
-    )(place, fc_weight, down_weight)
+    )(hidden, kv_own, qkv_weight, proj_weight, fc_weight, cot)
 
 
 GELU_A = math.sqrt(2 / math.pi)
@@ -635,9 +650,10 @@
         grad_ref[...] = total[...].astype(BF)
 
 
-def middle(rows, cot, weights, shard, tile):
+def middle(rows, cot, fc_all, down_all, tile):
     count, width = rows.shape
-    parts, quarter = weights.shape[0], weights.shape[1] - shard
+    parts, shard = fc_all.shape[:2]
+    quarter = down_all.shape[1]
     hidden = parts * quarter
     per = tile // quarter
     whole = pl.BlockSpec((count, width), lambda n: (0, 0), pipeline_mode=pl.Buffered(1))
@@ -654,68 +670,380 @@
             whole,
             whole,
             pl.BlockSpec((parts, shard, tile), lambda n: (0, 0, n)),
-            pl.BlockSpec((per, quarter, width), lambda n: (n, 1, 0)),
+            pl.BlockSpec((per, quarter, width), lambda n: (n, 0, 0)),
         ],
         out_specs=(cols, cols, pl.BlockSpec((count, width), lambda n: (0, 0))),
         scratch_shapes=[pltpu.VMEM((count, width), F32)],
         compiler_params=pltpu.CompilerParams(vmem_limit_bytes=60 << 20),
         cost_estimate=COST,
         name="middle",
-    )(rows, cot, weights, weights)
-
-
-def turned_kernel(order, left_ref, right_ref, left_two_ref, right_two_ref, out_ref):
-    rows = left_ref.shape[1]
-    out_ref[0, :rows] = dot_rows(left_ref[...], right_ref[...]).astype(BF)
-    out_ref[0, rows:] = dot_rows(left_two_ref[...], right_two_ref[...]).astype(BF)
-
-
-def turned(order, left, right, left_two, right_two, shard):
-    count, width = right.shape
-    chunks = order.shape[0]
-    if shard % 128:
-        one = dot_rows(left, right).astype(BF).reshape(-1, shard, width)
-        two = dot_rows(left_two, right_two).astype(BF).reshape(-1, shard, width)
-        both = jnp.concatenate([one, two], axis=1)
-        return jnp.stack([lax.dynamic_index_in_dim(both, order[i], 0, False) for i in range(chunks)])
-    whole = pl.BlockSpec((count, width), lambda n, o: (0, 0), pipeline_mode=pl.Buffered(1))
-    cols = pl.BlockSpec((count, shard), lambda n, o: (0, o[n]))
+    )(rows, cot, fc_all, down_all)
+
+
+def bridge_kernel(
+    heads,
+    proj,
+    hidden,
+    vectors,
+    down_own,
+    mlp_out,
+    resid_out,
+    down_out,
+    far_out,
+    far,
+    near_out,
+    near,
+    chip_in,
+    mine,
+    pair_sems,
+    chip_sems,
+    spread_chip,
+    spread_core,
+    down_sems,
+    local,
+    *,
+    count,
+):
+    s, f, owner, up, down, chip, core = neighbours(count)
+    greet(up, down, chip, core)
+    steps = count // 2
+    tokens = hidden.shape[0]
+    ring = KernelRing(count, down_own, down_out, down_sems, owner, up, down)
+    ring.start(1)
+    stays = [
+        pltpu.make_async_copy(down_own, down_out.at[f], local.at[0]),
+    ]
+    for copy in stays:
+        copy.start()
+
+    def part(i):
+        return dot_plain(heads[i * tokens : (i + 1) * tokens], proj[...])
+
+    far_out[...] = part(3).astype(BF)
+    pairs = [send(far_out, far, pair_sems, (0,), core)]
+    near_out[...] = part(1).astype(BF)
+    pairs.append(send(near_out, near, pair_sems, (1,), core))
+    middle = part(2)
+    pairs[0].wait()
+    far_out[...] = (middle + far[...].astype(F32)).astype(BF)
+    rows = tokens // 2
+    halves = [pl.ds(i * rows, rows) for i in range(2)]
+    across = [send(far_out.at[half], chip_in.at[half], chip_sems, (i,), chip) for i, half in enumerate(halves)]
+    resid_out[...] = hidden[...].astype(F32) + part(0)
+    pairs[1].wait()
+    resid_out[...] += near[...].astype(F32)
+    spread, spread_pair = [], []
+    block = 64
+    for i, half in enumerate(halves):
+        across[i].wait_recv()
+        for at in range(i * rows, (i + 1) * rows, block):
+            here = slice(at, at + block)
+            resid = resid_out[here] + chip_in[here].astype(F32)
+            resid_out[here] = resid
+            normed, _ = layer_norm(resid)
+            mine[here] = (normed * vectors[0:1] + vectors[1:2]).astype(BF)
+        spread.append(send(mine.at[half], mlp_out.at[2, half], spread_chip, (i,), chip))
+        spread_pair.append(send(mine.at[half], mlp_out.at[1, half], spread_core, (i,), core))
+        ring.arrived(i + 1)
+        ring.start(i + 2)
+    stays.append(pltpu.make_async_copy(mine, mlp_out.at[0], local.at[1]))
+    stays[-1].start()
+    for i, half in enumerate(halves):
+        spread[i].wait_recv()
+        spread_pair.append(send(mlp_out.at[2, half], mlp_out.at[3, half], spread_core, (2 + i,), core))
+    for step in range(3, steps + 1):
+        ring.arrived(step)
+        if step < steps:
+            ring.start(step + 1)
+    ring.finish()
+    for copy in across + spread:
+        copy.wait_send()
+    for copy in spread_pair + stays:
+        copy.wait()
+
+
+def bridge(heads, proj, hidden, vectors, down_own, fsdp_count):
+    tokens, width = hidden.shape
+    quarter = down_own.shape[0]
+    dma = pltpu.SemaphoreType.DMA
+    anywhere = pl.BlockSpec(memory_space=pltpu.HBM)
+    inside = pl.BlockSpec(memory_space=pltpu.VMEM)
+    wide = pltpu.VMEM((tokens, width), BF)
     return pl.pallas_call(
-        turned_kernel,
-        out_shape=jax.ShapeDtypeStruct((chunks, 2 * shard, width), BF),
-        grid_spec=pltpu.PrefetchScalarGridSpec(
-            num_scalar_prefetch=1,
-            grid=(chunks,),
-            in_specs=[cols, whole, cols, whole],
-            out_specs=pl.BlockSpec((1, 2 * shard, width), lambda n, o: (n, 0, 0)),
+        functools.partial(bridge_kernel, count=fsdp_count),
+        out_shape=(
+            jax.ShapeDtypeStruct((4, tokens, width), BF),
+            jax.ShapeDtypeStruct((tokens, width), F32),
+            jax.ShapeDtypeStruct((fsdp_count, quarter, width), BF),
         ),
-        compiler_params=pltpu.CompilerParams(vmem_limit_bytes=60 << 20),
+        in_specs=[inside] * 4 + [anywhere],
+        out_specs=(anywhere, inside, anywhere),
+        scratch_shapes=[wide] * 6
+        + [
+            dma((2, 2)),
+            dma((2, 2)),
+            dma((2, 2)),
+            dma((2, 4)),
+            dma((2, 2, fsdp_count // 2)),
+            dma((4,)),
+        ],
+        compiler_params=pltpu.CompilerParams(
+            collective_id=3, has_side_effects=True, vmem_limit_bytes=40 << 20
+        ),
         cost_estimate=COST,
-        name="turned",
-    )(order, left, right, left_two, right_two)
-
-
-def lower_kernel(rows_ref, down_ref, out_ref):
-    down = down_ref[...].reshape(-1, down_ref.shape[2])
-    out_ref[...] = dot_plain(rows_ref[...], down).astype(BF)
-
-
-def lower(rows, weights, shard, tile):
-    count = rows.shape[0]
-    parts, quarter, width = weights.shape[0], weights.shape[1] - shard, weights.shape[2]
+        name="bridge",
+    )(heads, proj, hidden, vectors, down_own)
+
+
+def feedback_kernel(
+    parts,
+    mlp_in,
+    pre_grad,
+    activ,
+    cot,
+    down_all,
+    resid,
+    gain,
+    branch_out,
+    result_out,
+    resid_out,
+    vectors_out,
+    up_out,
+    down_out,
+    rest_out,
+    mlp_here,
+    pre_here,
+    activ_here,
+    cot_here,
+    here,
+    across_out,
+    far,
+    near,
+    chip_in,
+    branch,
+    outs_first,
+    ins_first,
+    outs_next,
+    ins_next,
+    stage,
+    down_here,
+    low_here,
+    low_far,
+    low_near,
+    low_chip,
+    branch_low,
+    pair_sems,
+    chip_sems,
+    spread_chip,
+    spread_core,
+    ring_sems,
+    low_pair,
+    low_across,
+    local,
+    *,
+    count,
+    shard,
+    turned,
+):
+    s, f, owner, up, down, chip, core = neighbours(count)
+    greet(up, down, chip, core)
+    steps = count // 2
+    tokens, width = resid.shape
+    pairs = [send(parts.at[3], far, pair_sems, (0,), core), send(parts.at[1], near, pair_sems, (1,), core)]
+    loads = [
+        pltpu.make_async_copy(source, target, local.at[i])
+        for i, (source, target) in enumerate(
+            (
+                (pre_grad, pre_here),
+                (mlp_in, mlp_here),
+                (parts.at[2], across_out),
+                (cot, cot_here),
+                (activ, activ_here),
+                (parts.at[0], here),
+            )
+        )
+    ]
+    for copy in loads:
+        copy.start()
+
+    def product(left, right, place, out):
+        start = pl.multiple_of(place * shard, shard)
+        chosen = left[:, pl.ds(start, shard)] if turned else left[pl.ds(start, shard), :]
+        for at in range(0, width, 512):
+            cols = slice(at, at + 512)
+            value = dot_rows(chosen, right[:, cols]) if turned else dot_plain(chosen, right[:, cols])
+            out[:, cols] = value.astype(BF)
+
+    def chunk(place, out):
+        product(mlp_here, pre_here, place, out.at[pl.ds(0, shard)])
+        product(activ_here, cot_here, place, out.at[pl.ds(shard, shard)])
+
+    def low_part(j, down):
+        lines = slice(j * tokens, (j + 1) * tokens)
+        return dot_plain(activ_here[lines], down) if turned else dot_rows(activ_here[:, lines], down)
+
+    upper, under = pl.ds(0, shard), pl.ds(shard, shard)
+    devices = (up, down)
+    side = width // 2
+    sides = [
+        pltpu.make_async_copy(down_all.at[:, :, pl.ds(i * side, side)], down_here, local.at[10 + i])
+        for i in range(2)
+    ]
+    sides[0].start()
+    loads[0].wait()
+    loads[1].wait()
+    product(mlp_here, pre_here, owner(steps), outs_first.at[upper])
+    first = [send(outs_first.at[upper], ins_first.at[upper], ring_sems, (0, 0), up)]
+    loads[2].wait()
+    pairs[0].wait_recv()
+    across_out[...] = (across_out[...].astype(F32) + far[...].astype(F32)).astype(BF)
+    rows = tokens // 2
+    halves = [pl.ds(i * rows, rows) for i in range(2)]
+    across = [send(across_out.at[half], chip_in.at[half], chip_sems, (i,), chip) for i, half in enumerate(halves)]
+    loads[3].wait()
+    loads[4].wait()
+    product(activ_here, cot_here, owner(steps), outs_first.at[under])
+    first.append(send(outs_first.at[under], ins_first.at[under], ring_sems, (1, 0), down))
+    chunk(owner(steps - 1), outs_next.at[0])
+    chunk(owner(1 - steps), outs_next.at[1])
+    second = []
+    for way, part in enumerate((upper, under)):
+        first[way].wait_recv()
+        out = outs_next.at[way]
+        out[part] = (out[part].astype(F32) + ins_first[part].astype(F32)).astype(BF)
+        second.append(send(out, ins_next.at[way], ring_sems, (way, 1), devices[way]))
+
+    loads[5].wait()
+    pairs[1].wait_recv()
+    gain_grad = jnp.zeros((1, width), F32)
+    bias_grad = jnp.zeros((1, width), F32)
+    spread, spread_pair = [], []
+    block = 64
+    for i, half in enumerate(halves):
+        across[i].wait_recv()
+        for at in range(i * rows, (i + 1) * rows, block):
+            part = slice(at, at + block)
+            grad = here[part].astype(F32) + near[part].astype(F32) + chip_in[part].astype(F32)
+            normed, inverse = layer_norm(resid[part])
+            gain_grad += jnp.sum(grad * normed, axis=0, keepdims=True)
+            bias_grad += jnp.sum(grad, axis=0, keepdims=True)
+            value = cot_here[part].astype(F32) + norm_back(grad * gain[...], normed, inverse)
+            resid_out[part] = value
+            branch[part] = value.astype(BF)
+        spread.append(send(branch.at[half], branch_out.at[2, half], spread_chip, (i,), chip))
+        spread_pair.append(send(branch.at[half], branch_out.at[1, half], spread_core, (i,), core))
+    vectors_out[0:1] = gain_grad
+    vectors_out[1:2] = bias_grad
+    keep = pltpu.make_async_copy(branch, branch_out.at[0], local.at[6])
+    keep.start()
+
+    for copy in across:
+        copy.wait_send()
+    lows = (low_here, here, across_out, branch_low)
+    for i in range(2):
+        cols = pl.ds(i * side, side)
+        sides[i].wait()
+        down = down_here[...].reshape(-1, side)
+        for j in (3, 1, 2, 0):
+            value = low_part(j, down)
+            lows[j][:, cols] = value if j == 0 else value.astype(BF)
+        if i == 0:
+            sides[1].start()
+    low_sends = [send(lows[3], low_far, low_pair, (0,), core), send(lows[1], low_near, low_pair, (1,), core)]
+    low_sends[0].wait()
+    across_out[...] = (across_out[...].astype(F32) + low_far[...].astype(F32)).astype(BF)
+    low_chip_copy = send(across_out, low_chip, low_across, (0,), chip)
+
+    def rest(i, carry):
+        back = lax.rem(i + 1, 2)
+        n = (steps - (i + 1) // 2) * (1 - 2 * back)
+        chunk(owner(n), stage)
+        copy = pltpu.make_async_copy(stage, rest_out.at[i - 5], local.at[7])
+        copy.start()
+        copy.wait()
+        return carry
+
+    lax.fori_loop(5, count, rest, 0)
+    for i, half in enumerate(halves):
+        spread[i].wait_recv()
+        spread_pair.append(send(branch_out.at[2, half], branch_out.at[3, half], spread_core, (2 + i,), core))
+    leaving = []
+    low_sends[1].wait()
+    low_chip_copy.wait()
+    for at in range(0, tokens, block):
+        part = slice(at, at + block)
+        value = resid[part] + low_here[part] + low_near[part].astype(F32) + low_chip[part].astype(F32)
+        result_out[part] = value.astype(BF)
+    for way, target in enumerate((up_out, down_out)):
+        out = stage if way == 0 else outs_first
+        if way:
+            first[0].wait_send()
+            first[1].wait_send()
+        chunk(owner((steps - 2) * (1 - 2 * way)), out)
+        second[way].wait_recv()
+        out[...] = (out[...].astype(F32) + ins_next[way].astype(F32)).astype(BF)
+        leaving.append(pltpu.make_async_copy(out, target, local.at[8 + way]))
+        leaving[way].start()
+    for copy in pairs + spread + second:
+        copy.wait_send()
+    for copy in spread_pair + leaving + [keep]:
+        copy.wait()
+
+
+def feedback(parts, mlp_in, pre_grad, activ, cot, down_all, resid, gain, fsdp_count, shard):
+    tokens, width = resid.shape
+    turned = shard % 128 == 0
+    if not turned:
+        mlp_in, activ = mlp_in.T, activ.T
+    dma = pltpu.SemaphoreType.DMA
+    anywhere = pl.BlockSpec(memory_space=pltpu.HBM)
+    inside = pl.BlockSpec(memory_space=pltpu.VMEM)
+    wide = pltpu.VMEM((tokens, width), BF)
+    both = pltpu.VMEM((2 * shard, width), BF)
+    quarter = down_all.shape[1]
+    flow = jax.ShapeDtypeStruct((2 * shard, width), BF)
     return pl.pallas_call(
-        lower_kernel,
-        out_shape=jax.ShapeDtypeStruct((count, width), BF),
-        grid=(width // tile,),
-        in_specs=[
-            pl.BlockSpec(rows.shape, lambda n: (0, 0), pipeline_mode=pl.Buffered(1)),
-            pl.BlockSpec((parts, quarter, tile), lambda n: (0, 1, n)),
+        functools.partial(feedback_kernel, count=fsdp_count, shard=shard, turned=turned),
+        out_shape=(
+            jax.ShapeDtypeStruct((4, tokens, width), BF),
+            jax.ShapeDtypeStruct((tokens, width), BF),
+            jax.ShapeDtypeStruct((tokens, width), F32),
+            jax.ShapeDtypeStruct((2, width), F32),
+            flow,
+            flow,
+            jax.ShapeDtypeStruct((fsdp_count - 5, 2 * shard, width), BF),
+        ),
+        in_specs=[anywhere] * 6 + [inside] * 2,
+        out_specs=(anywhere, inside, inside, inside, anywhere, anywhere, anywhere),
+        scratch_shapes=[pltpu.VMEM(value.shape, BF) for value in (mlp_in, pre_grad, activ, cot)]
+        + [wide] * 6
+        + [
+            both,
+            both,
+            pltpu.VMEM((2, 2 * shard, width), BF),
+            pltpu.VMEM((2, 2 * shard, width), BF),
+            both,
+            pltpu.VMEM((fsdp_count, quarter, width // 2), BF),
+            pltpu.VMEM((tokens, width), F32),
+            wide,
+            wide,
+            wide,
+            wide,
+            dma((2, 2)),
+            dma((2, 2)),
+            dma((2, 2)),
+            dma((2, 4)),
+            dma((2, 2, 2)),
+            dma((2, 2)),
+            dma((2, 1)),
+            dma((12,)),
         ],
-        out_specs=pl.BlockSpec((count, tile), lambda n: (0, n)),
-        compiler_params=pltpu.CompilerParams(vmem_limit_bytes=60 << 20),
+        compiler_params=pltpu.CompilerParams(
+            collective_id=4, has_side_effects=True, vmem_limit_bytes=61 << 20
+        ),
         cost_estimate=COST,
-        name="lower",
-    )(rows, weights)
+        name="feedback",
+    )(parts, mlp_in, pre_grad, activ, cot, down_all, resid, gain)
 
 
 class KernelScatter:
@@ -765,14 +1093,15 @@
     attn_parts,
     ff_up,
     ff_down,
-    ff_last,
+    ff_rest,
     resid_grad,
     hidden,
     kv_weight,
     attn_in,
     mlp_vectors,
     grad_out,
-    attn_out,
+    q_out,
+    proj_out,
     ff_out,
     tail_out,
     kv_here,
@@ -787,6 +1116,8 @@
     q_chip_in,
     q_here,
     attn_here,
+    attn_own,
+    proj_here,
     attn_outs,
     attn_ins,
     ff_here,
@@ -810,6 +1141,9 @@
     ff_core_sems,
     tail_sems,
     swap_sems,
+    q_spread_sems,
+    proj_spread_sems,
+    move_sems,
     *,
     count,
     shard,
@@ -820,7 +1154,10 @@
     other, sibling = lax.rem(s + 2, 4), core[0]
     far = lax.rem(sibling + 2, 4)
     tokens = hidden.shape[0]
-    greet(up, down, chip, core)
+    per = count // 4
+    target = (lax.rem(f, 4), s * per + f // 4)
+    source = (f // per, 4 * lax.rem(f, per) + s)
+    greet_also((up, down, chip, core), (source,), met(target, s, f).astype(jnp.int32), s, f)
 
     kv_pair = [
         send(kv_parts.at[far], kv_far, kv_core_sems, (0,), core),
@@ -830,11 +1167,11 @@
         pltpu.make_async_copy(kv_parts.at[other], kv_here.at[1], local.at[0]),
         pltpu.make_async_copy(kv_parts.at[s], kv_here.at[0], local.at[1]),
         pltpu.make_async_copy(attn_parts, attn_here, local.at[2]),
-        pltpu.make_async_copy(ff_last, ff_here, local.at[3]),
+        pltpu.make_async_copy(ff_rest.at[ff_rest.shape[0] - 1], ff_here, local.at[3]),
     ]
     for copy in loads:
         copy.start()
-    ff_rows = ff_last.shape[0] // 2
+    ff_rows = ff_here.shape[0] // 2
     ff_parts = [pl.ds(i * ff_rows, ff_rows) for i in range(2)]
     ff_ring = []
 
@@ -878,21 +1215,24 @@
         here = kv_here[0, place].astype(F32) + kv_near[place].astype(F32)
         return here + kv_chip_in[order.index(n)].astype(F32)
 
+    loads[2].wait()
+
+    def attn_chunk(n):
+        return attn_here[order.index(steps if n == -steps else n)].astype(F32)
+
     kv = KernelScatter(count, kv_chunk, kv_outs, kv_ins, kv_sems, up, down)
+    attn = KernelScatter(count, attn_chunk, attn_outs, attn_ins, attn_sems, up, down)
     for step in range(steps):
-        for n in {steps - step, -(steps - step)} & set(order):
-            kv_across[n].wait_recv()
+        for n in (steps - step, step - steps):
+            if n in order:
+                kv_across[n].wait_recv()
         if step:
             kv.arrived(step - 1)
         kv.start(step)
+        if step:
+            attn.arrived(step - 1)
+        attn.start(step)
     ff_start(1)
-    loads[2].wait()
-
-    def attn_chunk(n):
-        return attn_here[order.index(steps if n == -steps else n)].astype(F32)
-
-    attn = KernelScatter(count, attn_chunk, attn_outs, attn_ins, attn_sems, up, down)
-    attn.start(0)
 
     loads[3].wait()
     ff_pair, ff_across = [], []
@@ -910,6 +1250,31 @@
     kv_across[0].wait_recv()
     kv.arrived(steps - 1)
     kv_total[...] = kv.total().astype(BF)
+
+    attn.arrived(steps - 1)
+    attn_own[...] = attn.total().astype(BF)
+    part = proj_out.shape[1]
+    lines = pl.ds(part, attn_own.shape[0] - part)
+    q_lines = attn_own.at[lines]
+    q_spread = [
+        send(q_lines, q_out.at[2], q_spread_sems, (0,), chip),
+        send(q_lines, q_out.at[1], q_spread_sems, (1,), core),
+    ]
+    q_keep = pltpu.make_async_copy(q_lines, q_out.at[0], local.at[5])
+    q_keep.start()
+    moved = Maybe(
+        attn_own.at[pl.ds(0, part)],
+        proj_here,
+        proj_here,
+        move_sems.at[0],
+        move_sems.at[1],
+        move_sems.at[1],
+        move_sems.at[2],
+        target,
+        source,
+        s,
+        f,
+    )
 
     q_pair[1].wait()
     for copy in q_across:
@@ -944,10 +1309,18 @@
         tail.start(step)
         if step == 0:
             ff_close(1)
-        attn.arrived(step)
-        if step < steps - 1:
-            attn.start(step + 1)
-    attn_out[...] = attn.total().astype(BF)
+            q_spread[0].wait_recv()
+            q_spread.append(send(q_out.at[2], q_out.at[3], q_spread_sems, (2,), core))
+            moved.arrived()
+            moved.left()
+            proj_spread = [
+                send(proj_here, proj_out.at[2], proj_spread_sems, (0,), chip),
+                send(proj_here, proj_out.at[1], proj_spread_sems, (1,), core),
+            ]
+            proj_keep = pltpu.make_async_copy(proj_here, proj_out.at[0], local.at[6])
+            proj_keep.start()
+    proj_spread[0].wait_recv()
+    proj_spread.append(send(proj_out.at[2], proj_out.at[3], proj_spread_sems, (2,), core))
     tail.arrived(steps - 1)
     total = tail.total()
     swap_out[0] = total.astype(BF)
@@ -963,6 +1336,12 @@
     swaps[1].wait_recv()
     tail_out[...] = swap_out[1].astype(F32) + swap_in[1].astype(F32)
     keep.wait()
+    q_keep.wait()
+    proj_keep.wait()
+    q_spread[0].wait_send()
+    proj_spread[0].wait_send()
+    for copy in q_spread[1:] + proj_spread[1:]:
+        copy.wait()
     for ring in (kv, attn, tail):
         ring.finish()
     for copy in kv_pair + q_across + list(kv_across.values()) + ff_ring + ff_across + swaps:
@@ -972,14 +1351,15 @@
 
 
 def closing(kv_parts, query_rows, q_weight, attn_parts, ff_flow, resid_grad, hidden, kv_weight, attn_in, mlp_vectors, shard):
-    ff_up, ff_down, ff_last = ff_flow
+    ff_up, ff_down, ff_rest = ff_flow
     fsdp_count, tokens, kv_cols = kv_parts.shape[1:]
     width = hidden.shape[1]
     steps = fsdp_count // 2
     dma = pltpu.SemaphoreType.DMA
-    anywhere = pl.BlockSpec(memory_space=pl.ANY)
+    anywhere = pl.BlockSpec(memory_space=pltpu.HBM)
     inside = pl.BlockSpec(memory_space=pltpu.VMEM)
     attn_shape = attn_parts.shape[1:]
+    part = shard // 4
     tail_shape = kv_weight.shape[1:]
     wide = pltpu.VMEM((tokens, width), BF)
     kv_all = pltpu.VMEM((fsdp_count, tokens, kv_cols), BF)
@@ -995,12 +1375,13 @@
         functools.partial(closing_kernel, count=fsdp_count, shard=shard),
         out_shape=(
             jax.ShapeDtypeStruct((tokens, width), BF),
-            jax.ShapeDtypeStruct(attn_shape, BF),
-            jax.ShapeDtypeStruct((4,) + ff_last.shape, BF),
+            jax.ShapeDtypeStruct((4, attn_shape[0] - part, width), BF),
+            jax.ShapeDtypeStruct((4, part, width), BF),
+            jax.ShapeDtypeStruct((4,) + ff_up.shape, BF),
             jax.ShapeDtypeStruct(tail_shape, F32),
         ),
         in_specs=[anywhere, inside, inside, anywhere, anywhere, anywhere, anywhere] + [inside] * 5,
-        out_specs=(inside, inside, anywhere, inside),
+        out_specs=(inside, anywhere, anywhere, anywhere, inside),
         scratch_shapes=[
             pltpu.VMEM((2, fsdp_count, tokens, kv_cols), BF),
             kv_all,
@@ -1014,18 +1395,20 @@
             wide,
             pltpu.VMEM((tokens, width), F32),
             pltpu.VMEM(attn_parts.shape, BF),
+            pltpu.VMEM(attn_shape, BF),
+            pltpu.VMEM((part, width), BF),
             pair(attn_shape),
             ring(attn_shape),
-            pltpu.VMEM(ff_last.shape, BF),
-            pltpu.VMEM((2,) + ff_last.shape, BF),
-            pltpu.VMEM(ff_last.shape, BF),
+            pltpu.VMEM(ff_up.shape, BF),
+            pltpu.VMEM((2,) + ff_up.shape, BF),
+            pltpu.VMEM(ff_up.shape, BF),
             pltpu.VMEM((tokens, kv_cols), BF),
             pltpu.VMEM((fsdp_count,) + tail_shape, F32),
             pair(tail_shape),
             ring(tail_shape),
             pltpu.VMEM((2,) + tail_shape, BF),
             pltpu.VMEM((2,) + tail_shape, BF),
-            dma((5,)),
+            dma((7,)),
             dma((2, 2)),
             dma((2, fsdp_count)),
             ring_sems,
@@ -1037,6 +1420,9 @@
             dma((2, 4)),
             ring_sems,
             dma((2, 2)),
+            dma((2, 3)),
+            dma((2, 3)),
+            dma((3,)),
         ],
         compiler_params=pltpu.CompilerParams(
             collective_id=2, has_side_effects=True, vmem_limit_bytes=61 << 20
@@ -1050,7 +1436,7 @@
         attn_parts,
         ff_up,
         ff_down,
-        ff_last,
+        ff_rest,
         resid_grad,
         hidden,
         kv_weight,
@@ -1121,6 +1507,31 @@
         cost_estimate=COST,
         name="stack_rows",
     )(place, *pieces)
+
+
+def qkv_kernel(place, q_ref, tail_ref, out_ref):
+    _, lines, width = q_ref.shape
+    rows = out_ref.shape[0]
+    folds = rows // lines
+    cols = width // folds
+    for i in range(q_ref.shape[0]):
+        start = pl.multiple_of((place[0] ^ i) * cols, cols)
+        for k in range(folds):
+            part = q_ref[i, :, k * cols : (k + 1) * cols].astype(F32)
+            out_ref[k * lines : (k + 1) * lines, pl.ds(start, cols)] = part
+    out_ref[:, width:] = tail_ref[:rows, : out_ref.shape[1] - width]
+
+
+def place_qkv(place, q_pieces, tail, rows, cols):
+    return pl.pallas_call(
+        qkv_kernel,
+        out_shape=jax.ShapeDtypeStruct((rows, cols), F32),
+        in_specs=[pl.BlockSpec(memory_space=pltpu.SMEM)] + [pl.BlockSpec(memory_space=pltpu.VMEM)] * 2,
+        out_specs=pl.BlockSpec(memory_space=pltpu.VMEM),
+        compiler_params=pltpu.CompilerParams(vmem_limit_bytes=30 << 20),
+        cost_estimate=COST,
+        name="place_qkv",
+    )(place, q_pieces, tail)
 
 
 def cols_kernel(place, *refs):
@@ -1222,28 +1633,23 @@
     ).reshape(-1)
 
     place = jnp.stack([s, f]).astype(jnp.int32)
-    ff_own, ff_slots = pack(place, fc_weight, down_weight, fsdp_count, quarter)
-    flow = Flow(ring, ring.gather(ff_own, ff_slots))
-
     part = shard // seq_count
-    pairs = [
-        (j * fsdp_count + q * (fsdp_count // seq_count) + t // seq_count, q * fsdp_count + t)
-        for q in range(seq_count)
-        for t in range(fsdp_count)
-        for j in [t % seq_count]
-    ]
-    back_pairs = [(b, a) for a, b in pairs]
-    own_proj = lax.ppermute(
-        lax.dynamic_slice_in_dim(proj_weight, s * part, part, 0), ("seq", "fsdp"), pairs
-    )
+    down_own = lax.dynamic_slice_in_dim(down_weight, s * quarter, quarter, 0)
+    if quarter % 128:
+        fc_weight = lax.dynamic_slice_in_dim(
+            fc_weight.reshape(shard, fsdp_count, seq_count, quarter), s, 1, 2
+        ).reshape(shard, fsdp_count * quarter)
 
     span = 32
     vectors = jnp.stack([norm_gain, norm_bias, mlp_gain, mlp_bias])
     padded = jnp.pad(vectors, ((0, span - 4), (0, 2 * HD - shard)))
     own_kv = jnp.concatenate([qkv_weight[:, width:], padded], axis=0)
-    own_q = lax.dynamic_slice_in_dim(qkv_weight, s * head_cols, head_cols, 1)
-    opened = opening(hidden_in.reshape(tokens_here, width), own_kv, own_q, own_proj, fsdp_count, shard)
-    hidden_all, kv_ring, q_ring, proj_ring, kv_all = flow.advance(opened)
+    hidden_own = hidden_in.reshape(tokens_here, width)
+    cotangent = out_cotangent.reshape(tokens_here, width)
+    hidden_all, kv_ring, q_ring, proj_ring, kv_all, fc_all, cotangent_all = opening(
+        hidden_own, own_kv, qkv_weight, proj_weight, fc_weight, cotangent, fsdp_count, head_cols
+    )
+    cotangent_all = cotangent_all.reshape(group, width)
     kv_weight = kv_ring[:, :shard].reshape(width, 2 * HD)
     vectors = kv_ring[:, shard : shard + 4, :shard].transpose(1, 0, 2).reshape(4, width).astype(F32)
     gain_one, bias_one, gain_two, bias_two = vectors[0], vectors[1], vectors[2], vectors[3]
@@ -1254,81 +1660,58 @@
     attn_in = (normed_all * gain_one + bias_one).astype(BF)
     own_attn_in = attn_in[:tokens_here]
     queries = dot_plain(attn_in, q_weight).astype(BF).reshape(seq_count, MB, count, head_cols)
-    cotangent = out_cotangent.reshape(tokens_here, width)
-    cotangent_all = jnp.concatenate(seq_gather(tie(cotangent, queries)), axis=0)
-
     heads_out, logs = attend(tables, first, queries, kv_all, blocks)
     heads_rows = heads_out.reshape(group, head_cols)
 
-    def pieces(rows):
-        return [rows[i * tokens_here : (i + 1) * tokens_here] for i in range(seq_count)]
-
-    hidden_own = hidden_in.reshape(tokens_here, width).astype(F32)
-    resid = hidden_own + seq_scatter([dot_plain(piece, proj_full) for piece in pieces(heads_rows)])
-    resid, cotangent_all = flow.advance((resid, cotangent_all))
-    normed_two, inverse_two = layer_norm(resid)
-    mlp_in_own = (normed_two * gain_two + bias_two).astype(BF)
-    mlp_in = flow.advance(jnp.concatenate(seq_gather(mlp_in_own), axis=0))
-    weights = flow.finish()
-    activ, pre_grad, mlp_in_part = middle(mlp_in, cotangent_all, weights, shard, BLOCK)
-    mlp_in_grad = seq_scatter([piece.astype(F32) for piece in pieces(mlp_in_part)])
-
-    order = ring.order()
-    early = 3
-    ff_early = turned(order[:early], mlp_in, pre_grad, activ, cotangent_all, shard)
-    ff_late = turned(order[early:], mlp_in, pre_grad, activ, cotangent_all, shard)
+    mlp_in, resid, down_all = bridge(
+        heads_rows, proj_full, hidden_own, vectors[2:], down_own, fsdp_count
+    )
+    mlp_in = mlp_in.reshape(group, width)
+    activ, pre_grad, mlp_in_parts = middle(mlp_in, cotangent_all, fc_all, down_all, 2 * BLOCK)
+    branch, result, resid_grad, mlp_vectors, ff_up, ff_down, ff_rest = feedback(
+        mlp_in_parts.reshape(seq_count, tokens_here, width),
+        mlp_in,
+        pre_grad,
+        activ,
+        cotangent_all,
+        down_all,
+        resid,
+        gain_two[None],
+        fsdp_count,
+        shard,
+    )
+    branch = branch.reshape(group, width)
     steps = ring.steps()
-
-    def ff_chunk(n):
-        at = steps.index(n)
-        return (ff_early[at] if at < early else ff_late[at - early]).astype(F32)
-
-    flow = Flow(ring, ring.scatter(ff_chunk, last=False))
-    mlp_in_grad, ff_late, activ_later = flow.advance((mlp_in_grad, ff_late, activ))
-    lowered = lower(activ_later, weights, shard, BLOCK)
-
-    mlp_gain_part = jnp.sum(mlp_in_grad * normed_two, axis=0)
-    mlp_bias_part = jnp.sum(mlp_in_grad, axis=0)
-    resid_grad = cotangent.astype(F32) + norm_back(mlp_in_grad * gain_two, normed_two, inverse_two)
-    branch_own = resid_grad.astype(BF)
-    branch, lowered = flow.advance((jnp.concatenate(seq_gather(branch_own), axis=0), lowered))
-    result = (resid + seq_scatter([piece.astype(F32) for piece in pieces(lowered)])).astype(BF)
+    flow = Flow(ring, ring.scatter(ff_up, ff_down, lambda n: ff_rest[steps.index(n) - 5]))
     heads_grad = dot_cols(branch, proj_full).astype(BF).reshape(seq_count, MB, count, head_cols)
     query_grads, kv_grads = attend_back(
         tables, first, queries, kv_all, heads_out, logs, heads_grad, blocks
     )
-    query_grads, kv_grads, result = flow.advance((query_grads, kv_grads, result))
+    query_grads, kv_grads = flow.advance((query_grads, kv_grads))
     query_rows = query_grads.reshape(group, head_cols)
 
     proj_sum = dot_rows(heads_rows, branch).astype(BF)
-    attn_parts = attn_turned(order, attn_in, query_rows, proj_sum, shard)
+    attn_parts = attn_turned(ring.order(), attn_in, query_rows, proj_sum, shard)
     ff_up, ff_down = flow.finish()
-    grad_input, attn_grad, ff_all, tail = closing(
+    grad_input, q_pieces, proj_pieces, ff_all, tail = closing(
         kv_grads.reshape(seq_count, fsdp_count, tokens_here, 2 * HD),
         query_rows,
         q_weight,
         attn_parts,
-        (ff_up, ff_down, ff_late[-1]),
+        (ff_up, ff_down, ff_rest),
         resid_grad,
-        hidden_in.reshape(tokens_here, width),
+        hidden_own,
         kv_ring,
         own_attn_in,
-        jnp.stack([mlp_gain_part, mlp_bias_part]),
+        mlp_vectors,
         shard,
     )
-    kv_weight_grad = tail[:shard, : 2 * HD]
     vector_grads = tail[shard : shard + 4, :shard]
-    folds = width // head_cols
-    proj_grad = lax.ppermute(attn_grad[:part], ("seq", "fsdp"), back_pairs)
-    query_weight_grad = (
-        attn_grad[part:].reshape(shard // folds, folds, head_cols).transpose(1, 0, 2).reshape(shard, head_cols)
-    )
     ff_pieces = [ff_all[i] for i in range(seq_count)]
     grad_fc = stack_cols(place, [piece[:shard] for piece in ff_pieces], quarter)
     grad_down = stack_rows(place, [piece[shard:] for piece in ff_pieces], BLOCK)
-    grad_proj = stack_rows(place, seq_gather(proj_grad), BLOCK)
-    grad_query = stack_cols(place, seq_gather(query_weight_grad), head_cols)
-    grad_qkv = jnp.concatenate([grad_query, kv_weight_grad], axis=1)
+    grad_proj = stack_rows(place, [proj_pieces[i] for i in range(seq_count)], width)
+    grad_qkv = place_qkv(place, q_pieces, tail, shard, qkv_weight.shape[1])
     return (
         result.reshape(hidden_in.shape),
         grad_input.reshape(hidden_in.shape),

time: 716 us -> 691 us (0.965)
  Pallas kernels: 408 us -> 601 us
  waiting for transfers between devices: 126 us -> 7.02 us
  other arithmetic: 58.1 us -> 19.4 us
  starting transfers between devices: 39 us -> 2.07 us
  local copies, waits for them, and re-layouts: 52.8 us -> 38.7 us
    pallas_call x4 -> x3, Pallas kernels: 49.3 us -> 192 us  [the longest x1 98.2 us: bridge(): pl.pallas_call(functools.partial(bridge_kernel, count=fsdp_count), out_sh...]
    ppermute x34 -> x0, waiting for transfers between devices: 107 us -> none  [the longest x8 53.8 us: chip_swap(): return lax.ppermute(value, 'seq', [(s, s ^ 2) for s in range(4)])]
    pallas_call x1, Pallas kernels: 132 us -> 169 us  [opening(): pl.pallas_call(functools.partial(opening_kernel, count=fsdp_count, shard=...]
    ppermute x34 -> x0, starting transfers between devices: 32.6 us -> none  [the longest x8 15.3 us: chip_swap(): return lax.ppermute(value, 'seq', [(s, s ^ 2) for s in range(4)])]
    pallas_call x1, Pallas kernels: 121 us -> 144 us  [closing(): pl.pallas_call(functools.partial(closing_kernel, count=fsdp_count, shard=...]
    convert_element_type x7 -> x1, other arithmetic: 26.5 us -> 7.92 us  [scatter(): down = (chunk(-step).astype(F32) + down.astype(F32)).astype(BF)]
    dynamic_update_slice x8 -> x0, local copies, waits for them, and re-layouts: 18.2 us -> none  [put(): lax.dynamic_update_slice(out, piece[None], (owner, row) + (0,) * (value.n...]
    concatenate x6 -> x0, other arithmetic: 13.2 us -> none  [the longest x1 3.88 us: shards(): cotangent_all = jnp.concatenate(seq_gather(tie(cotangent, queries)), axis=0)]
  transfers between devices with their start and end apart: 40 -> 2, of which waited for: 16 -> 2; matrix products, arithmetic and copies ran while one was open for 12% -> 2% of each run, Pallas kernels for 33% -> 3%
where the time goes in v4:
time: 691 us; the launch traced here: 681 us
  Pallas kernels  601 us (87%)
  local copies, waits for them, and re-layouts  38.7 us (6%)
  other arithmetic  19.4 us (3%)
  matrix products  11.2 us (2%)
  waiting for transfers between devices  7.02 us (1%)
    pallas_call x1, Pallas kernels, opening(): pl.pallas_call(functools.partial(opening_kernel, count=fsdp_count, shard=...  169 us
    pallas_call x1, Pallas kernels, closing(): pl.pallas_call(functools.partial(closing_kernel, count=fsdp_count, shard=...  144 us
    pallas_call x1, Pallas kernels, bridge(): pl.pallas_call(functools.partial(bridge_kernel, count=fsdp_count), out_sh...  98.2 us
    pallas_call x1, Pallas kernels, feedback(): pl.pallas_call(functools.partial(feedback_kernel, count=fsdp_count, shard...  91.4 us
    pallas_call x1, Pallas kernels, middle(): pl.pallas_call(functools.partial(middle_kernel, step=256), out_shape=(jax...  39.9 us
    unnamed x66, local copies, waits for them, and re-layouts  25.1 us
    pallas_call x1, Pallas kernels, attend_back(): pl.pallas_call(functools.partial(attend_back_kernel, heads=heads, blocks=...  22.7 us
    pallas_call x1, Pallas kernels, attend(): pl.pallas_call(functools.partial(attend_kernel, heads=heads, blocks=block...  16.2 us
  transfers between devices with their start and end apart: 2, of which 2 were waited for; matrix products, arithmetic and copies ran while one was open for 2% of the time, Pallas kernels for 3%

profile of v4, /device:TPU:0, one launch (start us, length us, event | category | flops | bytes accessed | tf_op | source)
XLA Modules:
  0.0 681.0 jit_solution(2705394503047322067)
XLA Ops:
  9.3 168.7 %opening.1 = (bf16[4,256,2048]{2,1,0:T(8,128)(2,1)S(1)}, bf16[8,288,256]{2,1,0:T(8,128)(2,1)S(1)}, bf16[8,256,512]{2,1,0:T(8,128)(2,1)S(1)}, bf16[8,64,2048]{2,1...) custom-call(bf16[256,2048]{1,0:T(8,128)(2,1)S(1)} %bitcast.115, ...), custom_call_target="tpu_custom_call" | custom-call | tf_op jit(solution)/shard_map/opening/pallas_call | solution.py:583
  178.0 2.0 copy-done
  185.3 3.0 convert_reduce_fusion
  190.0 3.3 add_convert_fusion
  193.3 3.3 convolution_convert_fusion.2
  198.1 2.2 copy-done.4
  201.5 16.2 %attend.1 = (bf16[4,2,128,512]{3,2,1,0:T(8,128)(2,1)S(1)}, f32[4,2,4,128]{3,2,1,0:T(4,128)S(1)}) custom-call(s32[160]{0:T(256)S(1)} %reshape.413.tables, bf16[4,2,128,512]{3,2,1,0:T(8,128)(2,1)S(1)} %bitcast.120, bf16[32,2,128,256]{3,2,1,0:T(8,128)(2,1)S(1)} %bitcast.111, s32[4,2,1,128]{3,2,1,0:T(1,128)S(1)} %add_subtract_fusion.first_ref), custom_call_target="tpu_custom_call" | custom-call | tf_op jit(solution)/shard_map/attend/pallas_call | solution.py:229
  220.3 98.2 %bridge.1 = (bf16[4,256,2048]{2,1,0:T(8,128)(2,1)S(1)}, f32[256,2048]{1,0:T(8,128)S(1)}, bf16[8,256,2048]{2,1,0:T(8,128)(2,1)}) custom-call(bf16[1024,512]{1,0:T(8,128)(2,1)S(1)} %bitcast.117, bf16[512,2048]{1,0:T(8,128)(2,1)S(1)} %bitcast.125, bf16[256,2048]{1,0:T(8,128)(2,1)S(1)} %bitcast.116, f32[2,2048]{1,0:T(2,128)S(1)} %bitcast.129, ...), custom_call_target="tpu_custom_call" | custom-call | tf_op jit(solution)/shard_map/bridge/pallas_call | solution.py:772
  321.8 39.9 %middle.1 = (bf16[1024,2048]{1,0:T(8,128)(2,1)}, bf16[1024,2048]{1,0:T(8,128)(2,1)}, bf16[1024,2048]{1,0:T(8,128)(2,1)}) custom-call(bf16[1024,2048]{1,0:T(8,128)(2,1)} %bitcast.112, bf16[1024,2048]{1,0:T(8,128)(2,1)} %bitcast.130, bf16[8,256,2048]{2,1,0:T(8,128)(2,1)} %get-tuple-element.51.fc_ref, bf16[8,256,2048]{2,1,0:T(8,128)(2,1)} %get-tuple-element.52.down_ref.down_all), custom_call_target="tpu_custom_call" | custom-call | tf_op jit(solution)/shard_map/middle/pallas_call | solution.py:661
  361.8 91.4 %feedback.1 = (bf16[4,256,2048]{2,1,0:T(8,128)(2,1)}, bf16[256,2048]{1,0:T(8,128)(2,1)}, f32[256,2048]{1,0:T(8,128)}, f32[2,2048]{1,0:T(2,128)}, bf16[512,2048]{...) custom-call(bf16[4,256,2048]{2,1,0:T(8,128)(2,1)} %bitcast.132, ...), custom_call_target="tpu_custom_call" | custom-call | tf_op jit(solution)/shard_map/feedback/pallas_call | solution.py:1005
  453.2 2.0 collective-permute-start.1
  455.3 3.7 fusion.3.rows_ref
  460.1 2.0 copy-done.2
  462.1 3.3 convolution_convert_fusion.1
  465.4 22.7 %attend_back.1 = (bf16[4,2,128,512]{3,2,1,0:T(8,128)(2,1)}, bf16[32,2,128,256]{3,2,1,0:T(8,128)(2,1)}) custom-call(s32[160]{0:T(256)} %copy-done.26, bf16[4,2,128,512]{3,2,1,0:T(8,128)(2,1)} %bitcast.119, bf16[32,2,128,256]{3,2,1,0:T(8,128)(2,1)} %bitcast.110, s32[4,2,1,128]{3,2,1,0:T(1,128)} %copy-done.24, bf16[4,2,128,512]{3,2,1,0:T(8,128)(2,1)} %copy-done.9, ...), custom_call_target="tpu_custom_call" | custom-call | tf_op jit(solution)/shard_map/attend_back/pallas_call | solution.py:262
  488.2 4.6 convolution_convert_fusion.proj_ref
  492.8 7.0 %collective-permute-done = bf16[512,2048]{1,0:T(8,128)(2,1)} collective-permute-done((bf16[512,2048]{1,0:T(8,128)(2,1)}, bf16[512,2048]{1,0:T(8,128)(2,1)}, u32[]{:S(2)}, u32[]{:S(2)}) %collective-permute-start) | collective-permute-done | bytes 2097184 | tf_op jit(solution)/shard_map/ppermute | solution.py:65
  499.9 7.9 %fusion.4 = (bf16[512,2048]{1,0:T(8,128)(2,1)}, bf16[512,2048]{1,0:T(8,128)(2,1)}) fusion(bf16[512,2048]{1,0:T(8,128)(2,1)} %collective-permute-done.1, bf16[3,512,2048]{2,1,0:T(8,128)(2,1)} %get-tuple-element.66.ff_rest, bf16[512,2048]{1,0:T(8,128)(2,1)} %collective-permute-done), kind=kLoop, calls=%fused_computation.9 | loop fusion | flops 8388608 | bytes 12582912 | tf_op jit(solution)/shard_map/convert_element_type | solution.py:69
  507.8 5.0 attn_turned.1.attn_parts
  514.8 144.0 %closing.1 = (bf16[256,2048]{1,0:T(8,128)(2,1)}, bf16[4,64,2048]{2,1,0:T(8,128)(2,1)}, bf16[4,64,2048]{2,1,0:T(8,128)(2,1)}, bf16[4,512,2048]{2,1,0:T(8,128)(2,1)}, f32[288,256]{1,0:T(8,128)}) custom-call(bf16[4,8,256,256]{3,2,1,0:T(8,128)(2,1)} %bitcast.134, bf16[1024,512]{1,0:T(8,128)(2,1)} %bitcast.121, bf16[2048,512]{1,0:T(8,128)(2,1)} %bitcast.124, ...), custom_call_target="tpu_custom_call" | custom-call | tf_op jit(solution)/shard_map/closing/pallas_call | solution.py:1374
  658.8 4.1 slice_bitcast_fusion
  663.7 2.1 place_qkv.1
  665.8 5.4 stack_rows.3
  671.2 5.4 stack_cols.1
  (100 shorter events, 32.1 us)
Async XLA Ops:
  178.0 2.0 copy-start
  181.3 12.0 %copy-start.13 = (bf16[8,256,512]{2,1,0:T(8,128)(2,1)}, bf16[8,256,512]{2,1,0:T(8,128)(2,1)S(1)}, u32[]{:S(2)}) copy-start(bf16[8,256,512]{2,1,0:T(8,128)(2,1)S(1)} %get-tuple-element.45) | copy-start | bytes 6291460
  183.9 14.1 %copy-start.24 = (s32[4,2,1,128]{3,2,1,0:T(1,128)}, s32[4,2,1,128]{3,2,1,0:T(1,128)S(1)}, u32[]{:S(2)}) copy-start(s32[4,2,1,128]{3,2,1,0:T(1,128)S(1)} %add_subtract_fusion.first_ref) | copy-start | bytes 12292
  185.3 12.8 %copy-start.26 = (s32[160]{0:T(256)}, s32[160]{0:T(256)S(1)}, u32[]{:S(2)}) copy-start(s32[160]{0:T(256)S(1)} %reshape.413.tables) | copy-start | bytes 1924
  185.3 3.5 copy-start.1
  196.6 21.7 %copy-start.8 = (bf16[2,128,2048]{2,1,0:T(8,128)(2,1)S(1)}, bf16[2,128,2048]{2,1,0:T(8,128)(2,1)}, u32[]{:S(2)}) copy-start(bf16[2,128,2048]{2,1,0:T(8,128)(2,1)} %param.12) | copy-start | bytes 3145732
  198.1 2.2 copy-start.4
  218.3 143.4 %copy-start.9 = (bf16[4,2,128,512]{3,2,1,0:T(8,128)(2,1)}, bf16[4,2,128,512]{3,2,1,0:T(8,128)(2,1)S(1)}, u32[]{:S(2)}) copy-start(bf16[4,2,128,512]{3,2,1,0:T(8,128)(2,1)S(1)} %get-tuple-element.47.out_ref) | copy-start | bytes 3145732
  218.3 2.0 copy-start.16
  318.5 2.0 copy-start.5
  453.2 46.6 %collective-permute-start = (bf16[512,2048]{1,0:T(8,128)(2,1)}, bf16[512,2048]{1,0:T(8,128)(2,1)}, u32[]{:S(2)}, u32[]{:S(2)}) collective-permute-start(bf16[512,2048]{1,0:T(8,128)(2,1)} %get-tuple-element.58), channel_id=1, source_target_pairs={{0,2},{2,4},{4,6},{6,7},{7,5},{5,3},{3,1},{1,0},{8,10},{10,12},{12... | collective-permute-start | bytes 6291464 | tf_op jit(solution)/shard_map/ppermute | solution.py:65
  453.2 46.6 %collective-permute-start.1 = (bf16[512,2048]{1,0:T(8,128)(2,1)}, bf16[512,2048]{1,0:T(8,128)(2,1)}, u32[]{:S(2)}, u32[]{:S(2)}) collective-permute-start(bf16[512,2048]{1,0:T(8,128)(2,1)} %get-tuple-element.59), channel_id=1, source_target_pairs={{2,0},{4,2},{6,4},{7,6},{5,7},{3,5},{1,3},{0,1},{10,8},{12,10},{14... | collective-permute-start | bytes 6291464 | tf_op jit(solution)/shard_map/ppermute | solution.py:66
  455.3 6.8 %copy-start.17 = (bf16[8,64,2048]{2,1,0:T(8,128)(2,1)S(1)}, bf16[8,64,2048]{2,1,0:T(8,128)(2,1)}, u32[]{:S(2)}) copy-start(bf16[8,64,2048]{2,1,0:T(8,128)(2,1)} %copy-done.15) | copy-start | bytes 6291460
  455.3 6.8 %copy-start.30 = (bf16[4,256,2048]{2,1,0:T(8,128)(2,1)S(1)}, bf16[4,256,2048]{2,1,0:T(8,128)(2,1)}, u32[]{:S(2)}) copy-start(bf16[4,256,2048]{2,1,0:T(8,128)(2,1)} %get-tuple-element.61) | copy-start | bytes 12582916
  460.1 2.0 copy-start.2
  465.4 22.8 %copy-start.10 = (bf16[4,2,128,512]{3,2,1,0:T(8,128)(2,1)S(1)}, bf16[4,2,128,512]{3,2,1,0:T(8,128)(2,1)}, u32[]{:S(2)}) copy-start(bf16[4,2,128,512]{3,2,1,0:T(8,128)(2,1)} %copy-done.9) | copy-start | bytes 3145732
  499.9 7.9 %copy-start.3 = (bf16[1024,2048]{1,0:T(8,128)(2,1)S(1)}, bf16[1024,2048]{1,0:T(8,128)(2,1)}, u32[]{:S(2)}) copy-start(bf16[1024,2048]{1,0:T(8,128)(2,1)} %copy-done.2) | copy-start | bytes 12582916
  499.9 7.9 %copy-start.12 = (bf16[4,2,128,512]{3,2,1,0:T(8,128)(2,1)S(1)}, bf16[4,2,128,512]{3,2,1,0:T(8,128)(2,1)}, u32[]{:S(2)}) copy-start(bf16[4,2,128,512]{3,2,1,0:T(8,128)(2,1)} %get-tuple-element.65) | copy-start | bytes 3145732
  512.8 2.0 copy-start.6
  658.8 4.2 copy-start.29
  658.8 4.3 copy-start.23
  658.8 4.9 copy-start.22
  671.2 7.4 %copy-start.27 = (bf16[256,2048]{1,0:T(8,128)(2,1)S(1)}, bf16[256,2048]{1,0:T(8,128)(2,1)}, u32[]{:S(2)}) copy-start(bf16[256,2048]{1,0:T(8,128)(2,1)} %get-tuple-element.57) | copy-start | bytes 3145732
  676.6 3.0 copy-start.28
  (9 other events, 10.5 us)

commit v5 on v4

--- a/solution.py
+++ b/solution.py
@@ -373,11 +373,13 @@
         self.owner, self.up, self.down = owner, up, down
         self.copies = {}
 
-    def start(self, step):
+    def start(self, step, given=None):
         half = self.slots.shape[1] // 2
         for way, device in enumerate((self.up, self.down)):
             slot = self.slots.at[self.owner((1 - step) if way == 0 else (step - 1))]
             source = self.own if step == 1 else slot
+            if given is not None:
+                source = given[way]
             if step == self.count // 2:
                 rows = pl.ds(way * half, half)
                 source, slot = source.at[rows], slot.at[rows]
@@ -408,6 +410,8 @@
     cot_out,
     weights,
     mine,
+    q_own,
+    fc_own,
     hid_chip,
     hid_core,
     kvw_sems,
@@ -435,8 +439,11 @@
     greet_also((up, down, chip, core), (source,), own_goes, s, f)
     part = proj_out.shape[1]
     q_cols = qw_out.shape[2]
-    q_own = qkv_weight.at[:, pl.ds(pl.multiple_of(s * q_cols, q_cols), q_cols)]
-    proj_own, fc_own = proj_out.at[f], fc_out.at[f]
+    q_cut = pltpu.make_async_copy(
+        qkv_weight.at[:, pl.ds(pl.multiple_of(s * q_cols, q_cols), q_cols)], q_own, local.at[4]
+    )
+    q_cut.start()
+    proj_own = proj_out.at[f]
     rings = [
         KernelRing(count, own, slots, sems, owner, up, down)
         for own, slots, sems in (
@@ -485,13 +492,18 @@
             (
                 (hidden, hidden_out.at[0]),
                 (kv_own, kvw_out.at[f]),
-                (q_own, qw_out.at[f]),
                 (cot, cot_out.at[0]),
             )
         )
     ]
     for copy in stays:
         copy.start()
+    q_cut.wait()
+    for copy in cuts:
+        copy.wait()
+    for i, (source, target) in enumerate(((q_own, qw_out.at[f]), (fc_own, fc_out.at[f]))):
+        stays.append(pltpu.make_async_copy(source, target, local.at[3 if i == 0 else 5]))
+        stays[-1].start()
     values = hidden[...].astype(F32)
     mean = jnp.mean(values, axis=-1, keepdims=True)
     center = values - mean
@@ -500,8 +512,6 @@
         kvw.arrived(step - 1)
         kvw.start(step)
     qw.start(1)
-    for copy in cuts:
-        copy.wait()
     fc.start(1)
     kvw.arrived(steps)
     stays[1].wait()
@@ -591,11 +601,13 @@
             jax.ShapeDtypeStruct((fsdp_count, shard, width), BF),
             jax.ShapeDtypeStruct((4,) + hidden.shape, BF),
         ),
-        in_specs=[inside] + [anywhere] * 5,
+        in_specs=[inside, inside] + [anywhere] * 3 + [inside],
         out_specs=(anywhere,) * 7,
         scratch_shapes=[
             pltpu.VMEM((fsdp_count,) + kv_own.shape, BF),
             pltpu.VMEM((count, 2 * HD), BF),
+            pltpu.VMEM((shard, q_cols), BF),
+            pltpu.VMEM((shard, width), BF),
             dma((2, 2)),
             dma((2, 3)),
             ring,
@@ -686,6 +698,8 @@
     hidden,
     vectors,
     down_own,
+    first_up,
+    first_down,
     mlp_out,
     resid_out,
     down_out,
@@ -709,9 +723,11 @@
     steps = count // 2
     tokens = hidden.shape[0]
     ring = KernelRing(count, down_own, down_out, down_sems, owner, up, down)
-    ring.start(1)
+    ring.start(2, (first_up, first_down))
     stays = [
         pltpu.make_async_copy(down_own, down_out.at[f], local.at[0]),
+        pltpu.make_async_copy(first_up, down_out.at[owner(-1)], local.at[2]),
+        pltpu.make_async_copy(first_down, down_out.at[owner(1)], local.at[3]),
     ]
     for copy in stays:
         copy.start()
@@ -744,14 +760,14 @@
             mine[here] = (normed * vectors[0:1] + vectors[1:2]).astype(BF)
         spread.append(send(mine.at[half], mlp_out.at[2, half], spread_chip, (i,), chip))
         spread_pair.append(send(mine.at[half], mlp_out.at[1, half], spread_core, (i,), core))
-        ring.arrived(i + 1)
-        ring.start(i + 2)
+        ring.arrived(i + 2)
+        ring.start(i + 3)
     stays.append(pltpu.make_async_copy(mine, mlp_out.at[0], local.at[1]))
     stays[-1].start()
     for i, half in enumerate(halves):
         spread[i].wait_recv()
         spread_pair.append(send(mlp_out.at[2, half], mlp_out.at[3, half], spread_core, (2 + i,), core))
-    for step in range(3, steps + 1):
+    for step in range(4, steps + 1):
         ring.arrived(step)
         if step < steps:
             ring.start(step + 1)
@@ -762,7 +778,7 @@
         copy.wait()
 
 
-def bridge(heads, proj, hidden, vectors, down_own, fsdp_count):
+def bridge(heads, proj, hidden, vectors, down_own, first, fsdp_count):
     tokens, width = hidden.shape
     quarter = down_own.shape[0]
     dma = pltpu.SemaphoreType.DMA
@@ -776,7 +792,7 @@
             jax.ShapeDtypeStruct((tokens, width), F32),
             jax.ShapeDtypeStruct((fsdp_count, quarter, width), BF),
         ),
-        in_specs=[inside] * 4 + [anywhere],
+        in_specs=[inside] * 7,
         out_specs=(anywhere, inside, anywhere),
         scratch_shapes=[wide] * 6
         + [
@@ -792,7 +808,7 @@
         ),
         cost_estimate=COST,
         name="bridge",
-    )(heads, proj, hidden, vectors, down_own)
+    )(heads, proj, hidden, vectors, down_own, *first)
 
 
 def feedback_kernel(
@@ -1650,6 +1666,8 @@
         hidden_own, own_kv, qkv_weight, proj_weight, fc_weight, cotangent, fsdp_count, head_cols
     )
     cotangent_all = cotangent_all.reshape(group, width)
+    down_first, kv_all = lax.optimization_barrier((down_own, kv_all))
+    down_given = (lax.ppermute(down_first, "fsdp", ring.up), lax.ppermute(down_first, "fsdp", ring.down))
     kv_weight = kv_ring[:, :shard].reshape(width, 2 * HD)
     vectors = kv_ring[:, shard : shard + 4, :shard].transpose(1, 0, 2).reshape(4, width).astype(F32)
     gain_one, bias_one, gain_two, bias_two = vectors[0], vectors[1], vectors[2], vectors[3]
@@ -1664,7 +1682,7 @@
     heads_rows = heads_out.reshape(group, head_cols)
 
     mlp_in, resid, down_all = bridge(
-        heads_rows, proj_full, hidden_own, vectors[2:], down_own, fsdp_count
+        heads_rows, proj_full, hidden_own, vectors[2:], down_own, down_given, fsdp_count
     )
     mlp_in = mlp_in.reshape(group, width)
     activ, pre_grad, mlp_in_parts = middle(mlp_in, cotangent_all, fc_all, down_all, 2 * BLOCK)

time: 691 us -> 666 us (0.964)
  Pallas kernels: 601 us -> 584 us
    pallas_call x1, Pallas kernels: 98.2 us -> 73.9 us  [bridge(): pl.pallas_call(functools.partial(bridge_kernel, count=fsdp_count), out_sh...]
  transfers between devices with their start and end apart: 2 -> 4, of which waited for: 2 -> 2; matrix products, arithmetic and copies ran while one was open for 2% -> 4% of each run, Pallas kernels for 3% -> 7%
where the time goes in v5:
time: 666 us; the launch traced here: 657 us
  Pallas kernels  584 us (88%)
  local copies, waits for them, and re-layouts  34.6 us (5%)
  other arithmetic  17.8 us (3%)
  matrix products  12.4 us (2%)
    pallas_call x1, Pallas kernels, opening(): pl.pallas_call(functools.partial(opening_kernel, count=fsdp_count, shard=...  168 us
    pallas_call x1, Pallas kernels, closing(): pl.pallas_call(functools.partial(closing_kernel, count=fsdp_count, shard=...  143 us
    pallas_call x1, Pallas kernels, feedback(): pl.pallas_call(functools.partial(feedback_kernel, count=fsdp_count, shard...  94.5 us
    pallas_call x1, Pallas kernels, bridge(): pl.pallas_call(functools.partial(bridge_kernel, count=fsdp_count), out_sh...  73.9 us
    pallas_call x1, Pallas kernels, middle(): pl.pallas_call(functools.partial(middle_kernel, step=256), out_shape=(jax...  40 us
    pallas_call x1, Pallas kernels, attend_back(): pl.pallas_call(functools.partial(attend_back_kernel, heads=heads, blocks=...  25.6 us
    unnamed x66, local copies, waits for them, and re-layouts  20.1 us
    pallas_call x1, Pallas kernels, attend(): pl.pallas_call(functools.partial(attend_kernel, heads=heads, blocks=block...  19.1 us
  transfers between devices with their start and end apart: 4, of which 2 were waited for; matrix products, arithmetic and copies ran while one was open for 4% of the time, Pallas kernels for 7%

profile of v5, /device:TPU:0, one launch (start us, length us, event | category | flops | bytes accessed | tf_op | source)
XLA Modules:
  0.0 656.8 jit_solution(855781894471439452)
XLA Ops:
  4.2 2.3 constant_dynamic-slice_fusion.down_own
  11.5 168.2 %opening.1 = (bf16[4,256,2048]{2,1,0:T(8,128)(2,1)S(1)}, bf16[8,288,256]{2,1,0:T(8,128)(2,1)S(1)}, bf16[8,256,512]{2,1,0:T(8,128)(2,1)S(1)}, bf16[8,64,2048]{2,1...) custom-call(bf16[256,2048]{1,0:T(8,128)(2,1)S(1)} %bitcast.115, ...), custom_call_target="tpu_custom_call" | custom-call | tf_op jit(solution)/shard_map/opening/pallas_call | solution.py:593
  179.8 2.0 copy-done
  184.4 2.0 collective-permute-start.1
  189.4 3.0 convert_reduce_fusion
  195.8 2.3 convolution_convert_fusion.2
  198.2 19.1 %attend.1 = (bf16[4,2,128,512]{3,2,1,0:T(8,128)(2,1)S(1)}, f32[4,2,4,128]{3,2,1,0:T(4,128)S(1)}) custom-call(s32[160]{0:T(256)S(1)} %reshape.413.tables, bf16[4,2,128,512]{3,2,1,0:T(8,128)(2,1)S(1)} %bitcast.117, bf16[32,2,128,256]{3,2,1,0:T(8,128)(2,1)S(1)} %bitcast.111, s32[4,2,1,128]{3,2,1,0:T(1,128)S(1)} %add_subtract_fusion.first_ref), custom_call_target="tpu_custom_call" | custom-call | tf_op jit(solution)/shard_map/attend/pallas_call | solution.py:229
  218.0 73.9 %bridge.1 = (bf16[4,256,2048]{2,1,0:T(8,128)(2,1)S(1)}, f32[256,2048]{1,0:T(8,128)S(1)}, bf16[8,256,2048]{2,1,0:T(8,128)(2,1)}) custom-call(bf16[1024,512]{1,0:T(8,128)(2,1)S(1)} %bitcast.119, bf16[512,2048]{1,0:T(8,128)(2,1)S(1)} %bitcast.125, bf16[256,2048]{1,0:T(8,128)(2,1)S(1)} %bitcast.116, f32[2,2048]{1,0:T(2,128)S(1)} %bitcast.129, ...), custom_call_target="tpu_custom_call" | custom-call | tf_op jit(solution)/shard_map/bridge/pallas_call | solution.py:788
  295.3 40.0 %middle.1 = (bf16[1024,2048]{1,0:T(8,128)(2,1)}, bf16[1024,2048]{1,0:T(8,128)(2,1)}, bf16[1024,2048]{1,0:T(8,128)(2,1)}) custom-call(bf16[1024,2048]{1,0:T(8,128)(2,1)} %bitcast.112, bf16[1024,2048]{1,0:T(8,128)(2,1)} %bitcast.130, bf16[8,256,2048]{2,1,0:T(8,128)(2,1)} %get-tuple-element.55.fc_ref, bf16[8,256,2048]{2,1,0:T(8,128)(2,1)} %get-tuple-element.56.down_ref.down_all), custom_call_target="tpu_custom_call" | custom-call | tf_op jit(solution)/shard_map/middle/pallas_call | solution.py:673
  335.3 94.5 %feedback.1 = (bf16[4,256,2048]{2,1,0:T(8,128)(2,1)}, bf16[256,2048]{1,0:T(8,128)(2,1)}, f32[256,2048]{1,0:T(8,128)}, f32[2,2048]{1,0:T(2,128)}, bf16[512,2048]{...) custom-call(bf16[4,256,2048]{2,1,0:T(8,128)(2,1)} %bitcast.132, ...), custom_call_target="tpu_custom_call" | custom-call | tf_op jit(solution)/shard_map/feedback/pallas_call | solution.py:1021
  429.9 2.0 collective-permute-start.3
  431.9 3.7 fusion.3.rows_ref
  436.7 2.0 copy-done.2
  438.9 5.5 convolution_convert_fusion.1
  444.4 25.6 %attend_back.1 = (bf16[4,2,128,512]{3,2,1,0:T(8,128)(2,1)}, bf16[32,2,128,256]{3,2,1,0:T(8,128)(2,1)}) custom-call(s32[160]{0:T(256)} %copy-done.27, bf16[4,2,128,512]{3,2,1,0:T(8,128)(2,1)} %bitcast.118, bf16[32,2,128,256]{3,2,1,0:T(8,128)(2,1)} %bitcast.110, s32[4,2,1,128]{3,2,1,0:T(1,128)} %copy-done.25, bf16[4,2,128,512]{3,2,1,0:T(8,128)(2,1)} %copy-done.10, ...), custom_call_target="tpu_custom_call" | custom-call | tf_op jit(solution)/shard_map/attend_back/pallas_call | solution.py:262
  470.0 4.6 convolution_convert_fusion.proj_ref
  474.6 2.3 collective-permute-done.2
  476.9 7.9 %fusion.4 = (bf16[512,2048]{1,0:T(8,128)(2,1)}, bf16[512,2048]{1,0:T(8,128)(2,1)}) fusion(bf16[512,2048]{1,0:T(8,128)(2,1)} %collective-permute-done.3, bf16[3,512,2048]{2,1,0:T(8,128)(2,1)} %get-tuple-element.70.ff_rest, bf16[512,2048]{1,0:T(8,128)(2,1)} %collective-permute-done.2), kind=kLoop, calls=%fused_computation.9 | loop fusion | flops 8388608 | bytes 12582912 | tf_op jit(solution)/shard_map/convert_element_type | solution.py:69
  484.8 5.0 attn_turned.1.attn_parts
  491.8 142.8 %closing.1 = (bf16[256,2048]{1,0:T(8,128)(2,1)}, bf16[4,64,2048]{2,1,0:T(8,128)(2,1)}, bf16[4,64,2048]{2,1,0:T(8,128)(2,1)}, bf16[4,512,2048]{2,1,0:T(8,128)(2,1)}, f32[288,256]{1,0:T(8,128)}) custom-call(bf16[4,8,256,256]{3,2,1,0:T(8,128)(2,1)} %bitcast.134, bf16[1024,512]{1,0:T(8,128)(2,1)} %bitcast.121, bf16[2048,512]{1,0:T(8,128)(2,1)} %bitcast.123, ...), custom_call_target="tpu_custom_call" | custom-call | tf_op jit(solution)/shard_map/closing/pallas_call | solution.py:1390
  634.7 4.1 slice_bitcast_fusion
  639.5 2.1 place_qkv.1
  641.6 5.4 stack_rows.3
  647.0 5.4 stack_cols.1
  (104 shorter events, 29.6 us)
Async XLA Ops:
  179.7 2.0 copy-start
  184.4 9.6 %copy-start.20 = (bf16[8,288,256]{2,1,0:T(8,128)(2,1)}, bf16[8,288,256]{2,1,0:T(8,128)(2,1)S(1)}, u32[]{:S(2)}) copy-start(bf16[8,288,256]{2,1,0:T(8,128)(2,1)S(1)} %get-tuple-element.46.kv_weight) | copy-start | bytes 3538948
  184.4 33.6 %collective-permute-start = (bf16[256,2048]{1,0:T(8,128)(2,1)}, bf16[256,2048]{1,0:T(8,128)(2,1)}, u32[]{:S(2)}, u32[]{:S(2)}) collective-permute-start(bf16[256,2048]{1,0:T(8,128)(2,1)} %constant_dynamic-slice_fusion.down_own), channel_id=1, source_target_pairs={{0,2},{2,4},{4,6},{6,7},{7,5},{5,3},{3,1},{1,0},{8,10},{10,12},{12... | collective-permute-start | bytes 3145736 | tf_op jit(solution)/shard_map/ppermute | solution.py:1670
  184.4 33.6 %collective-permute-start.1 = (bf16[256,2048]{1,0:T(8,128)(2,1)}, bf16[256,2048]{1,0:T(8,128)(2,1)}, u32[]{:S(2)}, u32[]{:S(2)}) collective-permute-start(bf16[256,2048]{1,0:T(8,128)(2,1)} %constant_dynamic-slice_fusion.down_own), channel_id=1, source_target_pairs={{2,0},{4,2},{6,4},{7,6},{5,7},{3,5},{1,3},{0,1},{10,8},{12,10},{14... | collective-permute-start | bytes 3145736 | tf_op jit(solution)/shard_map/ppermute | solution.py:1670
  188.0 10.2 %copy-start.25 = (s32[4,2,1,128]{3,2,1,0:T(1,128)}, s32[4,2,1,128]{3,2,1,0:T(1,128)S(1)}, u32[]{:S(2)}) copy-start(s32[4,2,1,128]{3,2,1,0:T(1,128)S(1)} %add_subtract_fusion.first_ref) | copy-start | bytes 12292
  189.3 8.9 %copy-start.27 = (s32[160]{0:T(256)}, s32[160]{0:T(256)S(1)}, u32[]{:S(2)}) copy-start(s32[160]{0:T(256)S(1)} %reshape.413.tables) | copy-start | bytes 1924
  189.3 3.5 copy-start.1
  195.8 2.4 copy-start.4
  198.2 93.7 %copy-start.9 = (bf16[1024,512]{1,0:T(8,128)(2,1)}, bf16[1024,512]{1,0:T(8,128)(2,1)S(1)}, u32[]{:S(2)}) copy-start(bf16[1024,512]{1,0:T(8,128)(2,1)S(1)} %convolution_convert_fusion.2) | copy-start | bytes 3145732
  198.2 19.8 %copy-start.8 = (bf16[2,128,2048]{2,1,0:T(8,128)(2,1)S(1)}, bf16[2,128,2048]{2,1,0:T(8,128)(2,1)}, u32[]{:S(2)}) copy-start(bf16[2,128,2048]{2,1,0:T(8,128)(2,1)} %param.12) | copy-start | bytes 3145732
  198.2 19.8 %copy-start.16 = (bf16[8,64,2048]{2,1,0:T(8,128)(2,1)S(1)}, bf16[8,64,2048]{2,1,0:T(8,128)(2,1)}, u32[]{:S(2)}) copy-start(bf16[8,64,2048]{2,1,0:T(8,128)(2,1)} %copy-done.15) | copy-start | bytes 6291460
  218.0 77.3 %copy-start.10 = (bf16[4,2,128,512]{3,2,1,0:T(8,128)(2,1)}, bf16[4,2,128,512]{3,2,1,0:T(8,128)(2,1)S(1)}, u32[]{:S(2)}) copy-start(bf16[4,2,128,512]{3,2,1,0:T(8,128)(2,1)S(1)} %get-tuple-element.50.out_ref) | copy-start | bytes 3145732
  291.9 2.0 copy-start.5
  429.8 47.1 %collective-permute-start.2 = (bf16[512,2048]{1,0:T(8,128)(2,1)}, bf16[512,2048]{1,0:T(8,128)(2,1)}, u32[]{:S(2)}, u32[]{:S(2)}) collective-permute-start(bf16[512,2048]{1,0:T(8,128)(2,1)} %get-tuple-element.62), channel_id=1, source_target_pairs={{0,2},{2,4},{4,6},{6,7},{7,5},{5,3},{3,1},{1,0},{8,10},{10,12},{12... | collective-permute-start | bytes 6291464 | tf_op jit(solution)/shard_map/ppermute | solution.py:65
  429.9 47.1 %collective-permute-start.3 = (bf16[512,2048]{1,0:T(8,128)(2,1)}, bf16[512,2048]{1,0:T(8,128)(2,1)}, u32[]{:S(2)}, u32[]{:S(2)}) collective-permute-start(bf16[512,2048]{1,0:T(8,128)(2,1)} %get-tuple-element.63), channel_id=1, source_target_pairs={{2,0},{4,2},{6,4},{7,6},{5,7},{3,5},{1,3},{0,1},{10,8},{12,10},{14... | collective-permute-start | bytes 6291464 | tf_op jit(solution)/shard_map/ppermute | solution.py:66
  431.9 7.0 %copy-start.17 = (bf16[8,64,2048]{2,1,0:T(8,128)(2,1)S(1)}, bf16[8,64,2048]{2,1,0:T(8,128)(2,1)}, u32[]{:S(2)}) copy-start(bf16[8,64,2048]{2,1,0:T(8,128)(2,1)} %copy-done.15) | copy-start | bytes 6291460
  444.4 25.6 %copy-start.11 = (bf16[4,2,128,512]{3,2,1,0:T(8,128)(2,1)S(1)}, bf16[4,2,128,512]{3,2,1,0:T(8,128)(2,1)}, u32[]{:S(2)}) copy-start(bf16[4,2,128,512]{3,2,1,0:T(8,128)(2,1)} %copy-done.10) | copy-start | bytes 3145732
  476.9 7.9 %copy-start.3 = (bf16[1024,2048]{1,0:T(8,128)(2,1)S(1)}, bf16[1024,2048]{1,0:T(8,128)(2,1)}, u32[]{:S(2)}) copy-start(bf16[1024,2048]{1,0:T(8,128)(2,1)} %copy-done.2) | copy-start | bytes 12582916
  476.9 7.9 %copy-start.12 = (bf16[4,2,128,512]{3,2,1,0:T(8,128)(2,1)S(1)}, bf16[4,2,128,512]{3,2,1,0:T(8,128)(2,1)}, u32[]{:S(2)}) copy-start(bf16[4,2,128,512]{3,2,1,0:T(8,128)(2,1)} %get-tuple-element.69) | copy-start | bytes 3145732
  634.6 4.2 copy-start.30
  634.7 4.3 copy-start.24
  634.7 4.9 copy-start.23
  647.0 7.4 %copy-start.28 = (bf16[256,2048]{1,0:T(8,128)(2,1)S(1)}, bf16[256,2048]{1,0:T(8,128)(2,1)}, u32[]{:S(2)}) copy-start(bf16[256,2048]{1,0:T(8,128)(2,1)} %get-tuple-element.61) | copy-start | bytes 3145732
  652.5 3.0 copy-start.29
  (11 other events, 15.3 us)

commit v6 on v5

--- a/solution.py
+++ b/solution.py
@@ -561,8 +561,9 @@
         else:
             proj.arrived(step - 1)
             proj.start(step)
-        fc.arrived(step)
-        if step < steps:
+        if step < steps - 1:
+            fc.arrived(step)
+        if step < steps - 2:
             fc.start(step + 1)
     other = lax.rem(s + 2, 4)
     far = []
@@ -1676,10 +1677,21 @@
     kv_all = kv_all.reshape(seq_count * fsdp_count, MB, count, 2 * HD)
     normed_all, _ = layer_norm(hidden_all.reshape(group, width).astype(F32))
     attn_in = (normed_all * gain_one + bias_one).astype(BF)
+    attn_in = lax.optimization_barrier(attn_in)
     own_attn_in = attn_in[:tokens_here]
     queries = dot_plain(attn_in, q_weight).astype(BF).reshape(seq_count, MB, count, head_cols)
     heads_out, logs = attend(tables, first, queries, kv_all, blocks)
     heads_rows = heads_out.reshape(group, head_cols)
+
+    far = fsdp_count // 2 - 1
+    low = lax.dynamic_index_in_dim(fc_all, ring.owner(1 - far), 0, keepdims=False)
+    high = lax.dynamic_index_in_dim(fc_all, ring.owner(far - 1), 0, keepdims=False)
+    low, high = lax.ppermute(low, "fsdp", ring.up), lax.ppermute(high, "fsdp", ring.down)
+    low, high, heads_rows = lax.optimization_barrier((low, high, heads_rows))
+    last_low = lax.ppermute(low[: shard // 2], "fsdp", ring.up)
+    last_high = lax.ppermute(high[shard // 2 :], "fsdp", ring.down)
+    for piece, step, row in ((low, -far, 0), (high, far, 0), (last_low, far + 1, 0), (last_high, far + 1, shard // 2)):
+        fc_all = lax.dynamic_update_slice(fc_all, piece[None], (ring.owner(step), row, 0))
 
     mlp_in, resid, down_all = bridge(
         heads_rows, proj_full, hidden_own, vectors[2:], down_own, down_given, fsdp_count

time: 666 us -> 653 us (0.980)
  Pallas kernels: 584 us -> 539 us
  waiting for transfers between devices: 2.34 us -> 18.3 us
  local copies, waits for them, and re-layouts: 34.6 us -> 46.7 us
    pallas_call x1, Pallas kernels: 168 us -> 134 us  [opening(): pl.pallas_call(functools.partial(opening_kernel, count=fsdp_count, shard=...]
    ppermute x0 -> x4, waiting for transfers between devices: none -> 7.01 us  [the longest x1 6.97 us: shards(): lax.ppermute(low, 'fsdp', ring.up)]
    unnamed x66 -> x60, local copies, waits for them, and re-layouts: 20.1 us -> 19.3 us
  transfers between devices with their start and end apart: 4 -> 8, of which waited for: 2 -> 3; matrix products, arithmetic and copies ran while one was open for 4% -> 6% of each run, Pallas kernels for 7% -> 17%
where the time goes in v6:
time: 653 us; the launch traced here: 646 us
  Pallas kernels  539 us (83%)
  local copies, waits for them, and re-layouts  46.7 us (7%)
  waiting for transfers between devices  18.3 us (3%)
  other arithmetic  16.3 us (2%)
  matrix products  14.6 us (2%)
  starting transfers between devices  9.16 us (1%)
    pallas_call x1, Pallas kernels, closing(): pl.pallas_call(functools.partial(closing_kernel, count=fsdp_count, shard=...  142 us
    pallas_call x1, Pallas kernels, opening(): pl.pallas_call(functools.partial(opening_kernel, count=fsdp_count, shard=...  134 us
    pallas_call x1, Pallas kernels, feedback(): pl.pallas_call(functools.partial(feedback_kernel, count=fsdp_count, shard...  92.4 us
    pallas_call x1, Pallas kernels, bridge(): pl.pallas_call(functools.partial(bridge_kernel, count=fsdp_count), out_sh...  72.7 us
    pallas_call x1, Pallas kernels, middle(): pl.pallas_call(functools.partial(middle_kernel, step=256), out_shape=(jax...  39.7 us
    pallas_call x1, Pallas kernels, attend_back(): pl.pallas_call(functools.partial(attend_back_kernel, heads=heads, blocks=...  22.1 us
    unnamed x60, local copies, waits for them, and re-layouts  19.3 us
    pallas_call x1, Pallas kernels, attend(): pl.pallas_call(functools.partial(attend_kernel, heads=heads, blocks=block...  15.7 us
  transfers between devices with their start and end apart: 8, of which 3 were waited for; matrix products, arithmetic and copies ran while one was open for 6% of the time, Pallas kernels for 17%

profile of v6, /device:TPU:0, one launch (start us, length us, event | category | flops | bytes accessed | tf_op | source)
XLA Modules:
  0.0 645.8 jit_solution(1644993901165933054)
XLA Ops:
  4.2 2.3 constant_dynamic-slice_fusion.down_own
  11.5 134.4 %opening.1 = (bf16[4,256,2048]{2,1,0:T(8,128)(2,1)S(1)}, bf16[8,288,256]{2,1,0:T(8,128)(2,1)S(1)}, bf16[8,256,512]{2,1,0:T(8,128)(2,1)S(1)}, bf16[8,64,2048]{2,1...) custom-call(bf16[256,2048]{1,0:T(8,128)(2,1)S(1)} %bitcast.126, ...), custom_call_target="tpu_custom_call" | custom-call | tf_op jit(solution)/shard_map/opening/pallas_call | solution.py:594
  152.4 3.1 dynamic-slice_bitcast_fusion
  158.5 3.0 convert_reduce_fusion
  164.6 3.1 fusion.3.rows_ref
  168.6 4.5 convolution_convert_fusion.2
  175.8 15.7 %attend.1 = (bf16[4,2,128,512]{3,2,1,0:T(8,128)(2,1)S(1)}, f32[4,2,4,128]{3,2,1,0:T(4,128)S(1)}) custom-call(s32[160]{0:T(256)S(1)} %reshape.394.tables, bf16[4,2,128,512]{3,2,1,0:T(8,128)(2,1)S(1)} %bitcast.128, bf16[32,2,128,256]{3,2,1,0:T(8,128)(2,1)S(1)} %bitcast.122, s32[4,2,1,128]{3,2,1,0:T(1,128)S(1)} %add_subtract_fusion.first_ref), custom_call_target="tpu_custom_call" | custom-call | tf_op jit(solution)/shard_map/attend/pallas_call | solution.py:229
  191.6 7.0 %collective-permute-done = bf16[256,2048]{1,0:T(8,128)(2,1)} collective-permute-done((bf16[256,2048]{1,0:T(8,128)(2,1)}, bf16[256,2048]{1,0:T(8,128)(2,1)}, u32[]{:S(2)}, u32[]{:S(2)}) %collective-permute-start) | collective-permute-done | bytes 1048608 | tf_op jit(solution)/shard_map/ppermute | solution.py:1689
  207.8 72.7 %bridge.1 = (bf16[4,256,2048]{2,1,0:T(8,128)(2,1)S(1)}, f32[256,2048]{1,0:T(8,128)S(1)}, bf16[8,256,2048]{2,1,0:T(8,128)(2,1)}) custom-call(bf16[1024,512]{1,0:T(8,128)(2,1)S(1)} %bitcast.130, bf16[512,2048]{1,0:T(8,128)(2,1)S(1)} %bitcast.136, bf16[256,2048]{1,0:T(8,128)(2,1)S(1)} %bitcast.127, f32[2,2048]{1,0:T(2,128)S(1)} %bitcast.140, ...), custom_call_target="tpu_custom_call" | custom-call | tf_op jit(solution)/shard_map/bridge/pallas_call | solution.py:789
  285.6 39.7 %middle.1 = (bf16[1024,2048]{1,0:T(8,128)(2,1)}, bf16[1024,2048]{1,0:T(8,128)(2,1)}, bf16[1024,2048]{1,0:T(8,128)(2,1)}) custom-call(bf16[1024,2048]{1,0:T(8,128)(2,1)} %bitcast.123, bf16[1024,2048]{1,0:T(8,128)(2,1)} %bitcast.141, bf16[8,256,2048]{2,1,0:T(8,128)(2,1)} %bitcast_dynamic-update-slice_fusion.2.fc_ref, ...), custom_call_target="tpu_custom_call" | custom-call | tf_op jit(solution)/shard_map/middle/pallas_call | solution.py:674
  325.4 92.4 %feedback.1 = (bf16[4,256,2048]{2,1,0:T(8,128)(2,1)}, bf16[256,2048]{1,0:T(8,128)(2,1)}, f32[256,2048]{1,0:T(8,128)}, f32[2,2048]{1,0:T(2,128)}, bf16[512,2048]{...) custom-call(bf16[4,256,2048]{2,1,0:T(8,128)(2,1)} %bitcast.143, ...), custom_call_target="tpu_custom_call" | custom-call | tf_op jit(solution)/shard_map/feedback/pallas_call | solution.py:1022
  417.8 2.5 collective-permute-start.6
  420.5 2.3 slice.176.attn_in
  423.0 5.5 convolution_convert_fusion.1
  428.5 22.1 %attend_back.1 = (bf16[4,2,128,512]{3,2,1,0:T(8,128)(2,1)}, bf16[32,2,128,256]{3,2,1,0:T(8,128)(2,1)}) custom-call(s32[160]{0:T(256)} %copy-done.24, bf16[4,2,128,512]{3,2,1,0:T(8,128)(2,1)} %bitcast.129, bf16[32,2,128,256]{3,2,1,0:T(8,128)(2,1)} %bitcast.121, s32[4,2,1,128]{3,2,1,0:T(1,128)} %copy-done.22, bf16[4,2,128,512]{3,2,1,0:T(8,128)(2,1)} %copy-done.9, ...), custom_call_target="tpu_custom_call" | custom-call | tf_op jit(solution)/shard_map/attend_back/pallas_call | solution.py:262
  450.7 4.6 convolution_convert_fusion.proj_ref
  455.2 8.9 %collective-permute-done.6 = bf16[512,2048]{1,0:T(8,128)(2,1)} collective-permute-done((bf16[512,2048]{1,0:T(8,128)(2,1)}, bf16[512,2048]{1,0:T(8,128)(2,1)}, u32[]{:S(2)}, u32[]{:S(2)}) %collective-permute-start.6) | collective-permute-done | bytes 2097184 | tf_op jit(solution)/shard_map/ppermute | solution.py:65
  464.1 2.4 collective-permute-done.7
  466.5 7.9 %fusion.4 = (bf16[512,2048]{1,0:T(8,128)(2,1)}, bf16[512,2048]{1,0:T(8,128)(2,1)}) fusion(bf16[512,2048]{1,0:T(8,128)(2,1)} %collective-permute-done.7, bf16[3,512,2048]{2,1,0:T(8,128)(2,1)} %get-tuple-element.76.ff_rest, bf16[512,2048]{1,0:T(8,128)(2,1)} %collective-permute-done.6), kind=kLoop, calls=%fused_computation.7 | loop fusion | flops 8388608 | bytes 12582912 | tf_op jit(solution)/shard_map/convert_element_type | solution.py:69
  474.4 5.0 attn_turned.1.attn_parts
  481.4 142.1 %closing.1 = (bf16[256,2048]{1,0:T(8,128)(2,1)}, bf16[4,64,2048]{2,1,0:T(8,128)(2,1)}, bf16[4,64,2048]{2,1,0:T(8,128)(2,1)}, bf16[4,512,2048]{2,1,0:T(8,128)(2,1)}, f32[288,256]{1,0:T(8,128)}) custom-call(bf16[4,8,256,256]{3,2,1,0:T(8,128)(2,1)} %bitcast.144, bf16[1024,512]{1,0:T(8,128)(2,1)} %bitcast.132, bf16[2048,512]{1,0:T(8,128)(2,1)} %bitcast.135, ...), custom_call_target="tpu_custom_call" | custom-call | tf_op jit(solution)/shard_map/closing/pallas_call | solution.py:1391
  623.6 4.1 slice_bitcast_fusion
  630.5 5.4 stack_rows.3
  636.0 5.4 stack_cols.1
  (112 shorter events, 48.0 us)
Async XLA Ops:
  150.3 18.2 %copy-start.12 = (bf16[8,256,512]{2,1,0:T(8,128)(2,1)}, bf16[8,256,512]{2,1,0:T(8,128)(2,1)S(1)}, u32[]{:S(2)}) copy-start(bf16[8,256,512]{2,1,0:T(8,128)(2,1)S(1)} %get-tuple-element.51) | copy-start | bytes 6291460
  150.3 57.5 %collective-permute-start.2 = (bf16[256,2048]{1,0:T(8,128)(2,1)}, bf16[256,2048]{1,0:T(8,128)(2,1)}, u32[]{:S(2)}, u32[]{:S(2)}) collective-permute-start(bf16[256,2048]{1,0:T(8,128)(2,1)} %constant_dynamic-slice_fusion.down_own), channel_id=1, source_target_pairs={{0,2},{2,4},{4,6},{6,7},{7,5},{5,3},{3,1},{1,0},{8,10},{10,12},{12... | collective-permute-start | bytes 3145736 | tf_op jit(solution)/shard_map/ppermute | solution.py:1671
  151.2 56.6 %collective-permute-start.3 = (bf16[256,2048]{1,0:T(8,128)(2,1)}, bf16[256,2048]{1,0:T(8,128)(2,1)}, u32[]{:S(2)}, u32[]{:S(2)}) collective-permute-start(bf16[256,2048]{1,0:T(8,128)(2,1)} %constant_dynamic-slice_fusion.down_own), channel_id=1, source_target_pairs={{2,0},{4,2},{6,4},{7,6},{5,7},{3,5},{1,3},{0,1},{10,8},{12,10},{14... | collective-permute-start | bytes 3145736 | tf_op jit(solution)/shard_map/ppermute | solution.py:1671
  155.5 43.1 %collective-permute-start = (bf16[256,2048]{1,0:T(8,128)(2,1)}, bf16[256,2048]{1,0:T(8,128)(2,1)}, u32[]{:S(2)}, u32[]{:S(2)}) collective-permute-start(bf16[256,2048]{1,0:T(8,128)(2,1)} %get-tuple-element.97), channel_id=1, source_target_pairs={{0,2},{2,4},{4,6},{6,7},{7,5},{5,3},{3,1},{1,0},{8,10},{10,12},{12... | collective-permute-start | bytes 3145736 | tf_op jit(solution)/shard_map/ppermute | solution.py:1689
  156.4 42.2 %collective-permute-start.1 = (bf16[256,2048]{1,0:T(8,128)(2,1)}, bf16[256,2048]{1,0:T(8,128)(2,1)}, u32[]{:S(2)}, u32[]{:S(2)}) collective-permute-start(bf16[256,2048]{1,0:T(8,128)(2,1)} %get-tuple-element.96), channel_id=1, source_target_pairs={{2,0},{4,2},{6,4},{7,6},{5,7},{3,5},{1,3},{0,1},{10,8},{12,10},{14... | collective-permute-start | bytes 3145736 | tf_op jit(solution)/shard_map/ppermute | solution.py:1689
  158.4 15.2 %copy-start.22 = (s32[4,2,1,128]{3,2,1,0:T(1,128)}, s32[4,2,1,128]{3,2,1,0:T(1,128)S(1)}, u32[]{:S(2)}) copy-start(s32[4,2,1,128]{3,2,1,0:T(1,128)S(1)} %add_subtract_fusion.first_ref) | copy-start | bytes 12292
  158.5 3.4 copy-start.1
  173.1 30.7 %copy-start.8 = (bf16[1024,512]{1,0:T(8,128)(2,1)}, bf16[1024,512]{1,0:T(8,128)(2,1)S(1)}, u32[]{:S(2)}) copy-start(bf16[1024,512]{1,0:T(8,128)(2,1)S(1)} %convolution_convert_fusion.2) | copy-start | bytes 3145732
  173.6 30.1 %copy-start.24 = (s32[160]{0:T(256)}, s32[160]{0:T(256)S(1)}, u32[]{:S(2)}) copy-start(s32[160]{0:T(256)S(1)} %reshape.394.tables) | copy-start | bytes 1924
  191.5 16.3 %copy-start.23 = (f32[4,2,4,128]{3,2,1,0:T(4,128)}, f32[4,2,4,128]{3,2,1,0:T(4,128)S(1)}, u32[]{:S(2)}) copy-start(f32[4,2,4,128]{3,2,1,0:T(4,128)S(1)} %get-tuple-element.70.log_ref) | copy-start | bytes 49156
  191.5 89.0 %copy-start.9 = (bf16[4,2,128,512]{3,2,1,0:T(8,128)(2,1)}, bf16[4,2,128,512]{3,2,1,0:T(8,128)(2,1)S(1)}, u32[]{:S(2)}) copy-start(bf16[4,2,128,512]{3,2,1,0:T(8,128)(2,1)S(1)} %get-tuple-element.54.out_ref) | copy-start | bytes 3145732
  191.6 16.2 %copy-start.7 = (bf16[2,128,2048]{2,1,0:T(8,128)(2,1)S(1)}, bf16[2,128,2048]{2,1,0:T(8,128)(2,1)}, u32[]{:S(2)}) copy-start(bf16[2,128,2048]{2,1,0:T(8,128)(2,1)} %param.12) | copy-start | bytes 3145732
  191.6 16.2 %copy-start.14 = (bf16[8,64,2048]{2,1,0:T(8,128)(2,1)S(1)}, bf16[8,64,2048]{2,1,0:T(8,128)(2,1)}, u32[]{:S(2)}) copy-start(bf16[8,64,2048]{2,1,0:T(8,128)(2,1)} %copy-done.13) | copy-start | bytes 6291460
  199.7 84.2 %collective-permute-start.4 = (bf16[128,2048]{1,0:T(8,128)(2,1)S(1)}, bf16[128,2048]{1,0:T(8,128)(2,1)S(1)}, u32[]{:S(2)}, u32[]{:S(2)}) collective-permute-start(bf16[128,2048]{1,0:T(8,128)(2,1)S(1)} %slice.140), channel_id=1, source_target_pairs={{0,2},{2,4},{4,6},{6,7},{7,5},{5,3},{3,1},{1,0},{8,10},{10,12},{12... | collective-permute-start | bytes 1572872 | tf_op jit(solution)/shard_map/ppermute | solution.py:1691
  204.8 79.9 %collective-permute-start.5 = (bf16[128,2048]{1,0:T(8,128)(2,1)S(1)}, bf16[128,2048]{1,0:T(8,128)(2,1)S(1)}, u32[]{:S(2)}, u32[]{:S(2)}) collective-permute-start(bf16[128,2048]{1,0:T(8,128)(2,1)S(1)} %slice.141), channel_id=1, source_target_pairs={{2,0},{4,2},{6,4},{7,6},{5,7},{3,5},{1,3},{0,1},{10,8},{12,10},{14... | collective-permute-start | bytes 1572872 | tf_op jit(solution)/shard_map/ppermute | solution.py:1692
  417.8 46.3 %collective-permute-start.6 = (bf16[512,2048]{1,0:T(8,128)(2,1)}, bf16[512,2048]{1,0:T(8,128)(2,1)}, u32[]{:S(2)}, u32[]{:S(2)}) collective-permute-start(bf16[512,2048]{1,0:T(8,128)(2,1)} %get-tuple-element.68), channel_id=1, source_target_pairs={{0,2},{2,4},{4,6},{6,7},{7,5},{5,3},{3,1},{1,0},{8,10},{10,12},{12... | collective-permute-start | bytes 6291464 | tf_op jit(solution)/shard_map/ppermute | solution.py:65
  420.3 46.2 %collective-permute-start.7 = (bf16[512,2048]{1,0:T(8,128)(2,1)}, bf16[512,2048]{1,0:T(8,128)(2,1)}, u32[]{:S(2)}, u32[]{:S(2)}) collective-permute-start(bf16[512,2048]{1,0:T(8,128)(2,1)} %get-tuple-element.69), channel_id=1, source_target_pairs={{2,0},{4,2},{6,4},{7,6},{5,7},{3,5},{1,3},{0,1},{10,8},{12,10},{14... | collective-permute-start | bytes 6291464 | tf_op jit(solution)/shard_map/ppermute | solution.py:66
  428.5 22.2 %copy-start.10 = (bf16[4,2,128,512]{3,2,1,0:T(8,128)(2,1)S(1)}, bf16[4,2,128,512]{3,2,1,0:T(8,128)(2,1)}, u32[]{:S(2)}) copy-start(bf16[4,2,128,512]{3,2,1,0:T(8,128)(2,1)} %copy-done.9) | copy-start | bytes 3145732
  466.5 7.9 %copy-start.2 = (bf16[1024,2048]{1,0:T(8,128)(2,1)S(1)}, bf16[1024,2048]{1,0:T(8,128)(2,1)}, u32[]{:S(2)}) copy-start(bf16[1024,2048]{1,0:T(8,128)(2,1)} %fusion.3.rows_ref) | copy-start | bytes 12582916
  466.5 7.9 %copy-start.11 = (bf16[4,2,128,512]{3,2,1,0:T(8,128)(2,1)S(1)}, bf16[4,2,128,512]{3,2,1,0:T(8,128)(2,1)}, u32[]{:S(2)}) copy-start(bf16[4,2,128,512]{3,2,1,0:T(8,128)(2,1)} %get-tuple-element.75) | copy-start | bytes 3145732
  623.5 4.2 copy-start.27
  623.6 4.3 copy-start.21
  623.6 4.9 copy-start.20
  635.9 7.4 %copy-start.25 = (bf16[256,2048]{1,0:T(8,128)(2,1)S(1)}, bf16[256,2048]{1,0:T(8,128)(2,1)}, u32[]{:S(2)}) copy-start(bf16[256,2048]{1,0:T(8,128)(2,1)} %get-tuple-element.67) | copy-start | bytes 3145732
  (12 other events, 19.9 us)

commit v7 on v6

--- a/solution.py
+++ b/solution.py
@@ -1697,7 +1697,7 @@
         heads_rows, proj_full, hidden_own, vectors[2:], down_own, down_given, fsdp_count
     )
     mlp_in = mlp_in.reshape(group, width)
-    activ, pre_grad, mlp_in_parts = middle(mlp_in, cotangent_all, fc_all, down_all, 2 * BLOCK)
+    activ, pre_grad, mlp_in_parts = middle(mlp_in, cotangent_all, fc_all, down_all, 4 * BLOCK)
     branch, result, resid_grad, mlp_vectors, ff_up, ff_down, ff_rest = feedback(
         mlp_in_parts.reshape(seq_count, tokens_here, width),
         mlp_in,

time: 653 us -> 650 us (level)
  transfers between devices with their start and end apart: 8 -> 8, of which waited for: 3 -> 3; matrix products, arithmetic and copies ran while one was open for 6% -> 6% of each run, Pallas kernels for 17% -> 18%
where the time goes in v7:
time: 650 us; the launch traced here: 643 us
  Pallas kernels  540 us (83%)
  local copies, waits for them, and re-layouts  46.7 us (7%)
  other arithmetic  16.3 us (3%)
  matrix products  14.6 us (2%)
  waiting for transfers between devices  14.3 us (2%)
  starting transfers between devices  9.64 us (1%)
    pallas_call x1, Pallas kernels, closing(): pl.pallas_call(functools.partial(closing_kernel, count=fsdp_count, shard=...  142 us
    pallas_call x1, Pallas kernels, opening(): pl.pallas_call(functools.partial(opening_kernel, count=fsdp_count, shard=...  134 us
    pallas_call x1, Pallas kernels, feedback(): pl.pallas_call(functools.partial(feedback_kernel, count=fsdp_count, shard...  92.4 us
    pallas_call x1, Pallas kernels, bridge(): pl.pallas_call(functools.partial(bridge_kernel, count=fsdp_count), out_sh...  70.8 us
    pallas_call x1, Pallas kernels, middle(): pl.pallas_call(functools.partial(middle_kernel, step=256), out_shape=(jax...  38.9 us
    pallas_call x1, Pallas kernels, attend_back(): pl.pallas_call(functools.partial(attend_back_kernel, heads=heads, blocks=...  24.2 us
    unnamed x60, local copies, waits for them, and re-layouts  19.3 us
    pallas_call x1, Pallas kernels, attend(): pl.pallas_call(functools.partial(attend_kernel, heads=heads, blocks=block...  17.7 us
  transfers between devices with their start and end apart: 8, of which 3 were waited for; matrix products, arithmetic and copies ran while one was open for 6% of the time, Pallas kernels for 18%

profile of v7, /device:TPU:0, one launch (start us, length us, event | category | flops | bytes accessed | tf_op | source)
XLA Modules:
  0.0 642.8 jit_solution(4413496532279941696)
XLA Ops:
  4.2 2.3 constant_dynamic-slice_fusion.down_own
  11.5 134.4 %opening.1 = (bf16[4,256,2048]{2,1,0:T(8,128)(2,1)S(1)}, bf16[8,288,256]{2,1,0:T(8,128)(2,1)S(1)}, bf16[8,256,512]{2,1,0:T(8,128)(2,1)S(1)}, bf16[8,64,2048]{2,1...) custom-call(bf16[256,2048]{1,0:T(8,128)(2,1)S(1)} %bitcast.126, ...), custom_call_target="tpu_custom_call" | custom-call | tf_op jit(solution)/shard_map/opening/pallas_call | solution.py:594
  152.4 3.1 dynamic-slice_bitcast_fusion
  158.5 3.0 convert_reduce_fusion
  164.6 3.1 fusion.3.rows_ref
  168.6 4.5 convolution_convert_fusion.2
  175.8 17.7 %attend.1 = (bf16[4,2,128,512]{3,2,1,0:T(8,128)(2,1)S(1)}, f32[4,2,4,128]{3,2,1,0:T(4,128)S(1)}) custom-call(s32[160]{0:T(256)S(1)} %reshape.394.tables, bf16[4,2,128,512]{3,2,1,0:T(8,128)(2,1)S(1)} %bitcast.128, bf16[32,2,128,256]{3,2,1,0:T(8,128)(2,1)S(1)} %bitcast.122, s32[4,2,1,128]{3,2,1,0:T(1,128)S(1)} %add_subtract_fusion.first_ref), custom_call_target="tpu_custom_call" | custom-call | tf_op jit(solution)/shard_map/attend/pallas_call | solution.py:229
  193.6 5.0 collective-permute-done
  208.1 70.8 %bridge.1 = (bf16[4,256,2048]{2,1,0:T(8,128)(2,1)S(1)}, f32[256,2048]{1,0:T(8,128)S(1)}, bf16[8,256,2048]{2,1,0:T(8,128)(2,1)}) custom-call(bf16[1024,512]{1,0:T(8,128)(2,1)S(1)} %bitcast.130, bf16[512,2048]{1,0:T(8,128)(2,1)S(1)} %bitcast.136, bf16[256,2048]{1,0:T(8,128)(2,1)S(1)} %bitcast.127, f32[2,2048]{1,0:T(2,128)S(1)} %bitcast.140, ...), custom_call_target="tpu_custom_call" | custom-call | tf_op jit(solution)/shard_map/bridge/pallas_call | solution.py:789
  284.0 38.9 %middle.1 = (bf16[1024,2048]{1,0:T(8,128)(2,1)}, bf16[1024,2048]{1,0:T(8,128)(2,1)}, bf16[1024,2048]{1,0:T(8,128)(2,1)}) custom-call(bf16[1024,2048]{1,0:T(8,128)(2,1)} %bitcast.123, bf16[1024,2048]{1,0:T(8,128)(2,1)} %bitcast.141, bf16[8,256,2048]{2,1,0:T(8,128)(2,1)} %bitcast_dynamic-update-slice_fusion.2.fc_ref, ...), custom_call_target="tpu_custom_call" | custom-call | tf_op jit(solution)/shard_map/middle/pallas_call | solution.py:674
  322.9 92.4 %feedback.1 = (bf16[4,256,2048]{2,1,0:T(8,128)(2,1)}, bf16[256,2048]{1,0:T(8,128)(2,1)}, f32[256,2048]{1,0:T(8,128)}, f32[2,2048]{1,0:T(2,128)}, bf16[512,2048]{...) custom-call(bf16[4,256,2048]{2,1,0:T(8,128)(2,1)} %bitcast.143, ...), custom_call_target="tpu_custom_call" | custom-call | tf_op jit(solution)/shard_map/feedback/pallas_call | solution.py:1022
  415.3 2.5 collective-permute-start.6
  418.3 2.3 slice.176.attn_in
  420.8 5.5 convolution_convert_fusion.1
  426.3 24.2 %attend_back.1 = (bf16[4,2,128,512]{3,2,1,0:T(8,128)(2,1)}, bf16[32,2,128,256]{3,2,1,0:T(8,128)(2,1)}) custom-call(s32[160]{0:T(256)} %copy-done.24, bf16[4,2,128,512]{3,2,1,0:T(8,128)(2,1)} %bitcast.129, bf16[32,2,128,256]{3,2,1,0:T(8,128)(2,1)} %bitcast.121, s32[4,2,1,128]{3,2,1,0:T(1,128)} %copy-done.22, bf16[4,2,128,512]{3,2,1,0:T(8,128)(2,1)} %copy-done.9, ...), custom_call_target="tpu_custom_call" | custom-call | tf_op jit(solution)/shard_map/attend_back/pallas_call | solution.py:262
  450.5 4.6 convolution_convert_fusion.proj_ref
  455.0 6.6 %collective-permute-done.6 = bf16[512,2048]{1,0:T(8,128)(2,1)} collective-permute-done((bf16[512,2048]{1,0:T(8,128)(2,1)}, bf16[512,2048]{1,0:T(8,128)(2,1)}, u32[]{:S(2)}, u32[]{:S(2)}) %collective-permute-start.6) | collective-permute-done | bytes 2097184 | tf_op jit(solution)/shard_map/ppermute | solution.py:65
  461.7 2.6 collective-permute-done.7
  464.3 7.9 %fusion.4 = (bf16[512,2048]{1,0:T(8,128)(2,1)}, bf16[512,2048]{1,0:T(8,128)(2,1)}) fusion(bf16[512,2048]{1,0:T(8,128)(2,1)} %collective-permute-done.7, bf16[3,512,2048]{2,1,0:T(8,128)(2,1)} %get-tuple-element.76.ff_rest, bf16[512,2048]{1,0:T(8,128)(2,1)} %collective-permute-done.6), kind=kLoop, calls=%fused_computation.7 | loop fusion | flops 8388608 | bytes 12582912 | tf_op jit(solution)/shard_map/convert_element_type | solution.py:69
  472.2 5.0 attn_turned.1.attn_parts
  479.2 141.7 %closing.1 = (bf16[256,2048]{1,0:T(8,128)(2,1)}, bf16[4,64,2048]{2,1,0:T(8,128)(2,1)}, bf16[4,64,2048]{2,1,0:T(8,128)(2,1)}, bf16[4,512,2048]{2,1,0:T(8,128)(2,1)}, f32[288,256]{1,0:T(8,128)}) custom-call(bf16[4,8,256,256]{3,2,1,0:T(8,128)(2,1)} %bitcast.144, bf16[1024,512]{1,0:T(8,128)(2,1)} %bitcast.132, bf16[2048,512]{1,0:T(8,128)(2,1)} %bitcast.135, ...), custom_call_target="tpu_custom_call" | custom-call | tf_op jit(solution)/shard_map/closing/pallas_call | solution.py:1391
  620.9 4.1 slice_bitcast_fusion
  627.9 5.4 stack_rows.3
  633.3 5.4 stack_cols.1
  (112 shorter events, 48.4 us)
Async XLA Ops:
  150.3 18.2 %copy-start.12 = (bf16[8,256,512]{2,1,0:T(8,128)(2,1)}, bf16[8,256,512]{2,1,0:T(8,128)(2,1)S(1)}, u32[]{:S(2)}) copy-start(bf16[8,256,512]{2,1,0:T(8,128)(2,1)S(1)} %get-tuple-element.51) | copy-start | bytes 6291460
  150.3 57.7 %collective-permute-start.2 = (bf16[256,2048]{1,0:T(8,128)(2,1)}, bf16[256,2048]{1,0:T(8,128)(2,1)}, u32[]{:S(2)}, u32[]{:S(2)}) collective-permute-start(bf16[256,2048]{1,0:T(8,128)(2,1)} %constant_dynamic-slice_fusion.down_own), channel_id=1, source_target_pairs={{0,2},{2,4},{4,6},{6,7},{7,5},{5,3},{3,1},{1,0},{8,10},{10,12},{12... | collective-permute-start | bytes 3145736 | tf_op jit(solution)/shard_map/ppermute | solution.py:1671
  151.2 56.8 %collective-permute-start.3 = (bf16[256,2048]{1,0:T(8,128)(2,1)}, bf16[256,2048]{1,0:T(8,128)(2,1)}, u32[]{:S(2)}, u32[]{:S(2)}) collective-permute-start(bf16[256,2048]{1,0:T(8,128)(2,1)} %constant_dynamic-slice_fusion.down_own), channel_id=1, source_target_pairs={{2,0},{4,2},{6,4},{7,6},{5,7},{3,5},{1,3},{0,1},{10,8},{12,10},{14... | collective-permute-start | bytes 3145736 | tf_op jit(solution)/shard_map/ppermute | solution.py:1671
  155.5 43.1 %collective-permute-start = (bf16[256,2048]{1,0:T(8,128)(2,1)}, bf16[256,2048]{1,0:T(8,128)(2,1)}, u32[]{:S(2)}, u32[]{:S(2)}) collective-permute-start(bf16[256,2048]{1,0:T(8,128)(2,1)} %get-tuple-element.97), channel_id=1, source_target_pairs={{0,2},{2,4},{4,6},{6,7},{7,5},{5,3},{3,1},{1,0},{8,10},{10,12},{12... | collective-permute-start | bytes 3145736 | tf_op jit(solution)/shard_map/ppermute | solution.py:1689
  156.4 42.2 %collective-permute-start.1 = (bf16[256,2048]{1,0:T(8,128)(2,1)}, bf16[256,2048]{1,0:T(8,128)(2,1)}, u32[]{:S(2)}, u32[]{:S(2)}) collective-permute-start(bf16[256,2048]{1,0:T(8,128)(2,1)} %get-tuple-element.96), channel_id=1, source_target_pairs={{2,0},{4,2},{6,4},{7,6},{5,7},{3,5},{1,3},{0,1},{10,8},{12,10},{14... | collective-permute-start | bytes 3145736 | tf_op jit(solution)/shard_map/ppermute | solution.py:1689
  158.4 15.2 %copy-start.22 = (s32[4,2,1,128]{3,2,1,0:T(1,128)}, s32[4,2,1,128]{3,2,1,0:T(1,128)S(1)}, u32[]{:S(2)}) copy-start(s32[4,2,1,128]{3,2,1,0:T(1,128)S(1)} %add_subtract_fusion.first_ref) | copy-start | bytes 12292
  158.5 3.4 copy-start.1
  173.1 30.7 %copy-start.8 = (bf16[1024,512]{1,0:T(8,128)(2,1)}, bf16[1024,512]{1,0:T(8,128)(2,1)S(1)}, u32[]{:S(2)}) copy-start(bf16[1024,512]{1,0:T(8,128)(2,1)S(1)} %convolution_convert_fusion.2) | copy-start | bytes 3145732
  173.6 30.1 %copy-start.24 = (s32[160]{0:T(256)}, s32[160]{0:T(256)S(1)}, u32[]{:S(2)}) copy-start(s32[160]{0:T(256)S(1)} %reshape.394.tables) | copy-start | bytes 1924
  193.5 14.5 %copy-start.23 = (f32[4,2,4,128]{3,2,1,0:T(4,128)}, f32[4,2,4,128]{3,2,1,0:T(4,128)S(1)}, u32[]{:S(2)}) copy-start(f32[4,2,4,128]{3,2,1,0:T(4,128)S(1)} %get-tuple-element.70.log_ref) | copy-start | bytes 49156
  193.5 85.4 %copy-start.9 = (bf16[4,2,128,512]{3,2,1,0:T(8,128)(2,1)}, bf16[4,2,128,512]{3,2,1,0:T(8,128)(2,1)S(1)}, u32[]{:S(2)}) copy-start(bf16[4,2,128,512]{3,2,1,0:T(8,128)(2,1)S(1)} %get-tuple-element.54.out_ref) | copy-start | bytes 3145732
  193.5 14.5 %copy-start.7 = (bf16[2,128,2048]{2,1,0:T(8,128)(2,1)S(1)}, bf16[2,128,2048]{2,1,0:T(8,128)(2,1)}, u32[]{:S(2)}) copy-start(bf16[2,128,2048]{2,1,0:T(8,128)(2,1)} %param.12) | copy-start | bytes 3145732
  193.5 14.5 %copy-start.14 = (bf16[8,64,2048]{2,1,0:T(8,128)(2,1)S(1)}, bf16[8,64,2048]{2,1,0:T(8,128)(2,1)}, u32[]{:S(2)}) copy-start(bf16[8,64,2048]{2,1,0:T(8,128)(2,1)} %copy-done.13) | copy-start | bytes 6291460
  199.7 82.5 %collective-permute-start.4 = (bf16[128,2048]{1,0:T(8,128)(2,1)S(1)}, bf16[128,2048]{1,0:T(8,128)(2,1)S(1)}, u32[]{:S(2)}, u32[]{:S(2)}) collective-permute-start(bf16[128,2048]{1,0:T(8,128)(2,1)S(1)} %slice.140), channel_id=1, source_target_pairs={{0,2},{2,4},{4,6},{6,7},{7,5},{5,3},{3,1},{1,0},{8,10},{10,12},{12... | collective-permute-start | bytes 1572872 | tf_op jit(solution)/shard_map/ppermute | solution.py:1691
  204.8 78.3 %collective-permute-start.5 = (bf16[128,2048]{1,0:T(8,128)(2,1)S(1)}, bf16[128,2048]{1,0:T(8,128)(2,1)S(1)}, u32[]{:S(2)}, u32[]{:S(2)}) collective-permute-start(bf16[128,2048]{1,0:T(8,128)(2,1)S(1)} %slice.141), channel_id=1, source_target_pairs={{2,0},{4,2},{6,4},{7,6},{5,7},{3,5},{1,3},{0,1},{10,8},{12,10},{14... | collective-permute-start | bytes 1572872 | tf_op jit(solution)/shard_map/ppermute | solution.py:1692
  415.3 46.4 %collective-permute-start.6 = (bf16[512,2048]{1,0:T(8,128)(2,1)}, bf16[512,2048]{1,0:T(8,128)(2,1)}, u32[]{:S(2)}, u32[]{:S(2)}) collective-permute-start(bf16[512,2048]{1,0:T(8,128)(2,1)} %get-tuple-element.68), channel_id=1, source_target_pairs={{0,2},{2,4},{4,6},{6,7},{7,5},{5,3},{3,1},{1,0},{8,10},{10,12},{12... | collective-permute-start | bytes 6291464 | tf_op jit(solution)/shard_map/ppermute | solution.py:65
  417.8 46.4 %collective-permute-start.7 = (bf16[512,2048]{1,0:T(8,128)(2,1)}, bf16[512,2048]{1,0:T(8,128)(2,1)}, u32[]{:S(2)}, u32[]{:S(2)}) collective-permute-start(bf16[512,2048]{1,0:T(8,128)(2,1)} %get-tuple-element.69), channel_id=1, source_target_pairs={{2,0},{4,2},{6,4},{7,6},{5,7},{3,5},{1,3},{0,1},{10,8},{12,10},{14... | collective-permute-start | bytes 6291464 | tf_op jit(solution)/shard_map/ppermute | solution.py:66
  426.3 24.2 %copy-start.10 = (bf16[4,2,128,512]{3,2,1,0:T(8,128)(2,1)S(1)}, bf16[4,2,128,512]{3,2,1,0:T(8,128)(2,1)}, u32[]{:S(2)}) copy-start(bf16[4,2,128,512]{3,2,1,0:T(8,128)(2,1)} %copy-done.9) | copy-start | bytes 3145732
  464.3 7.9 %copy-start.2 = (bf16[1024,2048]{1,0:T(8,128)(2,1)S(1)}, bf16[1024,2048]{1,0:T(8,128)(2,1)}, u32[]{:S(2)}) copy-start(bf16[1024,2048]{1,0:T(8,128)(2,1)} %fusion.3.rows_ref) | copy-start | bytes 12582916
  464.3 7.9 %copy-start.11 = (bf16[4,2,128,512]{3,2,1,0:T(8,128)(2,1)S(1)}, bf16[4,2,128,512]{3,2,1,0:T(8,128)(2,1)}, u32[]{:S(2)}) copy-start(bf16[4,2,128,512]{3,2,1,0:T(8,128)(2,1)} %get-tuple-element.75) | copy-start | bytes 3145732
  620.9 4.2 copy-start.27
  620.9 4.3 copy-start.21
  620.9 4.9 copy-start.20
  633.3 7.4 %copy-start.25 = (bf16[256,2048]{1,0:T(8,128)(2,1)S(1)}, bf16[256,2048]{1,0:T(8,128)(2,1)}, u32[]{:S(2)}) copy-start(bf16[256,2048]{1,0:T(8,128)(2,1)} %get-tuple-element.67) | copy-start | bytes 3145732
  (12 other events, 19.9 us)
